TPU v7x, 256 devices: a whole 4x4x8 slice. The times are simulated.
256 devices in a mesh: step: 4 (over y), tile: 64 (over z, x, core).
Axes of the slice: x: 4, y: 4, z: 8, core: 2. Of those that a mesh axis runs over, the one named last changes fastest.
Arguments:
- start_state: float32 [4, 512, 128], P(None, 'tile'), may hold values from -6 to 6
- covariates: bfloat16 [12, 512, 128], P(None, 'tile'), may hold values from -6 to 6
- noise: float32 [8, 4, 512, 128], P('step', None, 'tile'), may hold values from -6 to 6
- embedding: float32 [8, 128], P('step'), may hold values from -4 to 4
- w_in: bfloat16 [9, 128, 16], replicated, may hold values from -0.5 to 0.5
- w_first: bfloat16 [9, 128, 128], replicated, may hold values from -0.1875 to 0.1875
- w_second: bfloat16 [9, 128, 128], replicated, may hold values from -0.1875 to 0.1875
- w_out: bfloat16 [4, 128], replicated, may hold values from -0.5 to 0.5
Outputs:
- states: float32 [8, 4, 512, 128], P('step', None, 'tile')
All inputs are finite; a program needn't handle non-finite values.
Results may differ from a plain program's by a relative error of at most 0.0013.
Values may be sent and summed in bfloat16 or wider, within the bound.
A program may use at most 64 MiB of HBM per device.

v0:
```python
import jax
import jax.numpy as jnp
from jax import lax
from jax.sharding import PartitionSpec as P

STEPS = 8
SWEEPS = 2


def with_halo(x, sides, width):
    for axis, dim in sides:
        size, length = (lax.axis_size(axis), x.shape[dim])
        up = [(i, (i + 1) % size) for i in range(size - 1)]
        down = [(j, i) for i, j in up]
        last = lax.slice_in_dim(x, length - width, length, axis=dim)
        leading = lax.slice_in_dim(x, 0, width, axis=dim)
        before = lax.ppermute(last, axis, up)
        after = lax.ppermute(leading, axis, down)
        x = jnp.concatenate([before, x, after], axis=dim)
    return x


def carried_in(x, axis, combine, identity):
    size, here = (lax.axis_size(axis), lax.axis_index(axis))
    everything = lax.all_gather(x, axis)
    start = jnp.broadcast_to(jnp.asarray(identity, x.dtype), x.shape)

    def hop(k, before):
        reached = k < here
        new = combine(before, everything[k])
        return jnp.where(reached, new, before)

    return lax.fori_loop(0, size, hop, start)


def conv_cols(field, weight):
    columns = field.shape[2] - 2
    rows = field.shape[3]
    padded = jnp.pad(field, ((0, 0), (0, 0), (0, 0), (1, 1)))
    total = None
    for col_off in range(3):
        for row_off in range(3):
            piece = padded[:, :, col_off : col_off + columns, row_off : row_off + rows]
            term = jnp.einsum(
                "oi,sicr->socr",
                weight[3 * col_off + row_off],
                piece,
                preferred_element_type=jnp.float32,
            )
            total = term if total is None else total + term
    return total


def local(start_state, covariates, noise, embedding, w_in, w_first, w_second, w_out):
    local_steps = noise.shape[0]
    embed = embedding[:, :, None, None]
    deep = 1
    cov_steps = jnp.broadcast_to(covariates[None], (local_steps,) + covariates.shape)

    def hidden_rim(field):
        return with_halo(field, (("tile", 2),), 1)

    def add_terms(earlier, later):
        return earlier + later

    guesses = jnp.broadcast_to(start_state[None], (local_steps,) + start_state.shape)
    results = guesses
    for sweep_index in range(SWEEPS):
        inputs = jnp.concatenate([guesses.astype(jnp.bfloat16), cov_steps], axis=1)
        widened = with_halo(inputs, (("tile", 2),), deep)
        first_hidden = jax.nn.silu(conv_cols(widened, w_in) + embed).astype(jnp.bfloat16)
        second_hidden = jax.nn.silu(conv_cols(hidden_rim(first_hidden), w_first)).astype(
            jnp.bfloat16
        )
        block_out = (
            jax.nn.silu(conv_cols(hidden_rim(second_hidden), w_second))
            + first_hidden.astype(jnp.float32)
        ).astype(jnp.bfloat16)
        projected = jnp.einsum(
            "oi,sicr->socr", w_out, block_out, preferred_element_type=jnp.float32
        )
        drift_all = projected / STEPS + 0.3 * noise
        partial_sums = []
        running = jnp.zeros_like(start_state)
        for k in range(local_steps):
            running = running + drift_all[k]
            partial_sums.append(running)
        group_sum = partial_sums[-1]
        before = carried_in(group_sum, "step", add_terms, jnp.zeros_like(group_sum))
        base = start_state + before
        results = jnp.stack([base + partial_value for partial_value in partial_sums], axis=0)
        guesses = jnp.concatenate([base[None], results[:-1]], axis=0)
    return results


def solution(mesh):
    in_specs = (
        P(None, "tile", None),
        P(None, "tile", None),
        P("step", None, "tile", None),
        P("step", None),
        P(),
        P(),
        P(),
        P(),
    )
    out_specs = P("step", None, "tile", None)
    return jax.shard_map(local, mesh=mesh, in_specs=in_specs, out_specs=out_specs, check_vma=False)
```

profile of v0, /device:TPU:152, one launch (start us, length us, event | category | flops | bytes accessed | tf_op | source)
XLA Modules:
  0.0 120.0 jit_solution(14851858894694891390)
XLA Ops:
  0.0 0.8 copy.22
  0.8 0.7 convert_element_type.37
  1.5 1.9 %collective-permute-start = (bf16[2,16,1,128]{3,1,2,0:T(8,128)(2,1)S(1)}, bf16[2,16,1,128]{3,1,2,0:T(8,128)(2,1)S(1)}, u32[]{:S(2)}, u32[]{:S(2)}) collective-permute-start(bf16[2,16,1,128]{3,1,2,0:T(8,128)(2,1)S(1)} %get-tuple-element.227), channel_id=1, source_target_pairs={{0,1},{1,2},{2,3},{3,4},{4,5},{5,6},{6,7},{7,8},{8,9},{9,10},{10,1... | collective-permute-start | bytes 24584 | tf_op jit(solution)/shard_map/ppermute | solution.py:17
  3.5 7.0 %collective-permute-start.1 = (bf16[2,16,1,128]{3,1,2,0:T(8,128)(2,1)S(1)}, bf16[2,16,1,128]{3,1,2,0:T(8,128)(2,1)S(1)}, u32[]{:S(2)}, u32[]{:S(2)}) collective-permute-start(bf16[2,16,1,128]{3,1,2,0:T(8,128)(2,1)S(1)} %get-tuple-element.228), channel_id=1, source_target_pairs={{1,0},{2,1},{3,2},{4,3},{5,4},{6,5},{7,6},{8,7},{9,8},{10,9},{11,1... | collective-permute-start | bytes 24584 | tf_op jit(solution)/shard_map/ppermute | solution.py:18
  10.5 1.3 %collective-permute-done.1 = bf16[2,16,1,128]{3,1,2,0:T(8,128)(2,1)S(1)} collective-permute-done((bf16[2,16,1,128]{3,1,2,0:T(8,128)(2,1)S(1)}, bf16[2,16,1,128]{3,1,2,0:T(8,128)(2,1)S(1)}, u32[]{:S(2)}, u32[]{:S(2)}) %collective-permute-start.1) | collective-permute-done | bytes 8224 | tf_op jit(solution)/shard_map/ppermute | solution.py:18
  11.8 1.1 fusion.128
  13.0 0.3 fusion.111
  13.3 0.5 convolution_add_fusion.13
  13.8 0.5 convolution_add_fusion.12
  14.2 0.5 convolution_add_fusion.11
  14.7 0.3 convolution_add_fusion.10
  15.0 0.5 convolution_add_fusion.9
  15.5 0.5 convolution_add_fusion.8
  16.2 0.5 multiply_convert_fusion.3
  16.7 2.1 %collective-permute-start.2 = (bf16[2,128,1,128]{1,3,2,0:T(8,128)(2,1)S(1)}, bf16[2,128,1,128]{1,3,2,0:T(8,128)(2,1)S(1)}, u32[]{:S(2)}, u32[]{:S(2)}) collective-permute-start(bf16[2,128,1,128]{1,3,2,0:T(8,128)(2,1)S(1)} %get-tuple-element.225), channel_id=1, source_target_pairs={{0,1},{1,2},{2,3},{3,4},{4,5},{5,6},{6,7},{7,8},{8,9},{9,10},{10,1... | collective-permute-start | bytes 196616 | tf_op jit(solution)/shard_map/ppermute | solution.py:17
  18.8 7.0 %collective-permute-start.3 = (bf16[2,128,1,128]{1,3,2,0:T(8,128)(2,1)S(1)}, bf16[2,128,1,128]{1,3,2,0:T(8,128)(2,1)S(1)}, u32[]{:S(2)}, u32[]{:S(2)}) collective-permute-start(bf16[2,128,1,128]{1,3,2,0:T(8,128)(2,1)S(1)} %get-tuple-element.226), channel_id=1, source_target_pairs={{1,0},{2,1},{3,2},{4,3},{5,4},{6,5},{7,6},{8,7},{9,8},{10,9},{11,1... | collective-permute-start | bytes 196616 | tf_op jit(solution)/shard_map/ppermute | solution.py:18
  25.8 1.9 %collective-permute-done.3 = bf16[2,128,1,128]{1,3,2,0:T(8,128)(2,1)S(1)} collective-permute-done((bf16[2,128,1,128]{1,3,2,0:T(8,128)(2,1)S(1)}, bf16[2,128,1,128]{1,3,2,0:T(8,128)(2,1)S(1)}, u32[]{:S(2)}, u32[]{:S(2)}) %collective-permute-start.3) | collective-permute-done | bytes 65568 | tf_op jit(solution)/shard_map/ppermute | solution.py:18
  27.9 0.3 fusion.93
  28.8 0.3 convolution_add_fusion.36
  29.1 0.3 convolution_add_fusion.35
  29.7 0.3 convolution_add_fusion.33
  30.3 0.5 multiply_convert_fusion.2
  30.9 2.1 %collective-permute-start.4 = (bf16[2,128,1,128]{1,3,2,0:T(8,128)(2,1)S(1)}, bf16[2,128,1,128]{1,3,2,0:T(8,128)(2,1)S(1)}, u32[]{:S(2)}, u32[]{:S(2)}) collective-permute-start(bf16[2,128,1,128]{1,3,2,0:T(8,128)(2,1)S(1)} %get-tuple-element.223), channel_id=1, source_target_pairs={{0,1},{1,2},{2,3},{3,4},{4,5},{5,6},{6,7},{7,8},{8,9},{9,10},{10,1... | collective-permute-start | bytes 196616 | tf_op jit(solution)/shard_map/ppermute | solution.py:17
  32.9 7.0 %collective-permute-start.5 = (bf16[2,128,1,128]{1,3,2,0:T(8,128)(2,1)S(1)}, bf16[2,128,1,128]{1,3,2,0:T(8,128)(2,1)S(1)}, u32[]{:S(2)}, u32[]{:S(2)}) collective-permute-start(bf16[2,128,1,128]{1,3,2,0:T(8,128)(2,1)S(1)} %get-tuple-element.224), channel_id=1, source_target_pairs={{1,0},{2,1},{3,2},{4,3},{5,4},{6,5},{7,6},{8,7},{9,8},{10,9},{11,1... | collective-permute-start | bytes 196616 | tf_op jit(solution)/shard_map/ppermute | solution.py:18
  40.0 1.8 %collective-permute-done.5 = bf16[2,128,1,128]{1,3,2,0:T(8,128)(2,1)S(1)} collective-permute-done((bf16[2,128,1,128]{1,3,2,0:T(8,128)(2,1)S(1)}, bf16[2,128,1,128]{1,3,2,0:T(8,128)(2,1)S(1)}, u32[]{:S(2)}, u32[]{:S(2)}) %collective-permute-start.5) | collective-permute-done | bytes 65568 | tf_op jit(solution)/shard_map/ppermute | solution.py:18
  42.1 0.3 fusion.85
  42.4 0.5 copy-done.4
  43.2 0.3 convolution_add_fusion.31
  43.5 0.3 convolution_add_fusion.30
  44.4 1.3 %convolution_add_fusion.27 = f32[2,8,128,128]{3,2,1,0:T(8,128)} fusion(f32[2,8,128,128]{3,2,1,0:T(8,128)S(1)} %convolution_add_fusion.28, bf16[2,128,10,130]{1,3,2,0:T(8,128)(2,1)S(1)} %fusion.35, bf16[9,128,128]{2,1,0:T(8,128)(2,1)S(1)} %copy-done.2), kind=kOutput, calls=%fused_computation.47 | convolution fusion | flops 67371008 | bytes 2654208 | tf_op jit(solution)/shard_map/oi,sicr->socr/dot_general | solution.py:44
  45.7 1.3 %fusion.50 = f32[2,8,128,128]{3,2,1,0:T(8,128)} fusion(bf16[2,128,1,128]{1,3,2,0:T(8,128)(2,1)S(1)} %collective-permute-done.5, bf16[2,128,8,128]{1,3,2,0:T(8,128)(2,1)S(1)} %multiply_convert_fusion.2, bf16[9,128,128]{2,1,0:T(8,128)(2,1)S(1)} %copy-done.2), kind=kOutput, calls=%fused_computation.102 | convolution fusion | flops 68288512 | bytes 1671168 | tf_op jit(solution)/shard_map/oi,sicr->socr/dot_general | solution.py:44
  47.0 2.3 %fusion.22 = f32[2,4,8,128]{3,1,2,0:T(4,128)S(1)} fusion(bf16[2,128,8,128]{1,3,2,0:T(8,128)(2,1)S(1)} %multiply_convert_fusion.3, f32[2,8,128,128]{3,2,1,0:T(8,128)S(1)} %fusion.85, f32[2,8,128,128]{3,2,1,0:T(8,128)} %fusion.50, f32[2,8,128,128]{3,2,1,0:T(8,128)} %convolution_add_fusion.27, bf16[2,128,10,130]{1,3,2,0:T(8,128)(2,1)S(1)} %fusion.35, ...), kind=kOutput, calls=%fused_computation.66 | convolution fusion | flops 71852032 | bytes 4293632 | tf_op jit(solution)/shard_map/oi,sicr->socr/dot_general | solution.py:79
  49.3 11.9 %all_gather.8 = f32[4,4,8,128]{3,2,1,0:T(8,128)S(1)} all-gather(f32[1,4,8,128]{3,2,1,0:T(8,128)S(1)} %copy.25), channel_id=1, replica_groups=mesh['step'=4,'tile'=64] {'step'}, dimensions={0}, use_global_device_ids=true | all-gather | bytes 81920 | tf_op jit(solution)/shard_map/all_gather | solution.py:25
  61.3 1.9 %collective-permute-start.6 = (bf16[2,16,1,128]{3,1,2,0:T(8,128)(2,1)S(1)}, bf16[2,16,1,128]{3,1,2,0:T(8,128)(2,1)S(1)}, u32[]{:S(2)}, u32[]{:S(2)}) collective-permute-start(bf16[2,16,1,128]{3,1,2,0:T(8,128)(2,1)S(1)} %get-tuple-element.231), channel_id=1, source_target_pairs={{0,1},{1,2},{2,3},{3,4},{4,5},{5,6},{6,7},{7,8},{8,9},{9,10},{10,1... | collective-permute-start | bytes 24584 | tf_op jit(solution)/shard_map/ppermute | solution.py:17
  63.3 7.0 %collective-permute-start.7 = (bf16[2,16,1,128]{3,1,2,0:T(8,128)(2,1)S(1)}, bf16[2,16,1,128]{3,1,2,0:T(8,128)(2,1)S(1)}, u32[]{:S(2)}, u32[]{:S(2)}) collective-permute-start(bf16[2,16,1,128]{3,1,2,0:T(8,128)(2,1)S(1)} %get-tuple-element.232), channel_id=1, source_target_pairs={{1,0},{2,1},{3,2},{4,3},{5,4},{6,5},{7,6},{8,7},{9,8},{10,9},{11,1... | collective-permute-start | bytes 24584 | tf_op jit(solution)/shard_map/ppermute | solution.py:18
  70.2 1.3 %collective-permute-done.7 = bf16[2,16,1,128]{3,1,2,0:T(8,128)(2,1)S(1)} collective-permute-done((bf16[2,16,1,128]{3,1,2,0:T(8,128)(2,1)S(1)}, bf16[2,16,1,128]{3,1,2,0:T(8,128)(2,1)S(1)}, u32[]{:S(2)}, u32[]{:S(2)}) %collective-permute-start.7) | collective-permute-done | bytes 8224 | tf_op jit(solution)/shard_map/ppermute | solution.py:18
  71.6 0.5 fusion.129
  72.1 0.3 fusion.114
  72.4 0.5 convolution_add_fusion.7
  72.9 0.5 convolution_add_fusion.6
  73.3 0.5 convolution_add_fusion.5
  73.8 0.3 convolution_add_fusion.4
  74.1 0.5 convolution_add_fusion.3
  74.6 0.5 convolution_add_fusion.2
  75.1 0.5 multiply_convert_fusion.1
  75.6 1.9 %collective-permute-start.8 = (bf16[2,128,1,128]{1,3,2,0:T(8,128)(2,1)S(1)}, bf16[2,128,1,128]{1,3,2,0:T(8,128)(2,1)S(1)}, u32[]{:S(2)}, u32[]{:S(2)}) collective-permute-start(bf16[2,128,1,128]{1,3,2,0:T(8,128)(2,1)S(1)} %get-tuple-element.221), channel_id=1, source_target_pairs={{0,1},{1,2},{2,3},{3,4},{4,5},{5,6},{6,7},{7,8},{8,9},{9,10},{10,1... | collective-permute-start | bytes 196616 | tf_op jit(solution)/shard_map/ppermute | solution.py:17
  77.5 7.1 %collective-permute-start.9 = (bf16[2,128,1,128]{1,3,2,0:T(8,128)(2,1)S(1)}, bf16[2,128,1,128]{1,3,2,0:T(8,128)(2,1)S(1)}, u32[]{:S(2)}, u32[]{:S(2)}) collective-permute-start(bf16[2,128,1,128]{1,3,2,0:T(8,128)(2,1)S(1)} %get-tuple-element.222), channel_id=1, source_target_pairs={{1,0},{2,1},{3,2},{4,3},{5,4},{6,5},{7,6},{8,7},{9,8},{10,9},{11,1... | collective-permute-start | bytes 196616 | tf_op jit(solution)/shard_map/ppermute | solution.py:18
  84.7 1.7 %collective-permute-done.9 = bf16[2,128,1,128]{1,3,2,0:T(8,128)(2,1)S(1)} collective-permute-done((bf16[2,128,1,128]{1,3,2,0:T(8,128)(2,1)S(1)}, bf16[2,128,1,128]{1,3,2,0:T(8,128)(2,1)S(1)}, u32[]{:S(2)}, u32[]{:S(2)}) %collective-permute-start.9) | collective-permute-done | bytes 65568 | tf_op jit(solution)/shard_map/ppermute | solution.py:18
  86.6 0.3 fusion.78
  87.2 0.3 convolution_add_fusion.25
  87.5 0.3 convolution_add_fusion.24
  87.8 0.3 convolution_add_fusion.23
  88.4 0.3 convolution_add_fusion.21
  89.0 0.5 multiply_convert_fusion
  89.6 1.9 %collective-permute-start.10 = (bf16[2,128,1,128]{1,3,2,0:T(8,128)(2,1)S(1)}, bf16[2,128,1,128]{1,3,2,0:T(8,128)(2,1)S(1)}, u32[]{:S(2)}, u32[]{:S(2)}) collective-permute-start(bf16[2,128,1,128]{1,3,2,0:T(8,128)(2,1)S(1)} %get-tuple-element.219), channel_id=1, source_target_pairs={{0,1},{1,2},{2,3},{3,4},{4,5},{5,6},{6,7},{7,8},{8,9},{9,10},{10,1... | collective-permute-start | bytes 196616 | tf_op jit(solution)/shard_map/ppermute | solution.py:17
  91.5 7.0 %collective-permute-start.11 = (bf16[2,128,1,128]{1,3,2,0:T(8,128)(2,1)S(1)}, bf16[2,128,1,128]{1,3,2,0:T(8,128)(2,1)S(1)}, u32[]{:S(2)}, u32[]{:S(2)}) collective-permute-start(bf16[2,128,1,128]{1,3,2,0:T(8,128)(2,1)S(1)} %get-tuple-element.220), channel_id=1, source_target_pairs={{1,0},{2,1},{3,2},{4,3},{5,4},{6,5},{7,6},{8,7},{9,8},{10,9},{11,1... | collective-permute-start | bytes 196616 | tf_op jit(solution)/shard_map/ppermute | solution.py:18
  98.6 1.9 %collective-permute-done.11 = bf16[2,128,1,128]{1,3,2,0:T(8,128)(2,1)S(1)} collective-permute-done((bf16[2,128,1,128]{1,3,2,0:T(8,128)(2,1)S(1)}, bf16[2,128,1,128]{1,3,2,0:T(8,128)(2,1)S(1)}, u32[]{:S(2)}, u32[]{:S(2)}) %collective-permute-start.11) | collective-permute-done | bytes 65568 | tf_op jit(solution)/shard_map/ppermute | solution.py:18
  100.6 0.3 fusion.70
  101.5 0.3 convolution_add_fusion.18
  102.5 1.3 %convolution_add_fusion.15 = f32[2,8,128,128]{3,2,1,0:T(8,128)} fusion(f32[2,8,128,128]{3,2,1,0:T(8,128)S(1)} %convolution_add_fusion.16, bf16[2,128,10,130]{1,3,2,0:T(8,128)(2,1)S(1)} %select_maximum_fusion, bf16[9,128,128]{2,1,0:T(8,128)(2,1)S(1)} %copy-done.2), kind=kOutput, calls=%fused_computation.29 | convolution fusion | flops 67371008 | bytes 2654208 | tf_op jit(solution)/shard_map/oi,sicr->socr/dot_general | solution.py:44
  103.7 1.3 %fusion.66 = f32[2,8,128,128]{3,2,1,0:T(8,128)} fusion(bf16[2,128,1,128]{1,3,2,0:T(8,128)(2,1)S(1)} %collective-permute-done.11, bf16[2,128,8,128]{1,3,2,0:T(8,128)(2,1)S(1)} %multiply_convert_fusion, bf16[9,128,128]{2,1,0:T(8,128)(2,1)S(1)} %copy-done.2), kind=kOutput, calls=%fused_computation.118 | convolution fusion | flops 68288512 | bytes 1671168 | tf_op jit(solution)/shard_map/oi,sicr->socr/dot_general | solution.py:44
  105.0 2.2 %fusion.20 = f32[2,4,8,128]{3,1,2,0:T(4,128)S(1)} fusion(bf16[2,128,8,128]{1,3,2,0:T(8,128)(2,1)S(1)} %multiply_convert_fusion.1, f32[2,8,128,128]{3,2,1,0:T(8,128)S(1)} %fusion.70, f32[2,8,128,128]{3,2,1,0:T(8,128)} %fusion.66, f32[2,8,128,128]{3,2,1,0:T(8,128)} %convolution_add_fusion.15, bf16[2,128,10,130]{1,3,2,0:T(8,128)(2,1)S(1)} %select_maximum_fusion, ...), kind=kOutput, calls=%fused_computation.63 | convolution fusion | flops 71852032 | bytes 4293632 | tf_op jit(solution)/shard_map/oi,sicr->socr/dot_general | solution.py:79
  107.3 11.9 %all_gather.9 = f32[4,4,8,128]{3,2,1,0:T(8,128)S(1)} all-gather(f32[1,4,8,128]{3,2,1,0:T(8,128)S(1)} %copy.29), channel_id=1, replica_groups=mesh['step'=4,'tile'=64] {'step'}, dimensions={0}, use_global_device_ids=true | all-gather | bytes 81920 | tf_op jit(solution)/shard_map/all_gather | solution.py:25
  119.3 0.6 copy.32
  (74 shorter events, 5.7 us)
Async XLA Ops:
  0.0 47.0 %copy-start = (bf16[4,128]{1,0:T(4,128)(2,1)S(1)}, bf16[4,128]{1,0:T(4,128)(2,1)}, u32[]{:S(2)}) copy-start(bf16[4,128]{1,0:T(4,128)(2,1)} %param.19) | copy-start | bytes 3076
  0.0 13.0 %copy-start.6 = (bf16[9,128,16]{1,2,0:T(8,128)(2,1)S(1)}, bf16[9,128,16]{1,2,0:T(8,128)(2,1)}, u32[]{:S(2)}) copy-start(bf16[9,128,16]{1,2,0:T(8,128)(2,1)} %param.16) | copy-start | bytes 110596
  1.5 8.9 %collective-permute-start = (bf16[2,16,1,128]{3,1,2,0:T(8,128)(2,1)S(1)}, bf16[2,16,1,128]{3,1,2,0:T(8,128)(2,1)S(1)}, u32[]{:S(2)}, u32[]{:S(2)}) collective-permute-start(bf16[2,16,1,128]{3,1,2,0:T(8,128)(2,1)S(1)} %get-tuple-element.227), channel_id=1, source_target_pairs={{0,1},{1,2},{2,3},{3,4},{4,5},{5,6},{6,7},{7,8},{8,9},{9,10},{10,1... | collective-permute-start | bytes 24584 | tf_op jit(solution)/shard_map/ppermute | solution.py:17
  3.5 8.3 %collective-permute-start.1 = (bf16[2,16,1,128]{3,1,2,0:T(8,128)(2,1)S(1)}, bf16[2,16,1,128]{3,1,2,0:T(8,128)(2,1)S(1)}, u32[]{:S(2)}, u32[]{:S(2)}) collective-permute-start(bf16[2,16,1,128]{3,1,2,0:T(8,128)(2,1)S(1)} %get-tuple-element.228), channel_id=1, source_target_pairs={{1,0},{2,1},{3,2},{4,3},{5,4},{6,5},{7,6},{8,7},{9,8},{10,9},{11,1... | collective-permute-start | bytes 24584 | tf_op jit(solution)/shard_map/ppermute | solution.py:18
  15.5 0.7 copy-start.9
  16.7 11.1 %copy-start.1 = (bf16[9,128,128]{2,1,0:T(8,128)(2,1)S(1)}, bf16[9,128,128]{2,1,0:T(8,128)(2,1)}, u32[]{:S(2)}) copy-start(bf16[9,128,128]{2,1,0:T(8,128)(2,1)} %param.17) | copy-start | bytes 884740
  16.7 9.0 %collective-permute-start.2 = (bf16[2,128,1,128]{1,3,2,0:T(8,128)(2,1)S(1)}, bf16[2,128,1,128]{1,3,2,0:T(8,128)(2,1)S(1)}, u32[]{:S(2)}, u32[]{:S(2)}) collective-permute-start(bf16[2,128,1,128]{1,3,2,0:T(8,128)(2,1)S(1)} %get-tuple-element.225), channel_id=1, source_target_pairs={{0,1},{1,2},{2,3},{3,4},{4,5},{5,6},{6,7},{7,8},{8,9},{9,10},{10,1... | collective-permute-start | bytes 196616 | tf_op jit(solution)/shard_map/ppermute | solution.py:17
  18.8 8.9 %collective-permute-start.3 = (bf16[2,128,1,128]{1,3,2,0:T(8,128)(2,1)S(1)}, bf16[2,128,1,128]{1,3,2,0:T(8,128)(2,1)S(1)}, u32[]{:S(2)}, u32[]{:S(2)}) collective-permute-start(bf16[2,128,1,128]{1,3,2,0:T(8,128)(2,1)S(1)} %get-tuple-element.226), channel_id=1, source_target_pairs={{1,0},{2,1},{3,2},{4,3},{5,4},{6,5},{7,6},{8,7},{9,8},{10,9},{11,1... | collective-permute-start | bytes 196616 | tf_op jit(solution)/shard_map/ppermute | solution.py:18
  30.8 11.2 %copy-start.2 = (bf16[9,128,128]{2,1,0:T(8,128)(2,1)S(1)}, bf16[9,128,128]{2,1,0:T(8,128)(2,1)}, u32[]{:S(2)}) copy-start(bf16[9,128,128]{2,1,0:T(8,128)(2,1)} %param.18) | copy-start | bytes 884740
  30.9 9.1 %collective-permute-start.4 = (bf16[2,128,1,128]{1,3,2,0:T(8,128)(2,1)S(1)}, bf16[2,128,1,128]{1,3,2,0:T(8,128)(2,1)S(1)}, u32[]{:S(2)}, u32[]{:S(2)}) collective-permute-start(bf16[2,128,1,128]{1,3,2,0:T(8,128)(2,1)S(1)} %get-tuple-element.223), channel_id=1, source_target_pairs={{0,1},{1,2},{2,3},{3,4},{4,5},{5,6},{6,7},{7,8},{8,9},{9,10},{10,1... | collective-permute-start | bytes 196616 | tf_op jit(solution)/shard_map/ppermute | solution.py:17
  32.9 8.9 %collective-permute-start.5 = (bf16[2,128,1,128]{1,3,2,0:T(8,128)(2,1)S(1)}, bf16[2,128,1,128]{1,3,2,0:T(8,128)(2,1)S(1)}, u32[]{:S(2)}, u32[]{:S(2)}) collective-permute-start(bf16[2,128,1,128]{1,3,2,0:T(8,128)(2,1)S(1)} %get-tuple-element.224), channel_id=1, source_target_pairs={{1,0},{2,1},{3,2},{4,3},{5,4},{6,5},{7,6},{8,7},{9,8},{10,9},{11,1... | collective-permute-start | bytes 196616 | tf_op jit(solution)/shard_map/ppermute | solution.py:18
  40.0 1.9 %copy-start.3 = (bf16[2,128,1,128]{1,3,2,0:T(8,128)(2,1)}, bf16[2,128,1,128]{1,3,2,0:T(8,128)(2,1)S(1)}, u32[]{:S(2)}) copy-start(bf16[2,128,1,128]{1,3,2,0:T(8,128)(2,1)S(1)} %collective-permute-done.4) | copy-start | bytes 196612
  42.0 0.8 copy-start.4
  47.0 14.3 %copy-start.5 = (f32[4,8,128]{2,1,0:T(8,128)S(1)}, f32[4,8,128]{2,1,0:T(8,128)}, u32[]{:S(2)}) copy-start(f32[4,8,128]{2,1,0:T(8,128)} %param.12) | copy-start | bytes 49156
  47.0 24.6 %copy-start.7 = (bf16[9,128,16]{1,2,0:T(8,128)(2,1)S(1)}, bf16[9,128,16]{1,2,0:T(8,128)(2,1)}, u32[]{:S(2)}) copy-start(bf16[9,128,16]{1,2,0:T(8,128)(2,1)} %param.16) | copy-start | bytes 110596
  61.3 8.9 %collective-permute-start.6 = (bf16[2,16,1,128]{3,1,2,0:T(8,128)(2,1)S(1)}, bf16[2,16,1,128]{3,1,2,0:T(8,128)(2,1)S(1)}, u32[]{:S(2)}, u32[]{:S(2)}) collective-permute-start(bf16[2,16,1,128]{3,1,2,0:T(8,128)(2,1)S(1)} %get-tuple-element.231), channel_id=1, source_target_pairs={{0,1},{1,2},{2,3},{3,4},{4,5},{5,6},{6,7},{7,8},{8,9},{9,10},{10,1... | collective-permute-start | bytes 24584 | tf_op jit(solution)/shard_map/ppermute | solution.py:17
  63.3 8.3 %collective-permute-start.7 = (bf16[2,16,1,128]{3,1,2,0:T(8,128)(2,1)S(1)}, bf16[2,16,1,128]{3,1,2,0:T(8,128)(2,1)S(1)}, u32[]{:S(2)}, u32[]{:S(2)}) collective-permute-start(bf16[2,16,1,128]{3,1,2,0:T(8,128)(2,1)S(1)} %get-tuple-element.232), channel_id=1, source_target_pairs={{1,0},{2,1},{3,2},{4,3},{5,4},{6,5},{7,6},{8,7},{9,8},{10,9},{11,1... | collective-permute-start | bytes 24584 | tf_op jit(solution)/shard_map/ppermute | solution.py:18
  75.6 9.1 %collective-permute-start.8 = (bf16[2,128,1,128]{1,3,2,0:T(8,128)(2,1)S(1)}, bf16[2,128,1,128]{1,3,2,0:T(8,128)(2,1)S(1)}, u32[]{:S(2)}, u32[]{:S(2)}) collective-permute-start(bf16[2,128,1,128]{1,3,2,0:T(8,128)(2,1)S(1)} %get-tuple-element.221), channel_id=1, source_target_pairs={{0,1},{1,2},{2,3},{3,4},{4,5},{5,6},{6,7},{7,8},{8,9},{9,10},{10,1... | collective-permute-start | bytes 196616 | tf_op jit(solution)/shard_map/ppermute | solution.py:17
  77.5 8.9 %collective-permute-start.9 = (bf16[2,128,1,128]{1,3,2,0:T(8,128)(2,1)S(1)}, bf16[2,128,1,128]{1,3,2,0:T(8,128)(2,1)S(1)}, u32[]{:S(2)}, u32[]{:S(2)}) collective-permute-start(bf16[2,128,1,128]{1,3,2,0:T(8,128)(2,1)S(1)} %get-tuple-element.222), channel_id=1, source_target_pairs={{1,0},{2,1},{3,2},{4,3},{5,4},{6,5},{7,6},{8,7},{9,8},{10,9},{11,1... | collective-permute-start | bytes 196616 | tf_op jit(solution)/shard_map/ppermute | solution.py:18
  89.6 9.0 %collective-permute-start.10 = (bf16[2,128,1,128]{1,3,2,0:T(8,128)(2,1)S(1)}, bf16[2,128,1,128]{1,3,2,0:T(8,128)(2,1)S(1)}, u32[]{:S(2)}, u32[]{:S(2)}) collective-permute-start(bf16[2,128,1,128]{1,3,2,0:T(8,128)(2,1)S(1)} %get-tuple-element.219), channel_id=1, source_target_pairs={{0,1},{1,2},{2,3},{3,4},{4,5},{5,6},{6,7},{7,8},{8,9},{9,10},{10,1... | collective-permute-start | bytes 196616 | tf_op jit(solution)/shard_map/ppermute | solution.py:17
  91.5 8.9 %collective-permute-start.11 = (bf16[2,128,1,128]{1,3,2,0:T(8,128)(2,1)S(1)}, bf16[2,128,1,128]{1,3,2,0:T(8,128)(2,1)S(1)}, u32[]{:S(2)}, u32[]{:S(2)}) collective-permute-start(bf16[2,128,1,128]{1,3,2,0:T(8,128)(2,1)S(1)} %get-tuple-element.220), channel_id=1, source_target_pairs={{1,0},{2,1},{3,2},{4,3},{5,4},{6,5},{7,6},{8,7},{9,8},{10,9},{11,1... | collective-permute-start | bytes 196616 | tf_op jit(solution)/shard_map/ppermute | solution.py:18
  103.7 1.3 %copy-start.8 = (f32[2,4,8,128]{3,2,1,0:T(8,128)S(1)}, f32[2,4,8,128]{3,2,1,0:T(8,128)}, u32[]{:S(2)}) copy-start(f32[2,4,8,128]{3,2,1,0:T(8,128)} %param.14) | copy-start | bytes 98308
where the time goes:
time: 122 us; the launch traced here: 120 us
  starting transfers between devices  53.8 us (44%)
  matrix products  27.6 us (23%)
  blocking collectives  23.7 us (19%)
  waiting for transfers between devices  9.96 us (8%)
  local copies, waits for them, and re-layouts  2.23 us (2%)
  other arithmetic  1.76 us (1%)
    ppermute x6, starting transfers between devices, with_halo(): after = lax.ppermute(leading, axis, down)  42 us
    all_gather x2, blocking collectives, carried_in(): everything = lax.all_gather(x, axis)  23.7 us
    dot_general x52, matrix products, conv_cols(): jnp.einsum('oi,sicr->socr', weight[3 * col_off + row_off], piece, preferr...  23.1 us
    ppermute x6, starting transfers between devices, with_halo(): before = lax.ppermute(last, axis, up)  11.8 us
    ppermute x6, waiting for transfers between devices, with_halo(): after = lax.ppermute(leading, axis, down)  9.94 us
    dot_general x2, matrix products, local(): jnp.einsum('oi,sicr->socr', w_out, block_out, preferred_element_type=jnp....  4.52 us
  transfers between devices with their start and end apart: 12, of which 6 were waited for; matrix products, arithmetic and copies ran while one was open for 0% of the time, Pallas kernels for 0%

commit v1 on v0

v1 whole, which is shorter than its diff:
```python
import jax
import jax.numpy as jnp
from jax import lax
from jax.experimental import pallas as pl
from jax.experimental.pallas import tpu as pltpu
from jax.sharding import PartitionSpec as P

STEPS = 8
SWEEPS = 2
HALO = 3
BF = jnp.bfloat16
F32 = jnp.float32
MESH = pl.DeviceIdType.MESH


def silu(v):
    h = 0.5 * v
    return h * jnp.tanh(h) + h


def kernel(
    groups,
    tiles,
    start_ref,
    cov_ref,
    noise_ref,
    embed_ref,
    win_hbm,
    wfirst_hbm,
    wsecond_hbm,
    wout_ref,
    out_ref,
    x_ref,
    covf_ref,
    xs_ref,
    win_ref,
    w1_ref,
    w2_ref,
    w3_ref,
    wo_ref,
    eb_ref,
    nz_ref,
    fh_ref,
    sh_ref,
    bo_ref,
    part_ref,
    part_a,
    part_g,
    rx_ref,
    rxs_ref,
    rxf_ref,
    w_sem,
    halo_send,
    halo_recv,
    full_send,
    full_recv,
    edge_send,
    edge_recv,
    near_send,
    near_recv,
    last_send,
    last_recv,
):
    k = lax.axis_index("step")
    t = lax.axis_index("tile")
    cols = start_ref.shape[1]
    wide = cols + 2 * HALO
    rows = 128
    edge = HALO * rows
    has_left = t > 0
    has_right = t < tiles - 1

    win_copy = pltpu.make_async_copy(win_hbm, win_ref, w_sem.at[0])
    win_copy.start()
    copies = []
    for n, (src, dst) in enumerate(((wfirst_hbm, w2_ref), (wsecond_hbm, w3_ref))):
        group = []
        for tap in range(9):
            c = pltpu.make_async_copy(
                src.at[tap], dst.at[:, pl.ds(tap * 128, 128)], w_sem.at[1 + 9 * n + tap]
            )
            c.start()
            group.append(c)
        copies.append(group)

    barrier = pltpu.get_barrier_semaphore()

    def signal(step, tile):
        pl.semaphore_signal(barrier, inc=1, device_id=(step, tile), device_id_type=MESH)

    for side, there in ((-1, has_left), (1, has_right)):

        @pl.when(there)
        def _():
            signal(k, t + side)

        for d in range(1, groups):

            @pl.when(there & (k >= d))
            def _():
                signal(k - d, t + side)

    for d in range(1, groups):

        @pl.when(k >= d)
        def _():
            signal(k - d, t)

    sides = has_left.astype(jnp.int32) + has_right.astype(jnp.int32)
    later = groups - 1 - k

    covf_ref[...] = cov_ref[...].astype(F32)
    for c in range(cols):
        at = pl.ds((HALO + c) * rows, rows)
        x_ref[0:4, at] = start_ref[:, c, :]
        x_ref[4:16, at] = covf_ref[:, c, :]

    pl.semaphore_wait(barrier, sides + later * (1 + sides))

    def remote(src, dst, send, recv, step, tile):
        return pltpu.make_async_remote_copy(
            src_ref=src,
            dst_ref=dst,
            send_sem=send,
            recv_sem=recv,
            device_id=(step, tile),
            device_id_type=MESH,
        )

    own = pl.ds(HALO * rows, cols * rows)
    own_first = pl.ds(HALO * rows, edge)
    own_last = pl.ds(cols * rows, edge)
    left_halo = pl.ds(0, edge)
    right_halo = pl.ds((HALO + cols) * rows, edge)
    first_edge = pl.ds(0, edge)
    last_edge = pl.ds((cols - HALO) * rows, edge)

    def halo_left():
        return remote(
            x_ref.at[:, own_first], x_ref.at[:, right_halo], halo_send.at[0], halo_recv.at[0], k, t - 1
        )

    def halo_right():
        return remote(
            x_ref.at[:, own_last], x_ref.at[:, left_halo], halo_send.at[1], halo_recv.at[1], k, t + 1
        )

    @pl.when(has_left)
    def _():
        halo_left().start()

    @pl.when(has_right)
    def _():
        halo_right().start()

    @pl.when(jnp.logical_not(has_left))
    def _():
        x_ref[:, left_halo] = jnp.zeros((16, edge), F32)

    @pl.when(jnp.logical_not(has_right))
    def _():
        x_ref[:, right_halo] = jnp.zeros((16, edge), F32)

    win_copy.wait()
    w1_ref[...] = jnp.concatenate([win_ref[tap] for tap in range(9)], axis=1)
    wo = wout_ref[...]
    zero_wo = jnp.zeros_like(wo)
    wo_ref[0:4, 0:128] = wo
    wo_ref[0:4, 128:256] = zero_wo
    wo_ref[4:8, 0:128] = wo
    wo_ref[4:8, 128:256] = wo
    et = jnp.transpose(jnp.concatenate([embed_ref[...], jnp.zeros((6, 128), F32)], axis=0))
    for s in range(2):
        eb_ref[s] = jnp.broadcast_to(et[:, s : s + 1], (128, 128))
    for c in range(cols):
        at = pl.ds(c * rows, rows)
        n0 = 0.3 * noise_ref[0, :, c, :]
        nz_ref[0:4, at] = n0
        nz_ref[4:8, at] = n0 + 0.3 * noise_ref[1, :, c, :]

    @pl.when(has_left)
    def _():
        halo_left().wait_send()

    @pl.when(has_right)
    def _():
        halo_right().wait_send()

    @pl.when(has_left)
    def _():
        halo_right().wait_recv()

    @pl.when(has_right)
    def _():
        halo_left().wait_recv()

    lane = lax.broadcasted_iota(jnp.int32, (1, 2 * rows), 1) % rows
    keep_first = (lane > 0).astype(F32)
    keep_last = (lane < rows - 1).astype(F32)

    def store_taps(ref, value, lo, width):
        n = value.shape[0]
        for part in range(width):
            v = value[:, part * rows : (part + 1) * rows]
            at = pl.ds(lo + part * rows, rows)
            ref[0:n, at] = (pltpu.roll(v, 1, 1) * keep_first[:, :rows]).astype(BF)
            ref[n : 2 * n, at] = v.astype(BF)
            ref[2 * n : 3 * n, at] = (pltpu.roll(v, rows - 1, 1) * keep_last[:, :rows]).astype(BF)

    def taps_of(ref, lo):
        return jnp.concatenate(
            [ref[:, pl.ds(lo + a * rows, 2 * rows)] for a in range(3)], axis=0
        )

    left_one = has_left.astype(F32)
    right_one = has_right.astype(F32)

    def masked(v, pair, first_real, last_real):
        if pair < first_real:
            return v * left_one
        if pair >= last_real:
            return v * right_one
        return v

    half = HALO - 1
    for sweep in range(SWEEPS):
        for s in range(2):
            if sweep == 0 and s == 1:
                continue
            for c in range(wide):
                at = pl.ds(c * rows, rows)
                v = x_ref[:, at]
                if sweep == 1:
                    base = jnp.zeros((4, rows), F32)
                    for d in range(1, groups):
                        base = base + jnp.where(k >= d, rx_ref[d - 1, :, at], 0.0)
                    if s == 1:
                        base = base + rxs_ref[:, at]
                    state = v[0:4] + base
                    if c < HALO:
                        state = state * left_one
                    if c >= HALO + cols:
                        state = state * right_one
                    v = jnp.concatenate([state, v[4:16]], axis=0)
                store_taps(xs_ref.at[s], v, c * rows, 1)

        for pair in range((wide - 2) // 2):
            lo = pair * 2 * rows
            for s in range(2):
                if s == 0 or sweep == 1:
                    pre = jnp.dot(w1_ref[...], taps_of(xs_ref.at[s], lo), preferred_element_type=F32)
                e = eb_ref[s]
                h = silu(pre + jnp.concatenate([e, e], axis=1))
                h = masked(h, pair, 1, 1 + cols // 2)
                store_taps(fh_ref.at[s], h, lo, 2)

        if sweep == 0:
            for c in copies[0]:
                c.wait()
        for pair in range((cols + 2) // 2):
            lo = pair * 2 * rows
            for s in range(2):
                h = silu(jnp.dot(w2_ref[...], taps_of(fh_ref.at[s], lo), preferred_element_type=F32))
                if pair == 0:
                    h = jnp.concatenate([h[:, :rows] * left_one, h[:, rows:]], axis=1)
                if pair == cols // 2:
                    h = jnp.concatenate([h[:, :rows], h[:, rows:] * right_one], axis=1)
                store_taps(sh_ref.at[s], h, lo, 2)

        if sweep == 0:
            for c in copies[1]:
                c.wait()
        for pair in range(cols // 2):
            lo = pair * 2 * rows
            at = pl.ds(lo, 2 * rows)
            for s in range(2):
                h = silu(jnp.dot(w3_ref[...], taps_of(sh_ref.at[s], lo), preferred_element_type=F32))
                first = fh_ref[s, 128:256, pl.ds(lo + half * rows, 2 * rows)].astype(F32)
                bo_ref[128 * s : 128 * (s + 1), at] = (h + first).astype(BF)
            sums = jnp.dot(wo_ref[...], bo_ref[:, at], preferred_element_type=F32)
            sums = sums * (1.0 / STEPS) + nz_ref[:, at]
            part_ref[:, at] = sums
            part_a[:, at] = sums[0:4]
            part_g[sweep, :, at] = sums[4:8]

        if sweep == 0:
            rxs_ref[:, own] = part_a[...]

            def near_left():
                return remote(
                    part_a.at[:, first_edge], rxs_ref.at[:, right_halo], near_send.at[0], near_recv.at[0], k, t - 1
                )

            def near_right():
                return remote(
                    part_a.at[:, last_edge], rxs_ref.at[:, left_halo], near_send.at[1], near_recv.at[1], k, t + 1
                )

            def full(d):
                return remote(
                    part_g.at[0],
                    rx_ref.at[d - 1, :, own],
                    full_send.at[d - 1],
                    full_recv.at[d - 1],
                    k + d,
                    t,
                )

            def edge_left(d):
                return remote(
                    part_g.at[0, :, first_edge],
                    rx_ref.at[d - 1, :, right_halo],
                    edge_send.at[d - 1, 0],
                    edge_recv.at[d - 1, 0],
                    k + d,
                    t - 1,
                )

            def edge_right(d):
                return remote(
                    part_g.at[0, :, last_edge],
                    rx_ref.at[d - 1, :, left_halo],
                    edge_send.at[d - 1, 1],
                    edge_recv.at[d - 1, 1],
                    k + d,
                    t + 1,
                )

            def each(act_near_l, act_near_r, act_full, act_l, act_r, sending):
                for d in range(groups - 1, 0, -1):
                    reach = (k + d < groups) if sending else (k >= d)
                    pl.when(reach & has_left)(lambda d=d: act_l(d))
                    pl.when(reach & has_right)(lambda d=d: act_r(d))
                    pl.when(reach)(lambda d=d: act_full(d))
                pl.when(has_left)(act_near_l)
                pl.when(has_right)(act_near_r)

            each(
                lambda: near_left().start(),
                lambda: near_right().start(),
                lambda d: full(d).start(),
                lambda d: edge_left(d).start(),
                lambda d: edge_right(d).start(),
                True,
            )
            each(
                lambda: near_right().wait_recv(),
                lambda: near_left().wait_recv(),
                lambda d: full(d).wait_recv(),
                lambda d: edge_right(d).wait_recv(),
                lambda d: edge_left(d).wait_recv(),
                False,
            )
            each(
                lambda: near_left().wait_send(),
                lambda: near_right().wait_send(),
                lambda d: full(d).wait_send(),
                lambda d: edge_left(d).wait_send(),
                lambda d: edge_right(d).wait_send(),
                True,
            )

    def last(d):
        return remote(
            part_g.at[1], rxf_ref.at[d - 1], last_send.at[d - 1], last_recv.at[d - 1], k + d, t
        )

    for d in range(groups - 1, 0, -1):
        pl.when(k + d < groups)(lambda d=d: last(d).start())
    for d in range(1, groups):
        pl.when(k >= d)(lambda d=d: last(d).wait_recv())
    for c in range(cols):
        at = pl.ds(c * rows, rows)
        base = start_ref[:, c, :]
        for d in range(1, groups):
            base = base + jnp.where(k >= d, rxf_ref[d - 1, :, at], 0.0)
        out_ref[0, :, c, :] = base + part_ref[0:4, at]
        out_ref[1, :, c, :] = base + part_ref[4:8, at]
    for d in range(groups - 1, 0, -1):
        pl.when(k + d < groups)(lambda d=d: last(d).wait_send())


def solution(mesh):
    groups, tiles = mesh.shape["step"], mesh.shape["tile"]

    def local(start_state, covariates, noise, embedding, w_in, w_first, w_second, w_out):
        cols = start_state.shape[1]
        wide = cols + 2 * HALO
        cells = cols * 128
        vmem = pl.BlockSpec(memory_space=pltpu.VMEM)
        hbm = pl.BlockSpec(memory_space=pl.ANY)
        dma = pltpu.SemaphoreType.DMA

        def body(*refs):
            kernel(groups, tiles, *refs)

        return pl.pallas_call(
            body,
            out_shape=jax.ShapeDtypeStruct((2, 4, cols, 128), F32),
            in_specs=[vmem, vmem, vmem, vmem, hbm, hbm, hbm, vmem],
            out_specs=vmem,
            scratch_shapes=[
                pltpu.VMEM((16, wide * 128), F32),
                pltpu.VMEM((12, cols, 128), F32),
                pltpu.VMEM((2, 48, wide * 128), BF),
                pltpu.VMEM((9, 128, 16), BF),
                pltpu.VMEM((128, 144), BF),
                pltpu.VMEM((128, 1152), BF),
                pltpu.VMEM((128, 1152), BF),
                pltpu.VMEM((8, 256), BF),
                pltpu.VMEM((2, 128, 128), F32),
                pltpu.VMEM((8, cells), F32),
                pltpu.VMEM((2, 384, (wide - 2) * 128), BF),
                pltpu.VMEM((2, 384, (wide - 4) * 128), BF),
                pltpu.VMEM((256, cells), BF),
                pltpu.VMEM((8, cells), F32),
                pltpu.VMEM((4, cells), F32),
                pltpu.VMEM((2, 4, cells), F32),
                pltpu.VMEM((groups - 1, 4, wide * 128), F32),
                pltpu.VMEM((4, wide * 128), F32),
                pltpu.VMEM((groups - 1, 4, cells), F32),
                dma((19,)),
                dma((2,)),
                dma((2,)),
                dma((groups - 1,)),
                dma((groups - 1,)),
                dma((groups - 1, 2)),
                dma((groups - 1, 2)),
                dma((2,)),
                dma((2,)),
                dma((groups - 1,)),
                dma((groups - 1,)),
            ],
            compiler_params=pltpu.CompilerParams(
                collective_id=0, has_side_effects=True, vmem_limit_bytes=40 << 20
            ),
        )(start_state, covariates, noise, embedding, w_in, w_first, w_second, w_out)

    in_specs = (
        P(None, "tile", None),
        P(None, "tile", None),
        P("step", None, "tile", None),
        P("step", None),
        P(),
        P(),
        P(),
        P(),
    )
    out_specs = P("step", None, "tile", None)
    return jax.shard_map(local, mesh=mesh, in_specs=in_specs, out_specs=out_specs, check_vma=False)
```

time: 122 us -> 28.1 us (0.23)
  the two profiles are of different devices: /device:TPU:152 before, /device:TPU:127 now
where the time goes in v1:
time: 28.1 us; the launch traced here: 27.9 us
  Pallas kernels  23.8 us (85%)
  local copies, waits for them, and re-layouts  4.07 us (14%)
    pallas_call x1, Pallas kernels, local(): pl.pallas_call(body, out_shape=jax.ShapeDtypeStruct((2, 4, cols, 128), F3...  23.8 us
    unnamed x16, local copies, waits for them, and re-layouts  4.07 us

profile of v1, /device:TPU:127, one launch (start us, length us, event | category | flops | bytes accessed | tf_op | source)
XLA Modules:
  0.0 27.9 jit_solution(2701232289163084019)
XLA Ops:
  0.0 0.0 copy-start.6
  0.0 0.0 copy-start
  0.0 0.0 copy-start.5
  0.0 0.0 copy-start.2
  0.0 1.0 %copy.9.refs_4_ = bf16[9,128,16]{2,1,0:T(8,128)(2,1)S(1)} copy(bf16[9,128,16]{1,2,0:T(8,128)(2,1)} %param.12) | data formatting | bytes 73728 | tf_op args[4]
  1.0 0.0 copy-done.6
  1.1 0.0 copy-done
  1.1 0.0 copy-done.5
  1.1 0.0 copy-done.2
  1.1 0.0 copy-start.1
  1.1 1.0 %copy-done.1 = bf16[9,128,128]{2,1,0:T(8,128)(2,1)S(1)} copy-done((bf16[9,128,128]{2,1,0:T(8,128)(2,1)S(1)}, bf16[9,128,128]{2,1,0:T(8,128)(2,1)}, u32[]{:S(2)}) %copy-start.1) | copy-done | bytes 294936
  2.1 0.0 copy-start.3
  2.1 0.7 %copy-done.3 = bf16[12,8,128]{2,1,0:T(8,128)(2,1)S(1)} copy-done((bf16[12,8,128]{2,1,0:T(8,128)(2,1)S(1)}, bf16[12,8,128]{2,1,0:T(8,128)(2,1)}, u32[]{:S(2)}) %copy-start.3) | copy-done | bytes 24600
  2.8 0.0 copy-start.4
  2.8 0.7 %copy-done.4 = f32[4,8,128]{2,1,0:T(8,128)S(1)} copy-done((f32[4,8,128]{2,1,0:T(8,128)S(1)}, f32[4,8,128]{2,1,0:T(8,128)}, u32[]{:S(2)}) %copy-start.4) | copy-done | bytes 16408
  3.5 23.8 %shard_map.82 = f32[2,4,8,128]{3,2,1,0:T(8,128)S(1)} custom-call(f32[4,8,128]{2,1,0:T(8,128)S(1)} %copy-done.4, bf16[12,8,128]{2,1,0:T(8,128)(2,1)S(1)} %copy-done.3, f32[2,4,8,128]{3,2,1,0:T(8,128)S(1)} %copy-done.2, f32[2,128]{1,0:T(2,128)S(1)} %copy-done.5, bf16[9,128,16]{2,1,0:T(8,128)(2,1)S(1)} %copy.9.refs_4_, bf16[9,128,128]{2,1,0:T(8,128)(2,1)S(1)} %copy-done, ...), custom_call_target="tpu_custom_call" | custom-call | tf_op jit(solution)/shard_map/pallas_call | solution.py:397
  27.3 0.6 %copy.11 = f32[2,4,8,128]{3,2,1,0:T(8,128)} copy(f32[2,4,8,128]{3,2,1,0:T(8,128)S(1)} %shard_map.82) | data formatting | bytes 65536
Async XLA Ops:
  0.0 1.0 %copy-start.6 = (bf16[4,128]{1,0:T(4,128)(2,1)S(1)}, bf16[4,128]{1,0:T(4,128)(2,1)}, u32[]{:S(2)}) copy-start(bf16[4,128]{1,0:T(4,128)(2,1)} %refs_7_.1) | copy-start | bytes 3076
  0.0 1.1 %copy-start = (bf16[9,128,128]{2,1,0:T(8,128)(2,1)S(1)}, bf16[9,128,128]{2,1,0:T(8,128)(2,1)}, u32[]{:S(2)}) copy-start(bf16[9,128,128]{2,1,0:T(8,128)(2,1)} %refs_5_.1) | copy-start | bytes 884740
  0.0 1.1 %copy-start.5 = (f32[2,128]{1,0:T(2,128)S(1)}, f32[2,128]{1,0:T(2,128)}, u32[]{:S(2)}) copy-start(f32[2,128]{1,0:T(2,128)} %refs_3_.1) | copy-start | bytes 3076
  0.0 1.1 %copy-start.2 = (f32[2,4,8,128]{3,2,1,0:T(8,128)S(1)}, f32[2,4,8,128]{3,2,1,0:T(8,128)}, u32[]{:S(2)}) copy-start(f32[2,4,8,128]{3,2,1,0:T(8,128)} %refs_2_.1) | copy-start | bytes 98308
  1.1 1.0 %copy-start.1 = (bf16[9,128,128]{2,1,0:T(8,128)(2,1)S(1)}, bf16[9,128,128]{2,1,0:T(8,128)(2,1)}, u32[]{:S(2)}) copy-start(bf16[9,128,128]{2,1,0:T(8,128)(2,1)} %refs_6_.1) | copy-start | bytes 884740
  2.1 0.7 %copy-start.3 = (bf16[12,8,128]{2,1,0:T(8,128)(2,1)S(1)}, bf16[12,8,128]{2,1,0:T(8,128)(2,1)}, u32[]{:S(2)}) copy-start(bf16[12,8,128]{2,1,0:T(8,128)(2,1)} %refs_1_.1) | copy-start | bytes 73732
  2.8 0.7 %copy-start.4 = (f32[4,8,128]{2,1,0:T(8,128)S(1)}, f32[4,8,128]{2,1,0:T(8,128)}, u32[]{:S(2)}) copy-start(f32[4,8,128]{2,1,0:T(8,128)} %refs_0_.1) | copy-start | bytes 49156

commit v2 on v0

v2 whole, which is shorter than its diff:
```python
import jax
import jax.numpy as jnp
from jax import lax
from jax.experimental import pallas as pl
from jax.experimental.pallas import tpu as pltpu
from jax.sharding import PartitionSpec as P

STEPS = 8
SWEEPS = 2
HALO = 3
ROWS = 128
BF = jnp.bfloat16
F32 = jnp.float32
MESH = pl.DeviceIdType.MESH


def silu_of_half(h):
    return h * jnp.tanh(h) + h


def kernel(
    groups,
    tiles,
    start_hbm,
    cov_hbm,
    noise_hbm,
    embed_hbm,
    win_hbm,
    wfirst_hbm,
    wsecond_hbm,
    wout_hbm,
    out_ref,
    start_ref,
    cov_ref,
    noise_ref,
    embed_ref,
    win_ref,
    wout_ref,
    covf_ref,
    st_ref,
    xb_ref,
    xs_ref,
    w1_ref,
    w2_ref,
    w3_ref,
    wo_ref,
    eb_ref,
    nz_ref,
    fh_ref,
    sh_ref,
    bo_ref,
    part_ref,
    part_a,
    part_g,
    rx_ref,
    rxs_ref,
    rxf_ref,
    in_sem,
    w_sem,
    halo_send,
    halo_recv,
    rim_send,
    rim_recv,
    full_send,
    full_recv,
    edge_send,
    edge_recv,
    near_send,
    near_recv,
    last_send,
    last_recv,
):
    k = lax.axis_index("step")
    t = lax.axis_index("tile")
    cols = start_ref.shape[1]
    wide = cols + 2 * HALO
    edge = HALO * ROWS
    has_left = t > 0
    has_right = t < tiles - 1

    local = [
        pltpu.make_async_copy(src, dst, in_sem.at[n])
        for n, (src, dst) in enumerate(
            (
                (start_hbm, start_ref),
                (cov_hbm, cov_ref),
                (win_hbm, win_ref),
                (embed_hbm, embed_ref),
                (noise_hbm, noise_ref),
                (wout_hbm, wout_ref),
            )
        )
    ]
    get_start, get_cov, get_win, get_embed, get_noise, get_wout = local
    weights = []
    for n, (src, dst) in enumerate(((wfirst_hbm, w2_ref), (wsecond_hbm, w3_ref))):
        weights.append(
            [
                pltpu.make_async_copy(src.at[tap], dst.at[:, pl.ds(tap * 128, 128)], w_sem.at[n, tap])
                for tap in range(9)
            ]
        )

    barrier = pltpu.get_barrier_semaphore()

    def signal(step, tile):
        pl.semaphore_signal(barrier, inc=1, device_id=(step, tile), device_id_type=MESH)

    get_start.start()
    get_cov.start()
    for side, there in ((-1, has_left), (1, has_right)):

        @pl.when(there)
        def _():
            signal(k, t + side)

    for d in range(1, groups):

        @pl.when(k >= d)
        def _():
            signal(k - d, t)

    for d in range(1, groups):
        for side, there in ((-1, has_left), (1, has_right)):

            @pl.when(there & (k >= d))
            def _():
                signal(k - d, t + side)

    for c in (get_win, get_embed, get_noise, get_wout, *weights[0], *weights[1]):
        c.start()

    get_cov.wait()
    covf_ref[...] = cov_ref[...].astype(F32)
    get_start.wait()
    for c in range(cols):
        at = pl.ds((HALO + c) * ROWS, ROWS)
        state = start_ref[:, c, :]
        st_ref[:, at] = state
        xb_ref[:, at] = jnp.concatenate([state, covf_ref[:, c, :]], axis=0).astype(BF)

    sides = has_left.astype(jnp.int32) + has_right.astype(jnp.int32)
    pl.semaphore_wait(barrier, sides + (groups - 1 - k) * (1 + sides))

    def remote(src, dst, send, recv, step, tile):
        return pltpu.make_async_remote_copy(
            src_ref=src,
            dst_ref=dst,
            send_sem=send,
            recv_sem=recv,
            device_id=(step, tile),
            device_id_type=MESH,
        )

    own = pl.ds(HALO * ROWS, cols * ROWS)
    own_first = pl.ds(HALO * ROWS, edge)
    own_last = pl.ds(cols * ROWS, edge)
    left_halo = pl.ds(0, edge)
    right_halo = pl.ds((HALO + cols) * ROWS, edge)
    first_edge = pl.ds(0, edge)
    last_edge = pl.ds((cols - HALO) * ROWS, edge)

    def to_left(ref, send, recv):
        return remote(ref.at[:, own_first], ref.at[:, right_halo], send.at[0], recv.at[0], k, t - 1)

    def to_right(ref, send, recv):
        return remote(ref.at[:, own_last], ref.at[:, left_halo], send.at[1], recv.at[1], k, t + 1)

    halo = (xb_ref, halo_send, halo_recv)
    rim = (st_ref, rim_send, rim_recv)
    pl.when(has_left)(lambda: to_left(*halo).start())
    pl.when(has_right)(lambda: to_right(*halo).start())
    pl.when(has_left)(lambda: to_left(*rim).start())
    pl.when(has_right)(lambda: to_right(*rim).start())

    @pl.when(jnp.logical_not(has_left))
    def _():
        xb_ref[:, left_halo] = jnp.zeros((16, edge), BF)

    @pl.when(jnp.logical_not(has_right))
    def _():
        xb_ref[:, right_halo] = jnp.zeros((16, edge), BF)

    get_win.wait()
    w1_ref[...] = jnp.transpose(win_ref[...].astype(F32) * 0.5).astype(BF)
    get_embed.wait()
    et = 0.5 * jnp.transpose(jnp.concatenate([embed_ref[...], jnp.zeros((6, 128), F32)], axis=0))
    for s in range(2):
        eb_ref[s] = jnp.broadcast_to(et[:, s : s + 1], (128, 128))

    lane = lax.broadcasted_iota(jnp.int32, (1, ROWS), 1)
    keep_first = (lane > 0).astype(F32).astype(BF)
    keep_last = (lane < ROWS - 1).astype(F32).astype(BF)
    left_one = has_left.astype(F32)
    right_one = has_right.astype(F32)
    ones = jnp.ones((1, ROWS), F32)
    outside = jnp.concatenate([ones * left_one, ones * right_one], axis=1)

    def store_taps(ref, v, slot):
        n = v.shape[0]
        at = pl.ds(slot * ROWS, ROWS)
        ref[0:n, at] = pltpu.roll(v, 1, 1) * keep_first
        ref[n : 2 * n, at] = v
        ref[2 * n : 3 * n, at] = pltpu.roll(v, ROWS - 1, 1) * keep_last

    def taps_of(ref, pair):
        return jnp.concatenate(
            [
                jnp.concatenate([ref[:, pl.ds((c + a) * ROWS, ROWS)] for c in pair], axis=1)
                for a in range(3)
            ],
            axis=0,
        )

    def first_pre(s, pair):
        return jnp.dot(
            w1_ref[...], taps_of(xs_ref.at[s], [c + 2 for c in pair]), preferred_element_type=F32
        )

    def first_store(s, pair, pre):
        e = eb_ref[s]
        h = silu_of_half(pre + jnp.concatenate([e, e], axis=1))
        if pair[0] < 0:
            h = h * outside
        h = h.astype(BF)
        for n, c in enumerate(pair):
            store_taps(fh_ref.at[s], h[:, n * ROWS : (n + 1) * ROWS], c + 2)

    def second(s, pair):
        h = jnp.dot(
            w2_ref[...], taps_of(fh_ref.at[s], [c + 1 for c in pair]), preferred_element_type=F32
        )
        h = silu_of_half(h)
        if pair[0] < 0:
            h = h * outside
        h = h.astype(BF)
        for n, c in enumerate(pair):
            store_taps(sh_ref.at[s], h[:, n * ROWS : (n + 1) * ROWS], c + 1)

    def block(s, pair):
        h = jnp.dot(
            w3_ref[...], taps_of(sh_ref.at[s], list(pair)), preferred_element_type=F32
        )
        h = silu_of_half(h)
        for n, c in enumerate(pair):
            first = fh_ref[s, 128:256, pl.ds((c + 2) * ROWS, ROWS)].astype(F32)
            at = pl.ds(c * ROWS, ROWS)
            bo_ref[128 * s : 128 * (s + 1), at] = (h[:, n * ROWS : (n + 1) * ROWS] + first).astype(BF)

    def project(sweep, pair):
        ats = [pl.ds(c * ROWS, ROWS) for c in pair]
        sums = jnp.dot(
            wo_ref[...],
            jnp.concatenate([bo_ref[:, at] for at in ats], axis=1),
            preferred_element_type=F32,
        )
        for n, at in enumerate(ats):
            v = sums[:, n * ROWS : (n + 1) * ROWS] * (1.0 / STEPS) + nz_ref[:, at]
            part_ref[:, at] = v
            if sweep == 0:
                part_a[:, at] = v[0:4]
            part_g[sweep, :, at] = v[4:8]

    mid = cols // 2
    first_in = [(c, c + 1) for c in range(1, cols - 1, 2)]
    first_out = [(c, cols - 1 - c) for c in (-2, -1, 0)]
    second_in = [(c, c + 1) for c in range(2, cols - 2, 2)]
    second_out = [(c, cols - 1 - c) for c in (1, 0, -1)]
    block_in = [(c, c + 1) for c in range(3, cols - 3, 2)]
    block_out = [(c, cols - 1 - c) for c in (2, 1, 0)]

    def inputs_first(c):
        store_taps(xs_ref.at[0], xb_ref[:, pl.ds((c + HALO) * ROWS, ROWS)], c + HALO)

    for c in range(cols):
        inputs_first(c)
    for pair in first_in:
        pre = first_pre(0, pair)
        for s in range(2):
            first_store(s, pair, pre)
    for c in weights[0]:
        c.wait()
    w2_ref[...] = w2_ref[...] * BF(0.5)
    for s in range(2):
        for pair in second_in:
            second(s, pair)
    for c in weights[1]:
        c.wait()
    w3_ref[...] = w3_ref[...] * BF(0.5)
    for s in range(2):
        for pair in block_in:
            block(s, pair)
    get_wout.wait()
    wo = wout_ref[...]
    zero_wo = jnp.zeros_like(wo)
    wo_ref[0:4, 0:128] = wo
    wo_ref[0:4, 128:256] = zero_wo
    wo_ref[4:8, 0:128] = wo
    wo_ref[4:8, 128:256] = wo
    get_noise.wait()
    for c in range(cols):
        at = pl.ds(c * ROWS, ROWS)
        n0 = 0.3 * noise_ref[0, :, c, :]
        nz_ref[0:4, at] = n0
        nz_ref[4:8, at] = n0 + 0.3 * noise_ref[1, :, c, :]
    for pair in block_in:
        project(0, pair)

    pl.when(has_left)(lambda: to_right(*halo).wait_recv())
    pl.when(has_right)(lambda: to_left(*halo).wait_recv())

    for c in (*range(-HALO, 0), *range(cols, cols + HALO)):
        inputs_first(c)
    pres = [first_pre(0, pair) for pair in first_out]
    for s in range(2):
        for pair, pre in zip(first_out, pres):
            first_store(s, pair, pre)
    for s in range(2):
        for pair in second_out:
            second(s, pair)
    for s in range(2):
        for pair in block_out:
            block(s, pair)
    for pair in block_out:
        project(0, pair)

    def near_left():
        return remote(
            part_a.at[:, first_edge], rxs_ref.at[:, right_halo], near_send.at[0], near_recv.at[0], k, t - 1
        )

    def near_right():
        return remote(
            part_a.at[:, last_edge], rxs_ref.at[:, left_halo], near_send.at[1], near_recv.at[1], k, t + 1
        )

    def full(d):
        return remote(
            part_g.at[0], rx_ref.at[d - 1, :, own], full_send.at[d - 1], full_recv.at[d - 1], k + d, t
        )

    def edge_left(d):
        return remote(
            part_g.at[0, :, first_edge],
            rx_ref.at[d - 1, :, right_halo],
            edge_send.at[d - 1, 0],
            edge_recv.at[d - 1, 0],
            k + d,
            t - 1,
        )

    def edge_right(d):
        return remote(
            part_g.at[0, :, last_edge],
            rx_ref.at[d - 1, :, left_halo],
            edge_send.at[d - 1, 1],
            edge_recv.at[d - 1, 1],
            k + d,
            t + 1,
        )

    for d in range(groups - 1, 0, -1):
        pl.when((k + d < groups) & has_left)(lambda d=d: edge_left(d).start())
        pl.when((k + d < groups) & has_right)(lambda d=d: edge_right(d).start())
    for d in range(groups - 1, 0, -1):
        pl.when(k + d < groups)(lambda d=d: full(d).start())
    pl.when(has_left)(lambda: near_left().start())
    pl.when(has_right)(lambda: near_right().start())
    rxs_ref[:, own] = part_a[...]

    pl.when(has_left)(lambda: to_right(*rim).wait_recv())
    pl.when(has_right)(lambda: to_left(*rim).wait_recv())
    pl.when(has_left)(lambda: near_right().wait_recv())
    pl.when(has_right)(lambda: near_left().wait_recv())
    for d in range(1, groups):
        pl.when(k >= d)(lambda d=d: full(d).wait_recv())
        pl.when((k >= d) & has_left)(lambda d=d: edge_right(d).wait_recv())
        pl.when((k >= d) & has_right)(lambda d=d: edge_left(d).wait_recv())

    for c in range(-HALO, cols + HALO):
        at = pl.ds((c + HALO) * ROWS, ROWS)
        base = st_ref[:, at]
        for d in range(1, groups):
            base = base + jnp.where(k >= d, rx_ref[d - 1, :, at], 0.0)
        cov = xb_ref[:, at].astype(F32)[4:16]
        for s in range(2):
            state = base + rxs_ref[:, at] if s == 1 else base
            if c < 0:
                state = jnp.where(has_left, state, 0.0)
            if c >= cols:
                state = jnp.where(has_right, state, 0.0)
            v = jnp.concatenate([state, cov], axis=0).astype(BF)
            store_taps(xs_ref.at[s], v, c + HALO)
    for s in range(2):
        for pair in first_out + first_in:
            first_store(s, pair, first_pre(s, pair))
    for s in range(2):
        for pair in second_out + second_in:
            second(s, pair)
    for s in range(2):
        for pair in block_out + block_in:
            block(s, pair)
    for pair in block_out + block_in:
        project(1, pair)

    def last(d):
        return remote(
            part_g.at[1], rxf_ref.at[d - 1], last_send.at[d - 1], last_recv.at[d - 1], k + d, t
        )

    for d in range(groups - 1, 0, -1):
        pl.when(k + d < groups)(lambda d=d: last(d).start())

    pl.when(has_left)(lambda: to_left(*halo).wait_send())
    pl.when(has_right)(lambda: to_right(*halo).wait_send())
    pl.when(has_left)(lambda: to_left(*rim).wait_send())
    pl.when(has_right)(lambda: to_right(*rim).wait_send())
    pl.when(has_left)(lambda: near_left().wait_send())
    pl.when(has_right)(lambda: near_right().wait_send())
    for d in range(1, groups):
        pl.when(k + d < groups)(lambda d=d: full(d).wait_send())
        pl.when((k + d < groups) & has_left)(lambda d=d: edge_left(d).wait_send())
        pl.when((k + d < groups) & has_right)(lambda d=d: edge_right(d).wait_send())

    for d in range(1, groups):
        pl.when(k >= d)(lambda d=d: last(d).wait_recv())
    for c in range(cols):
        at = pl.ds(c * ROWS, ROWS)
        base = start_ref[:, c, :]
        for d in range(1, groups):
            base = base + jnp.where(k >= d, rxf_ref[d - 1, :, at], 0.0)
        out_ref[0, :, c, :] = base + part_ref[0:4, at]
        out_ref[1, :, c, :] = base + part_ref[4:8, at]
    for d in range(1, groups):
        pl.when(k + d < groups)(lambda d=d: last(d).wait_send())


def solution(mesh):
    groups, tiles = mesh.shape["step"], mesh.shape["tile"]

    def local(start_state, covariates, noise, embedding, w_in, w_first, w_second, w_out):
        cols = start_state.shape[1]
        wide = cols + 2 * HALO
        cells = cols * ROWS
        vmem = pl.BlockSpec(memory_space=pltpu.VMEM)
        hbm = pl.BlockSpec(memory_space=pltpu.HBM)
        dma = pltpu.SemaphoreType.DMA
        w_in = jnp.swapaxes(w_in, 1, 2).reshape(144, 128)

        def body(*refs):
            kernel(groups, tiles, *refs)

        args = [
            pltpu.with_memory_space_constraint(v, pltpu.HBM)
            for v in (start_state, covariates, noise, embedding, w_in, w_first, w_second, w_out)
        ]

        return pl.pallas_call(
            body,
            out_shape=pltpu.VMEM((2, 4, cols, ROWS), F32),
            in_specs=[hbm] * 8,
            out_specs=vmem,
            scratch_shapes=[
                pltpu.VMEM((4, cols, ROWS), F32),
                pltpu.VMEM((12, cols, ROWS), BF),
                pltpu.VMEM((2, 4, cols, ROWS), F32),
                pltpu.VMEM((2, 128), F32),
                pltpu.VMEM((144, 128), BF),
                pltpu.VMEM((4, 128), BF),
                pltpu.VMEM((12, cols, ROWS), F32),
                pltpu.VMEM((4, wide * ROWS), F32),
                pltpu.VMEM((16, wide * ROWS), BF),
                pltpu.VMEM((2, 48, wide * ROWS), BF),
                pltpu.VMEM((128, 144), BF),
                pltpu.VMEM((128, 1152), BF),
                pltpu.VMEM((128, 1152), BF),
                pltpu.VMEM((8, 256), BF),
                pltpu.VMEM((2, 128, ROWS), F32),
                pltpu.VMEM((8, cells), F32),
                pltpu.VMEM((2, 384, (wide - 2) * ROWS), BF),
                pltpu.VMEM((2, 384, (wide - 4) * ROWS), BF),
                pltpu.VMEM((256, cells), BF),
                pltpu.VMEM((8, cells), F32),
                pltpu.VMEM((4, cells), F32),
                pltpu.VMEM((2, 4, cells), F32),
                pltpu.VMEM((groups - 1, 4, wide * ROWS), F32),
                pltpu.VMEM((4, wide * ROWS), F32),
                pltpu.VMEM((groups - 1, 4, cells), F32),
                dma((6,)),
                dma((2, 9)),
                dma((2,)),
                dma((2,)),
                dma((2,)),
                dma((2,)),
                dma((groups - 1,)),
                dma((groups - 1,)),
                dma((groups - 1, 2)),
                dma((groups - 1, 2)),
                dma((2,)),
                dma((2,)),
                dma((groups - 1,)),
                dma((groups - 1,)),
            ],
            compiler_params=pltpu.CompilerParams(
                collective_id=0, has_side_effects=True, vmem_limit_bytes=40 << 20
            ),
        )(*args)

    in_specs = (
        P(None, "tile", None),
        P(None, "tile", None),
        P("step", None, "tile", None),
        P("step", None),
        P(),
        P(),
        P(),
        P(),
    )
    out_specs = P("step", None, "tile", None)
    return jax.shard_map(local, mesh=mesh, in_specs=in_specs, out_specs=out_specs, check_vma=False)
```

time: 122 us -> 21.4 us (0.18)
  the two profiles are of different devices: /device:TPU:152 before, /device:TPU:127 now
where the time goes in v2:
time: 21.4 us; the launch traced here: 21.2 us
  Pallas kernels  20.6 us (96%)
  local copies, waits for them, and re-layouts  0.62 us (3%)
    pallas_call x1, Pallas kernels, local(): pl.pallas_call(body, out_shape=pltpu.VMEM((2, 4, cols, ROWS), F32), in_sp...  20.6 us
    unnamed x1, local copies, waits for them, and re-layouts  0.62 us

profile of v2, /device:TPU:127, one launch (start us, length us, event | category | flops | bytes accessed | tf_op | source)
XLA Modules:
  0.0 21.2 jit_solution(559336718601732953)
XLA Ops:
  0.0 20.6 %shard_map.82 = f32[2,4,8,128]{3,2,1,0:T(8,128)S(1)} custom-call(f32[4,8,128]{2,1,0:T(8,128)} %refs_0_.1, bf16[12,8,128]{2,1,0:T(8,128)(2,1)} %refs_1_.1, f32[2,4,8,128]{3,2,1,0:T(8,128)} %refs_2_.1, f32[2,128]{1,0:T(2,128)} %refs_3_.1, bf16[144,128]{1,0:T(8,128)(2,1)} %bitcast.3, bf16[9,128,128]{2,1,0:T(8,128)(2,1)} %refs_5_.1, ...), custom_call_target="tpu_custom_call" | custom-call | tf_op jit(solution)/shard_map/pallas_call | solution.py:458
  20.6 0.6 %copy.10 = f32[2,4,8,128]{3,2,1,0:T(8,128)} copy(f32[2,4,8,128]{3,2,1,0:T(8,128)S(1)} %shard_map.82) | data formatting | bytes 65536

commit v3 on v0

v3 whole, which is shorter than its diff:
```python
import jax
import jax.numpy as jnp
from jax import lax
from jax.experimental import pallas as pl
from jax.experimental.pallas import tpu as pltpu
from jax.sharding import PartitionSpec as P

STEPS = 8
SWEEPS = 2
HALO = 3
ROWS = 128
BF = jnp.bfloat16
F32 = jnp.float32
MESH = pl.DeviceIdType.MESH


def silu_of_half(h):
    return h * jnp.tanh(h) + h


def kernel(
    groups,
    tiles,
    start_hbm,
    cov_hbm,
    noise_hbm,
    embed_hbm,
    win_hbm,
    wfirst_hbm,
    wsecond_hbm,
    wout_hbm,
    out_ref,
    start_ref,
    cov_ref,
    noise_ref,
    embed_ref,
    win_ref,
    wout_ref,
    covf_ref,
    st_ref,
    xb_ref,
    xs_ref,
    w1_ref,
    w2_ref,
    w3_ref,
    wo_ref,
    eb_ref,
    nz_ref,
    fh_ref,
    sh_ref,
    part_ref,
    part_a,
    part_g,
    rx_ref,
    rxs_ref,
    rxf_ref,
    in_sem,
    w_sem,
    halo_send,
    halo_recv,
    rim_send,
    rim_recv,
    near_send,
    near_recv,
    mid_send,
    mid_recv,
    last_send,
    last_recv,
    chain,
):
    k = lax.axis_index("step")
    t = lax.axis_index("tile")
    cols = start_ref.shape[1]
    wide = cols + 2 * HALO

    even = t % 2 == 0
    fast = jnp.where(even, t + 1, t - 1)
    slow = jnp.where(even, t - 1, t + 1)
    has_slow = (slow >= 0) & (slow < tiles)
    slow_one = has_slow.astype(F32)

    def col(i):
        return jnp.where(even, cols - 1 - i, i)

    def lanes(at, width, unit=ROWS):
        return pl.ds(pl.multiple_of(at * unit, ROWS), width * unit)

    local = [
        pltpu.make_async_copy(src, dst, in_sem.at[n])
        for n, (src, dst) in enumerate(
            (
                (start_hbm, start_ref),
                (cov_hbm, cov_ref),
                (win_hbm, win_ref),
                (embed_hbm, embed_ref),
                (noise_hbm, noise_ref),
                (wout_hbm, wout_ref),
            )
        )
    ]
    get_start, get_cov, get_win, get_embed, get_noise, get_wout = local
    weights = []
    for n, (src, dst) in enumerate(((wfirst_hbm, w2_ref), (wsecond_hbm, w3_ref))):
        weights.append(
            [
                pltpu.make_async_copy(src.at[tap], dst.at[:, pl.ds(tap * 128, 128)], w_sem.at[n, tap])
                for tap in range(9)
            ]
        )
    get_start.start()
    get_cov.start()

    st_ref[...] = jnp.zeros_like(st_ref)
    xb_ref[...] = jnp.zeros_like(xb_ref)
    rx_ref[...] = jnp.zeros_like(rx_ref)
    rxs_ref[...] = jnp.zeros_like(rxs_ref)
    rxf_ref[...] = jnp.zeros_like(rxf_ref)

    barrier = pltpu.get_barrier_semaphore()

    def signal(sem, step, tile):
        pl.semaphore_signal(sem, inc=1, device_id=(step, tile), device_id_type=MESH)

    pl.when(has_slow)(lambda: signal(barrier, k, slow))
    pl.when(k > 0)(lambda: signal(barrier, k - 1, t))
    pl.when(k < groups - 1)(lambda: signal(barrier, k + 1, t))
    signal(barrier, k, fast)

    for c in (get_win, get_embed, *weights[0], *weights[1], get_noise, get_wout):
        c.start()

    get_cov.wait()
    covf_ref[...] = cov_ref[...].astype(F32)
    get_start.wait()
    for c in range(cols):
        at = pl.ds((HALO + c) * ROWS, ROWS)
        state = start_ref[:, c, :]
        st_ref[:, at] = state
        xb_ref[:, at] = jnp.concatenate([state, covf_ref[:, c, :]], axis=0).astype(BF)

    def one(p):
        return p.astype(jnp.int32)

    pl.semaphore_wait(barrier, 1 + one(has_slow) + one(k > 0) + one(k < groups - 1))

    def remote(src, dst, send, recv, step, tile):
        return pltpu.make_async_remote_copy(
            src_ref=src,
            dst_ref=dst,
            send_sem=send,
            recv_sem=recv,
            device_id=(step, tile),
            device_id_type=MESH,
        )

    to_fast = lanes(jnp.where(even, cols - HALO, 0), HALO)
    to_slow = lanes(jnp.where(even, 0, cols - HALO), HALO)
    own_to_fast = lanes(jnp.where(even, cols, HALO), HALO)
    own_to_slow = lanes(jnp.where(even, HALO, cols), HALO)
    at_fast = lanes(jnp.where(even, 0, HALO + cols), HALO)
    at_slow = lanes(jnp.where(even, HALO + cols, 0), HALO)
    early = lanes(jnp.where(even, HALO, 0), cols - HALO)
    own_early = lanes(jnp.where(even, 2 * HALO, HALO), cols - HALO)

    def to_sides(ref, send, recv):
        f = remote(ref.at[:, own_to_fast], ref.at[:, at_fast], send.at[0], recv.at[0], k, fast)
        s = remote(ref.at[:, own_to_slow], ref.at[:, at_slow], send.at[1], recv.at[1], k, slow)
        return f, s

    halo_fast, halo_slow = to_sides(xb_ref, halo_send, halo_recv)
    rim_fast, rim_slow = to_sides(st_ref, rim_send, rim_recv)
    pl.when(has_slow)(halo_slow.start)
    halo_fast.start()
    pl.when(has_slow)(rim_slow.start)
    rim_fast.start()

    def pass_on(n):
        if n < groups - 1:
            pl.when((k > 0) & (k < groups - n))(lambda: signal(chain.at[n], k - 1, t))

    def hear(n):
        pl.when(k < groups - 1 - n)(lambda: pl.semaphore_wait(chain.at[n], 1))

    pass_on(0)

    get_win.wait()
    w1_ref[...] = jnp.transpose(win_ref[...].astype(F32) * 0.5).astype(BF)
    get_embed.wait()
    et = 0.5 * jnp.transpose(jnp.concatenate([embed_ref[...], jnp.zeros((6, 128), F32)], axis=0))
    for s in range(2):
        eb_ref[:, pl.ds(s * ROWS, ROWS)] = jnp.broadcast_to(et[:, s : s + 1], (128, ROWS))

    lane = lax.broadcasted_iota(jnp.int32, (1, ROWS), 1)
    keep_first = (lane > 0).astype(F32).astype(BF)
    keep_last = (lane < ROWS - 1).astype(F32).astype(BF)

    def store_taps(ref, v, slot):
        n = v.shape[0]
        for s in range(2):
            at = pl.ds(pl.multiple_of((2 * slot + s) * ROWS, ROWS), ROWS)
            x = v[:, s * ROWS : (s + 1) * ROWS]
            ref[0:n, at] = pltpu.roll(x, 1, 1) * keep_first
            ref[n : 2 * n, at] = x
            ref[2 * n : 3 * n, at] = pltpu.roll(x, ROWS - 1, 1) * keep_last

    def taps_of(ref, slot):
        return jnp.concatenate([ref[:, lanes(slot + a, 1, 2 * ROWS)] for a in range(3)], axis=0)

    def first(c, may_be_outside):
        pre = jnp.dot(w1_ref[...], taps_of(xs_ref, c + 2), preferred_element_type=F32)
        h = silu_of_half(pre + eb_ref[...])
        if may_be_outside:
            h = h * slow_one
        store_taps(fh_ref, h.astype(BF), c + 2)

    def second(c, may_be_outside):
        h = jnp.dot(w2_ref[...], taps_of(fh_ref, c + 1), preferred_element_type=F32)
        h = silu_of_half(h)
        if may_be_outside:
            h = h * slow_one
        store_taps(sh_ref, h.astype(BF), c + 1)

    def block(c):
        h = silu_of_half(jnp.dot(w3_ref[...], taps_of(sh_ref, c), preferred_element_type=F32))
        h = (h + fh_ref[128:256, lanes(c + 2, 1, 2 * ROWS)].astype(F32)).astype(BF)
        return jnp.concatenate([h[:, :ROWS], h[:, ROWS:]], axis=0)

    def project(sweep, cs, blocks):
        sums = jnp.dot(wo_ref[...], jnp.concatenate(blocks, axis=1), preferred_element_type=F32)
        for n, c in enumerate(cs):
            at = lanes(c, 1)
            v = sums[:, n * ROWS : (n + 1) * ROWS] + nz_ref[:, at]
            if sweep == 0:
                part_a[:, at] = v[0:4]
            else:
                part_ref[:, at] = v
            part_g[sweep, :, at] = v[4:8]

    def inputs_first(c):
        x = xb_ref[:, lanes(c + HALO, 1)]
        store_taps(xs_ref, jnp.concatenate([x, x], axis=1), c + HALO)

    def inputs_next(c):
        at = lanes(c + HALO, 1)
        base = st_ref[:, at]
        for d in range(groups - 1):
            base = base + rx_ref[d, :, at]
        cov = xb_ref[:, at].astype(F32)[4:16]
        v = jnp.concatenate(
            [
                jnp.concatenate([base, base + rxs_ref[:, at]], axis=1),
                jnp.concatenate([cov, cov], axis=1),
            ],
            axis=0,
        )
        store_taps(xs_ref, v.astype(BF), c + HALO)

    inner_x = range(cols)
    inner_1, inner_2, inner_3 = range(1, cols - 1), range(2, cols - 2), range(3, cols - 3)
    fast_x, fast_1, fast_2, fast_3 = (-1, -2, -3), (0, -1, -2), (1, 0, -1), (2, 1, 0)

    def other(group):
        return [cols - 1 - i for i in group]

    slow_x, slow_1, slow_2, slow_3 = other(fast_x), other(fast_1), other(fast_2), other(fast_3)

    def stages(sweep, group_1, group_2, group_3, between=lambda n: None):
        for i in group_1:
            first(col(i), i >= cols)
        between(0)
        for i in group_2:
            second(col(i), i >= cols)
        between(1)
        cs = [col(i) for i in group_3]
        blocks = [block(c) for c in cs]
        between(2)
        project(sweep, cs, blocks)

    for i in inner_x:
        inputs_first(col(i))

    def ready(n):
        if n < 2:
            for c in weights[n]:
                c.wait()
            ref = (w2_ref, w3_ref)[n]
            ref[...] = ref[...] * BF(0.5)
            hear(n)
            pass_on(n + 1)
        else:
            get_wout.wait()
            wo = wout_ref[...] * BF(1.0 / STEPS)
            zero_wo = jnp.zeros_like(wo)
            wo_ref[0:4, 0:128] = wo
            wo_ref[0:4, 128:256] = zero_wo
            wo_ref[4:8, 0:128] = wo
            wo_ref[4:8, 128:256] = wo
            get_noise.wait()
            for c in range(cols):
                at = pl.ds(c * ROWS, ROWS)
                n0 = 0.3 * noise_ref[0, :, c, :]
                nz_ref[0:4, at] = n0
                nz_ref[4:8, at] = n0 + 0.3 * noise_ref[1, :, c, :]

    stages(0, inner_1, inner_2, inner_3, ready)

    halo_fast.wait_recv()
    for i in fast_x:
        inputs_first(col(i))
    stages(0, fast_1, fast_2, fast_3)
    for n in range(2, groups - 1):
        hear(n)
        pass_on(n + 1)

    def mids(d):
        g = part_g.at[0]
        r = rx_ref.at[d - 1]

        def send(n, src, dst, tile):
            return remote(
                g.at[:, src], r.at[:, dst], mid_send.at[d - 1, n], mid_recv.at[d - 1, n], k + d, tile
            )

        return (
            send(0, early, own_early, t),
            send(1, to_fast, at_fast, fast),
            send(2, to_slow, own_to_slow, t),
            send(3, to_slow, at_slow, slow),
        )

    mid = {d: mids(d) for d in range(1, groups)}
    near_fast = remote(
        part_a.at[:, to_fast], rxs_ref.at[:, at_fast], near_send.at[0], near_recv.at[0], k, fast
    )
    near_slow = remote(
        part_a.at[:, to_slow], rxs_ref.at[:, at_slow], near_send.at[1], near_recv.at[1], k, slow
    )
    far = range(groups - 1, 0, -1)

    for d in far:

        @pl.when(k + d < groups)
        def _():
            mid[d][1].start()
            mid[d][0].start()

    near_fast.start()

    pl.when(has_slow)(halo_slow.wait_recv)
    for i in slow_x:
        inputs_first(col(i))
    stages(0, slow_1, slow_2, slow_3)

    for d in far:
        pl.when((k + d < groups) & has_slow)(mid[d][3].start)
    for d in far:
        pl.when(k + d < groups)(mid[d][2].start)
    pl.when(has_slow)(near_slow.start)
    rxs_ref[:, pl.ds(HALO * ROWS, cols * ROWS)] = part_a[...]

    rim_fast.wait_recv()
    near_fast.wait_recv()
    for d in range(1, groups):

        @pl.when(k >= d)
        def _():
            mid[d][0].wait_recv()
            mid[d][1].wait_recv()
            mid[d][2].wait_recv()

    for i in (*inner_x, *fast_x):
        inputs_next(col(i))
    stages(1, (*inner_1, *fast_1), (*inner_2, *fast_2), (*inner_3, *fast_3))

    def lasts(d):
        def send(n, at):
            return remote(
                part_g.at[1, :, at],
                rxf_ref.at[d - 1, :, at],
                last_send.at[d - 1, n],
                last_recv.at[d - 1, n],
                k + d,
                t,
            )

        return send(0, early), send(1, to_slow)

    last = {d: lasts(d) for d in range(1, groups)}
    for d in far:
        pl.when(k + d < groups)(last[d][0].start)

    @pl.when(has_slow)
    def _():
        rim_slow.wait_recv()
        near_slow.wait_recv()

    for d in range(1, groups):
        pl.when((k >= d) & has_slow)(mid[d][3].wait_recv)
    for i in slow_x:
        inputs_next(col(i))
    stages(1, slow_1, slow_2, slow_3)
    for d in far:
        pl.when(k + d < groups)(last[d][1].start)

    halo_fast.wait_send()
    rim_fast.wait_send()
    near_fast.wait_send()

    @pl.when(has_slow)
    def _():
        halo_slow.wait_send()
        rim_slow.wait_send()
        near_slow.wait_send()

    for d in range(1, groups):

        @pl.when(k + d < groups)
        def _():
            mid[d][0].wait_send()
            mid[d][1].wait_send()
            mid[d][2].wait_send()

        pl.when((k + d < groups) & has_slow)(mid[d][3].wait_send)

    for d in range(1, groups):

        @pl.when(k >= d)
        def _():
            last[d][0].wait_recv()
            last[d][1].wait_recv()

    for c in range(cols):
        at = pl.ds(c * ROWS, ROWS)
        base = start_ref[:, c, :]
        for d in range(groups - 1):
            base = base + rxf_ref[d, :, at]
        out_ref[0, :, c, :] = base + part_ref[0:4, at]
        out_ref[1, :, c, :] = base + part_ref[4:8, at]
    for d in range(1, groups):

        @pl.when(k + d < groups)
        def _():
            last[d][0].wait_send()
            last[d][1].wait_send()


def solution(mesh):
    groups, tiles = mesh.shape["step"], mesh.shape["tile"]

    def local(start_state, covariates, noise, embedding, w_in, w_first, w_second, w_out):
        cols = start_state.shape[1]
        wide = cols + 2 * HALO
        cells = cols * ROWS
        hbm = pl.BlockSpec(memory_space=pltpu.HBM)
        dma = pltpu.SemaphoreType.DMA
        w_in = jnp.swapaxes(w_in, 1, 2).reshape(144, 128)

        def body(*refs):
            kernel(groups, tiles, *refs)

        args = [
            pltpu.with_memory_space_constraint(v, pltpu.HBM)
            for v in (start_state, covariates, noise, embedding, w_in, w_first, w_second, w_out)
        ]
        return pl.pallas_call(
            body,
            out_shape=pltpu.VMEM((2, 4, cols, ROWS), F32),
            in_specs=[hbm] * 8,
            out_specs=pl.BlockSpec(memory_space=pltpu.VMEM),
            scratch_shapes=[
                pltpu.VMEM((4, cols, ROWS), F32),
                pltpu.VMEM((12, cols, ROWS), BF),
                pltpu.VMEM((2, 4, cols, ROWS), F32),
                pltpu.VMEM((2, 128), F32),
                pltpu.VMEM((144, 128), BF),
                pltpu.VMEM((4, 128), BF),
                pltpu.VMEM((12, cols, ROWS), F32),
                pltpu.VMEM((4, wide * ROWS), F32),
                pltpu.VMEM((16, wide * ROWS), BF),
                pltpu.VMEM((48, wide * 2 * ROWS), BF),
                pltpu.VMEM((128, 144), BF),
                pltpu.VMEM((128, 1152), BF),
                pltpu.VMEM((128, 1152), BF),
                pltpu.VMEM((8, 256), BF),
                pltpu.VMEM((128, 2 * ROWS), F32),
                pltpu.VMEM((8, cells), F32),
                pltpu.VMEM((384, (wide - 2) * 2 * ROWS), BF),
                pltpu.VMEM((384, (wide - 4) * 2 * ROWS), BF),
                pltpu.VMEM((8, cells), F32),
                pltpu.VMEM((4, cells), F32),
                pltpu.VMEM((2, 4, cells), F32),
                pltpu.VMEM((groups - 1, 4, wide * ROWS), F32),
                pltpu.VMEM((4, wide * ROWS), F32),
                pltpu.VMEM((groups - 1, 4, cells), F32),
                dma((6,)),
                dma((2, 9)),
                dma((2,)),
                dma((2,)),
                dma((2,)),
                dma((2,)),
                dma((2,)),
                dma((2,)),
                dma((groups - 1, 4)),
                dma((groups - 1, 4)),
                dma((groups - 1, 2)),
                dma((groups - 1, 2)),
                pltpu.SemaphoreType.REGULAR((groups - 1,)),
            ],
            compiler_params=pltpu.CompilerParams(
                collective_id=0, has_side_effects=True, vmem_limit_bytes=40 << 20
            ),
        )(*args)

    in_specs = (
        P(None, "tile", None),
        P(None, "tile", None),
        P("step", None, "tile", None),
        P("step", None),
        P(),
        P(),
        P(),
        P(),
    )
    out_specs = P("step", None, "tile", None)
    return jax.shard_map(local, mesh=mesh, in_specs=in_specs, out_specs=out_specs, check_vma=False)
```

time: 122 us -> 20.8 us (0.17)
  the two profiles are of different devices: /device:TPU:152 before, /device:TPU:216 now
where the time goes in v3:
time: 20.8 us; the launch traced here: 20.7 us
  Pallas kernels  20 us (96%)
  local copies, waits for them, and re-layouts  0.62 us (3%)
    pallas_call x1, Pallas kernels, local(): pl.pallas_call(body, out_shape=pltpu.VMEM((2, 4, cols, ROWS), F32), in_sp...  20 us
    unnamed x1, local copies, waits for them, and re-layouts  0.62 us

profile of v3, /device:TPU:216, one launch (start us, length us, event | category | flops | bytes accessed | tf_op | source)
XLA Modules:
  0.0 20.7 jit_solution(15754969237624575605)
XLA Ops:
  0.0 20.0 %shard_map.82 = f32[2,4,8,128]{3,2,1,0:T(8,128)S(1)} custom-call(f32[4,8,128]{2,1,0:T(8,128)} %refs_0_.1, bf16[12,8,128]{2,1,0:T(8,128)(2,1)} %refs_1_.1, f32[2,4,8,128]{3,2,1,0:T(8,128)} %refs_2_.1, f32[2,128]{1,0:T(2,128)} %refs_3_.1, bf16[144,128]{1,0:T(8,128)(2,1)} %bitcast.3, bf16[9,128,128]{2,1,0:T(8,128)(2,1)} %refs_5_.1, ...), custom_call_target="tpu_custom_call" | custom-call | tf_op jit(solution)/shard_map/pallas_call | solution.py:465
  20.1 0.6 %copy.10 = f32[2,4,8,128]{3,2,1,0:T(8,128)} copy(f32[2,4,8,128]{3,2,1,0:T(8,128)S(1)} %shard_map.82) | data formatting | bytes 65536

commit v4 on v3

v4 whole, which is shorter than its diff:
```python
import jax
import jax.numpy as jnp
from jax import lax
from jax.experimental import pallas as pl
from jax.experimental.pallas import tpu as pltpu
from jax.sharding import PartitionSpec as P

STEPS = 8
SWEEPS = 2
CH = 4
HALO = 3
ROWS = 128
BF = jnp.bfloat16
F32 = jnp.float32
MESH = pl.DeviceIdType.MESH


def silu_of_half(h):
    return h * jnp.tanh(h) + h


def kernel(
    groups,
    tiles,
    start_hbm,
    cov_hbm,
    noise_hbm,
    embed_hbm,
    win_hbm,
    wfirst_hbm,
    wsecond_hbm,
    wout_hbm,
    out_ref,
    start_ref,
    cov_ref,
    noise_ref,
    embed_ref,
    win_ref,
    wout_ref,
    covf_ref,
    st_ref,
    base_ref,
    xb_ref,
    x1_ref,
    x2_ref,
    w1_ref,
    w2_ref,
    w3_ref,
    wo_ref,
    eb_ref,
    nz_ref,
    fh_ref,
    sh_ref,
    bo_ref,
    pa_ref,
    pg_ref,
    pd_ref,
    rx_ref,
    rxs_ref,
    rxf_ref,
    in_sem,
    w_sem,
    halo_send,
    halo_recv,
    rim_send,
    rim_recv,
    near_send,
    near_recv,
    mid_send,
    mid_recv,
    last_send,
    last_recv,
    chain,
):
    k = lax.axis_index("step")
    t = lax.axis_index("tile")
    cols = start_ref.shape[1]
    half = cols // 2
    rim = CH * half
    has_left = t > 0
    has_right = t < tiles - 1

    local = [
        pltpu.make_async_copy(src, dst, in_sem.at[n])
        for n, (src, dst) in enumerate(
            (
                (start_hbm, start_ref),
                (cov_hbm, cov_ref),
                (win_hbm, win_ref),
                (embed_hbm, embed_ref),
                (noise_hbm, noise_ref),
                (wout_hbm, wout_ref),
            )
        )
    ]
    get_start, get_cov, get_win, get_embed, get_noise, get_wout = local
    weights = []
    for n, (src, dst) in enumerate(((wfirst_hbm, w2_ref), (wsecond_hbm, w3_ref))):
        weights.append(
            [
                pltpu.make_async_copy(src.at[tap], dst.at[:, pl.ds(tap * 128, 128)], w_sem.at[n, tap])
                for tap in range(9)
            ]
        )
    get_start.start()
    get_cov.start()

    for ref in (st_ref, xb_ref, rx_ref, rxs_ref, rxf_ref):
        ref[...] = jnp.zeros_like(ref)

    barrier = pltpu.get_barrier_semaphore()

    def signal(sem, step, tile):
        pl.semaphore_signal(sem, inc=1, device_id=(step, tile), device_id_type=MESH)

    pl.when(has_left)(lambda: signal(barrier, k, t - 1))
    pl.when(has_right)(lambda: signal(barrier, k, t + 1))
    pl.when(k > 0)(lambda: signal(barrier, k - 1, t))
    pl.when(k < groups - 1)(lambda: signal(barrier, k + 1, t))

    for c in (get_win, get_embed, *weights[0], *weights[1], get_noise, get_wout):
        c.start()

    def slot(c):
        return pl.ds((c + HALO) * ROWS, ROWS)

    get_cov.wait()
    covf_ref[...] = cov_ref[...].astype(F32)
    get_start.wait()
    for c in range(cols):
        xb_ref[:, slot(c)] = jnp.concatenate([start_ref[:, c, :], covf_ref[:, c, :]], axis=0).astype(BF)

    def one(p):
        return p.astype(jnp.int32)

    pl.semaphore_wait(barrier, one(has_left) + one(has_right) + one(k > 0) + one(k < groups - 1))

    def remote(src, dst, send, recv, step, tile):
        return pltpu.make_async_remote_copy(
            src_ref=src,
            dst_ref=dst,
            send_sem=send,
            recv_sem=recv,
            device_id=(step, tile),
            device_id_type=MESH,
        )

    def strip(c):
        return pl.ds((c + HALO) * ROWS, HALO * ROWS)

    halo_left = remote(
        xb_ref.at[:, strip(0)], xb_ref.at[:, strip(cols)], halo_send.at[0], halo_recv.at[0], k, t - 1
    )
    halo_right = remote(
        xb_ref.at[:, strip(cols - HALO)], xb_ref.at[:, strip(-HALO)], halo_send.at[1], halo_recv.at[1], k, t + 1
    )
    pl.when(has_left)(halo_left.start)
    pl.when(has_right)(halo_right.start)

    at_left, own_left, own_right, at_right = [pl.ds(n * rim, rim) for n in range(4)]
    first_half, second_half = pl.ds(0, rim), pl.ds(rim, rim)
    own = pl.ds(rim, 2 * rim)

    for ch in range(CH):
        st_ref[pl.ds(rim + ch, cols, stride=CH), :] = start_ref[ch]
    rim_left = remote(st_ref.at[own_left], st_ref.at[at_right], rim_send.at[0], rim_recv.at[0], k, t - 1)
    rim_right = remote(st_ref.at[own_right], st_ref.at[at_left], rim_send.at[1], rim_recv.at[1], k, t + 1)
    pl.when(has_left)(rim_left.start)
    pl.when(has_right)(rim_right.start)

    def pass_on(n):
        if n < groups - 1:
            pl.when((k > 0) & (k < groups - n))(lambda: signal(chain.at[n], k - 1, t))

    def hear(n):
        pl.when(k < groups - 1 - n)(lambda: pl.semaphore_wait(chain.at[n], 1))

    pass_on(0)

    get_win.wait()
    w1_ref[...] = jnp.transpose(win_ref[...].astype(F32) * 0.5).astype(BF)
    get_embed.wait()
    et = 0.5 * jnp.transpose(jnp.concatenate([embed_ref[...], jnp.zeros((6, 128), F32)], axis=0))
    for s in range(2):
        eb_ref[:, pl.ds(s * ROWS, ROWS)] = jnp.broadcast_to(et[:, s : s + 1], (128, ROWS))

    lane = lax.broadcasted_iota(jnp.int32, (1, ROWS), 1)
    keep_first = (lane > 0).astype(F32).astype(BF)
    keep_last = (lane < ROWS - 1).astype(F32).astype(BF)
    left_one = has_left.astype(F32)
    right_one = has_right.astype(F32)

    def store_taps(ref, x, at):
        n = x.shape[0]
        at = pl.ds(at * ROWS, ROWS)
        ref[0:n, at] = pltpu.roll(x, 1, 1) * keep_first
        ref[n : 2 * n, at] = x
        ref[2 * n : 3 * n, at] = pltpu.roll(x, ROWS - 1, 1) * keep_last

    def store_both(ref, h, at):
        for s in range(2):
            store_taps(ref, h[:, s * ROWS : (s + 1) * ROWS], 2 * at + s)

    def taps_of(ref, at):
        return jnp.concatenate(
            [ref[:, pl.ds((at + a) * 2 * ROWS, 2 * ROWS)] for a in range(3)], axis=0
        )

    def inside(h, c):
        if c < 0:
            return h * left_one
        if c >= cols:
            return h * right_one
        return h

    def first_done(pre, c):
        h = inside(silu_of_half(pre + eb_ref[...]), c)
        store_both(fh_ref, h.astype(BF), c + 2)

    def first(c):
        first_done(jnp.dot(w1_ref[...], taps_of(x2_ref, c + 2), preferred_element_type=F32), c)

    def first_pair(pair):
        taps = jnp.concatenate(
            [
                jnp.concatenate([x1_ref[:, pl.ds((c + 2 + a) * ROWS, ROWS)] for c in pair], axis=1)
                for a in range(3)
            ],
            axis=0,
        )
        pre = jnp.dot(w1_ref[...], taps, preferred_element_type=F32)
        for n, c in enumerate(pair):
            p = pre[:, n * ROWS : (n + 1) * ROWS]
            first_done(jnp.concatenate([p, p], axis=1), c)

    def second(c):
        h = jnp.dot(w2_ref[...], taps_of(fh_ref, c + 1), preferred_element_type=F32)
        store_both(sh_ref, inside(silu_of_half(h), c).astype(BF), c + 1)

    def block(c):
        h = silu_of_half(jnp.dot(w3_ref[...], taps_of(sh_ref, c), preferred_element_type=F32))
        h = (h + fh_ref[128:256, pl.ds((c + 2) * 2 * ROWS, 2 * ROWS)].astype(F32)).astype(BF)
        for s in range(2):
            at = (s * half + c % half) * 128
            bo_ref[at : at + 128, pl.ds((c // half) * ROWS, ROWS)] = h[:, s * ROWS : (s + 1) * ROWS]

    def project():
        p = jnp.dot(wo_ref[...], bo_ref[...], preferred_element_type=F32)
        p = jnp.concatenate([p[:, :ROWS], p[:, ROWS:]], axis=0)
        a = jnp.concatenate([p[0:rim], p[2 * rim : 3 * rim]], axis=0) + nz_ref[0]
        g = jnp.concatenate([p[rim : 2 * rim], p[3 * rim : 4 * rim]], axis=0) + nz_ref[1]
        return a, g

    def inputs_first(c):
        store_taps(x1_ref, xb_ref[:, slot(c)], c + HALO)

    for c in range(cols):
        inputs_first(c)
    for c in range(1, cols - 1, 2):
        first_pair((c, c + 1))
    hear(0)
    pass_on(1)
    for c in weights[0]:
        c.wait()
    w2_ref[...] = w2_ref[...] * BF(0.5)
    for c in range(2, cols - 2):
        second(c)
    hear(1)
    pass_on(2)
    for c in weights[1]:
        c.wait()
    w3_ref[...] = w3_ref[...] * BF(0.5)
    for c in range(3, cols - 3):
        block(c)
    get_wout.wait()
    wo = wout_ref[...].astype(F32) * (1.0 / STEPS)
    none = jnp.zeros((CH, 128), F32)
    lhs = []
    for sums in range(2):
        for j in range(half):
            parts = [wo if s <= sums and i == j else none for s in range(2) for i in range(half)]
            lhs.append(jnp.concatenate(parts, axis=1))
    wo_ref[...] = jnp.concatenate(lhs, axis=0).astype(BF)
    get_noise.wait()
    for ch in range(CH):
        at = pl.ds(ch, cols, stride=CH)
        n0 = 0.3 * noise_ref[0, ch]
        nz_ref[0, at, :] = n0
        nz_ref[1, at, :] = n0 + 0.3 * noise_ref[1, ch]
    for n in range(2, groups - 1):
        hear(n)
        pass_on(n + 1)

    pl.when(has_left)(halo_right.wait_recv)
    pl.when(has_right)(halo_left.wait_recv)
    for c in (-1, cols, -2, cols + 1, -3, cols + 2):
        inputs_first(c)
    for c in (0, -1, -2):
        first_pair((c, cols - 1 - c))
    for c in (1, 0, -1):
        second(c)
        second(cols - 1 - c)
    for c in (2, 1, 0):
        block(c)
        block(cols - 1 - c)
    a, g = project()
    pg_ref[...] = g.astype(BF)
    pa_ref[...] = a.astype(BF)

    def mids(d):
        def send(n, src, dst, tile):
            return remote(
                pg_ref.at[src],
                rx_ref.at[d - 1, dst],
                mid_send.at[d - 1, n],
                mid_recv.at[d - 1, n],
                k + d,
                tile,
            )

        return (
            send(0, first_half, at_right, t - 1),
            send(1, second_half, at_left, t + 1),
            send(2, pl.ds(0, 2 * rim), own, t),
        )

    mid = {d: mids(d) for d in range(1, groups)}
    near_left = remote(
        pa_ref.at[first_half], rxs_ref.at[at_right], near_send.at[0], near_recv.at[0], k, t - 1
    )
    near_right = remote(
        pa_ref.at[second_half], rxs_ref.at[at_left], near_send.at[1], near_recv.at[1], k, t + 1
    )
    far = sorted(range(1, groups), key=lambda d: -min(d, groups - d))
    for d in far:
        pl.when((k + d < groups) & has_left)(mid[d][0].start)
        pl.when((k + d < groups) & has_right)(mid[d][1].start)
    for d in far:
        pl.when(k + d < groups)(mid[d][2].start)
    pl.when(has_left)(near_left.start)
    pl.when(has_right)(near_right.start)

    @pl.when(has_left)
    def _():
        rim_right.wait_recv()
        near_right.wait_recv()

    @pl.when(has_right)
    def _():
        rim_left.wait_recv()
        near_left.wait_recv()

    for d in range(1, groups):
        pl.when(k >= d)(mid[d][2].wait_recv)
        pl.when((k >= d) & has_left)(mid[d][1].wait_recv)
        pl.when((k >= d) & has_right)(mid[d][0].wait_recv)

    base = st_ref[...]
    for d in range(groups - 1):
        base = base + rx_ref[d].astype(F32)
    base_ref[...] = base[rim : 3 * rim]
    step = jnp.concatenate(
        [rxs_ref[at_left].astype(F32), a, rxs_ref[at_right].astype(F32)], axis=0
    )
    states = (base, base + step)
    for c in range(-HALO, cols + HALO):
        at = CH * (c + half)
        cov = xb_ref[:, slot(c)].astype(F32)[CH:]
        for s in range(2):
            v = jnp.concatenate([states[s][at : at + CH], cov], axis=0)
            store_taps(x2_ref, v.astype(BF), 2 * (c + HALO) + s)
    for c in range(-2, cols + 2):
        first(c)
    for c in range(-1, cols + 1):
        second(c)
    for c in range(cols):
        block(c)
    a, g = project()
    pd_ref[...] = (g - pg_ref[...].astype(F32)).astype(BF)
    last = {
        d: remote(pd_ref, rxf_ref.at[d - 1], last_send.at[d - 1], last_recv.at[d - 1], k + d, t)
        for d in range(1, groups)
    }
    for d in far:
        pl.when(k + d < groups)(last[d].start)

    @pl.when(has_left)
    def _():
        halo_left.wait_send()
        rim_left.wait_send()
        near_left.wait_send()

    @pl.when(has_right)
    def _():
        halo_right.wait_send()
        rim_right.wait_send()
        near_right.wait_send()

    for d in range(1, groups):
        pl.when(k + d < groups)(mid[d][2].wait_send)
        pl.when((k + d < groups) & has_left)(mid[d][0].wait_send)
        pl.when((k + d < groups) & has_right)(mid[d][1].wait_send)

    for d in range(1, groups):
        pl.when(k >= d)(last[d].wait_recv)
    base = base_ref[...]
    for d in range(groups - 1):
        base = base + rxf_ref[d].astype(F32)
    for s, v in enumerate((a, g)):
        base_ref[...] = base + v
        for ch in range(CH):
            out_ref[s, ch] = base_ref[pl.ds(ch, cols, stride=CH), :]
    for d in range(1, groups):
        pl.when(k + d < groups)(last[d].wait_send)


def solution(mesh):
    groups, tiles = mesh.shape["step"], mesh.shape["tile"]

    def local(start_state, covariates, noise, embedding, w_in, w_first, w_second, w_out):
        cols = start_state.shape[1]
        wide = cols + 2 * HALO
        hbm = pl.BlockSpec(memory_space=pltpu.HBM)
        dma = pltpu.SemaphoreType.DMA
        w_in = jnp.swapaxes(w_in, 1, 2).reshape(144, 128)

        def body(*refs):
            kernel(groups, tiles, *refs)

        args = [
            pltpu.with_memory_space_constraint(v, pltpu.HBM)
            for v in (start_state, covariates, noise, embedding, w_in, w_first, w_second, w_out)
        ]
        return pl.pallas_call(
            body,
            out_shape=pltpu.VMEM((2, 4, cols, ROWS), F32),
            in_specs=[hbm] * 8,
            out_specs=pl.BlockSpec(memory_space=pltpu.VMEM),
            scratch_shapes=[
                pltpu.VMEM((CH, cols, ROWS), F32),
                pltpu.VMEM((12, cols, ROWS), BF),
                pltpu.VMEM((2, CH, cols, ROWS), F32),
                pltpu.VMEM((2, 128), F32),
                pltpu.VMEM((144, 128), BF),
                pltpu.VMEM((CH, 128), BF),
                pltpu.VMEM((12, cols, ROWS), F32),
                pltpu.VMEM((2 * CH * cols, ROWS), F32),
                pltpu.VMEM((CH * cols, ROWS), F32),
                pltpu.VMEM((16, wide * ROWS), BF),
                pltpu.VMEM((48, wide * ROWS), BF),
                pltpu.VMEM((48, wide * 2 * ROWS), BF),
                pltpu.VMEM((128, 144), BF),
                pltpu.VMEM((128, 1152), BF),
                pltpu.VMEM((128, 1152), BF),
                pltpu.VMEM((CH * cols, 128 * cols), BF),
                pltpu.VMEM((128, 2 * ROWS), F32),
                pltpu.VMEM((2, CH * cols, ROWS), F32),
                pltpu.VMEM((384, (wide - 2) * 2 * ROWS), BF),
                pltpu.VMEM((384, (wide - 4) * 2 * ROWS), BF),
                pltpu.VMEM((128 * cols, 2 * ROWS), BF),
                pltpu.VMEM((CH * cols, ROWS), BF),
                pltpu.VMEM((CH * cols, ROWS), BF),
                pltpu.VMEM((CH * cols, ROWS), BF),
                pltpu.VMEM((groups - 1, 2 * CH * cols, ROWS), BF),
                pltpu.VMEM((2 * CH * cols, ROWS), BF),
                pltpu.VMEM((groups - 1, CH * cols, ROWS), BF),
                dma((6,)),
                dma((2, 9)),
                dma((2,)),
                dma((2,)),
                dma((2,)),
                dma((2,)),
                dma((2,)),
                dma((2,)),
                dma((groups - 1, 3)),
                dma((groups - 1, 3)),
                dma((groups - 1,)),
                dma((groups - 1,)),
                pltpu.SemaphoreType.REGULAR((groups - 1,)),
            ],
            compiler_params=pltpu.CompilerParams(
                collective_id=0, has_side_effects=True, vmem_limit_bytes=40 << 20
            ),
        )(*args)

    in_specs = (
        P(None, "tile", None),
        P(None, "tile", None),
        P("step", None, "tile", None),
        P("step", None),
        P(),
        P(),
        P(),
        P(),
    )
    out_specs = P("step", None, "tile", None)
    return jax.shard_map(local, mesh=mesh, in_specs=in_specs, out_specs=out_specs, check_vma=False)
```

time: 20.8 us -> 19.1 us (0.918)
  the two profiles are of different devices: /device:TPU:216 before, /device:TPU:127 now
where the time goes in v4:
time: 19.1 us; the launch traced here: 19 us
  Pallas kernels  18.3 us (96%)
  local copies, waits for them, and re-layouts  0.62 us (3%)
    pallas_call x1, Pallas kernels, local(): pl.pallas_call(body, out_shape=pltpu.VMEM((2, 4, cols, ROWS), F32), in_sp...  18.3 us
    unnamed x1, local copies, waits for them, and re-layouts  0.62 us

profile of v4, /device:TPU:127, one launch (start us, length us, event | category | flops | bytes accessed | tf_op | source)
XLA Modules:
  0.0 19.0 jit_solution(15670984742673707093)
XLA Ops:
  0.0 18.3 %shard_map.82 = f32[2,4,8,128]{3,2,1,0:T(8,128)S(1)} custom-call(f32[4,8,128]{2,1,0:T(8,128)} %refs_0_.1, bf16[12,8,128]{2,1,0:T(8,128)(2,1)} %refs_1_.1, f32[2,4,8,128]{3,2,1,0:T(8,128)} %refs_2_.1, f32[2,128]{1,0:T(2,128)} %refs_3_.1, bf16[144,128]{1,0:T(8,128)(2,1)} %bitcast.3, bf16[9,128,128]{2,1,0:T(8,128)(2,1)} %refs_5_.1, ...), custom_call_target="tpu_custom_call" | custom-call | tf_op jit(solution)/shard_map/pallas_call | solution.py:434
  18.3 0.6 %copy.10 = f32[2,4,8,128]{3,2,1,0:T(8,128)} copy(f32[2,4,8,128]{3,2,1,0:T(8,128)S(1)} %shard_map.82) | data formatting | bytes 65536

commit v5 on v4

v5 whole, which is shorter than its diff:
```python
import jax
import jax.numpy as jnp
from jax import lax
from jax.experimental import pallas as pl
from jax.experimental.pallas import tpu as pltpu
from jax.sharding import PartitionSpec as P

STEPS = 8
SWEEPS = 2
CH = 4
HALO = 3
ROWS = 128
BF = jnp.bfloat16
F32 = jnp.float32
MESH = pl.DeviceIdType.MESH


def silu_of_half(h):
    return h * jnp.tanh(h) + h


def kernel(
    groups,
    tiles,
    start_hbm,
    cov_hbm,
    noise_hbm,
    embed_hbm,
    win_hbm,
    wfirst_hbm,
    wsecond_hbm,
    wout_hbm,
    out_ref,
    start_ref,
    cov_ref,
    noise_ref,
    embed_ref,
    win_ref,
    wout_ref,
    covf_ref,
    st_ref,
    base_ref,
    xb_ref,
    x1_ref,
    x2_ref,
    w1_ref,
    w2_ref,
    w3_ref,
    wo_ref,
    eb_ref,
    nz_ref,
    fh_ref,
    sh_ref,
    bo_ref,
    pa_ref,
    pg_ref,
    pd_ref,
    rx_ref,
    rxs_ref,
    rxf_ref,
    in_sem,
    win_sem,
    w_sem,
    halo_send,
    halo_recv,
    rim_send,
    rim_recv,
    near_send,
    near_recv,
    mid_send,
    mid_recv,
    last_send,
    last_recv,
    chain,
):
    k = lax.axis_index("step")
    t = lax.axis_index("tile")
    cols = start_ref.shape[1]
    half = cols // 2
    rim = CH * half

    even = t % 2 == 0
    fast = jnp.where(even, t + 1, t - 1)
    slow = jnp.where(even, t - 1, t + 1)
    has_slow = (slow >= 0) & (slow < tiles)

    def turned(n, count):
        return jnp.where(even, count - 1 - n, n)

    def either_way(f):
        @pl.when(even)
        def _():
            for c in range(cols):
                f(c, cols - 1 - c)

        @pl.when(jnp.logical_not(even))
        def _():
            for c in range(cols):
                f(c, c)

    get_start, get_cov, get_embed, get_noise, get_wout = [
        pltpu.make_async_copy(src, dst, in_sem.at[n])
        for n, (src, dst) in enumerate(
            (
                (start_hbm, start_ref),
                (cov_hbm, cov_ref),
                (embed_hbm, embed_ref),
                (noise_hbm, noise_ref),
                (wout_hbm, wout_ref),
            )
        )
    ]
    get_win = [
        pltpu.make_async_copy(
            win_hbm.at[pl.ds(a * 48, 48)],
            win_ref.at[pl.ds(pl.multiple_of(turned(a, 3) * 48, 48), 48)],
            win_sem.at[a],
        )
        for a in range(3)
    ]
    weights = []
    for n, (src, dst) in enumerate(((wfirst_hbm, w2_ref), (wsecond_hbm, w3_ref))):
        weights.append(
            [
                pltpu.make_async_copy(
                    src.at[3 * a + b],
                    dst.at[:, pl.ds(pl.multiple_of((3 * turned(a, 3) + b) * 128, 128), 128)],
                    w_sem.at[n, 3 * a + b],
                )
                for a in range(3)
                for b in range(3)
            ]
        )
    get_start.start()
    get_cov.start()

    for ref in (st_ref, xb_ref, rx_ref, rxs_ref, rxf_ref):
        ref[...] = jnp.zeros_like(ref)

    barrier = pltpu.get_barrier_semaphore()

    def signal(sem, step, tile):
        pl.semaphore_signal(sem, inc=1, device_id=(step, tile), device_id_type=MESH)

    pl.when(has_slow)(lambda: signal(barrier, k, slow))
    pl.when(k > 0)(lambda: signal(barrier, k - 1, t))
    pl.when(k < groups - 1)(lambda: signal(barrier, k + 1, t))
    signal(barrier, k, fast)

    for c in (*get_win, get_embed, *weights[0], *weights[1], get_noise, get_wout):
        c.start()

    def lanes(n, width=1):
        return pl.ds(n * ROWS, width * ROWS)

    def place(i):
        if i < 0:
            return -1 - i
        if i >= cols:
            return HALO + cols + HALO - 1 - (i - cols)
        return HALO + i

    def row_of(i):
        if i < 0:
            return CH * (-1 - i)
        if i >= cols:
            return 3 * rim + CH * (half - 1 - (i - cols))
        return rim + CH * i

    get_cov.wait()
    covf_ref[...] = cov_ref[...].astype(F32)
    get_start.wait()

    def put_inputs(c, i):
        x = jnp.concatenate([start_ref[:, c, :], covf_ref[:, c, :]], axis=0)
        xb_ref[:, lanes(place(i))] = x.astype(BF)

    either_way(put_inputs)

    def one(p):
        return p.astype(jnp.int32)

    pl.semaphore_wait(barrier, 1 + one(has_slow) + one(k > 0) + one(k < groups - 1))

    def remote(src, dst, send, recv, step, tile):
        return pltpu.make_async_remote_copy(
            src_ref=src,
            dst_ref=dst,
            send_sem=send,
            recv_sem=recv,
            device_id=(step, tile),
            device_id_type=MESH,
        )

    def to_sides(ref, parts, send, recv):
        at_fast, own_fast, own_slow, at_slow = parts
        return (
            remote(ref.at[own_fast], ref.at[at_fast], send.at[0], recv.at[0], k, fast),
            remote(ref.at[own_slow], ref.at[at_slow], send.at[1], recv.at[1], k, slow),
        )

    strips = [(slice(None), lanes(n, HALO)) for n in (0, HALO, cols, cols + HALO)]
    halo_fast, halo_slow = to_sides(xb_ref, strips, halo_send, halo_recv)
    pl.when(has_slow)(halo_slow.start)
    halo_fast.start()

    at_fast, own_fast, own_slow, at_slow = quarters = [pl.ds(n * rim, rim) for n in range(4)]
    halves = (pl.ds(0, rim), pl.ds(rim, rim))

    def put_state(c, i):
        st_ref[row_of(i) : row_of(i) + CH, :] = start_ref[:, c, :]

    either_way(put_state)
    rim_fast, rim_slow = to_sides(st_ref, quarters, rim_send, rim_recv)
    pl.when(has_slow)(rim_slow.start)
    rim_fast.start()

    def pass_on(n):
        if n < groups - 1:
            pl.when((k > 0) & (k < groups - n))(lambda: signal(chain.at[n], k - 1, t))

    def hear(n):
        pl.when(k < groups - 1 - n)(lambda: pl.semaphore_wait(chain.at[n], 1))

    pass_on(0)

    for c in get_win:
        c.wait()
    w1_ref[...] = jnp.transpose(win_ref[...].astype(F32) * 0.5).astype(BF)
    get_embed.wait()
    et = 0.5 * jnp.transpose(jnp.concatenate([embed_ref[...], jnp.zeros((6, 128), F32)], axis=0))
    for s in range(2):
        eb_ref[:, pl.ds(s * ROWS, ROWS)] = jnp.broadcast_to(et[:, s : s + 1], (128, ROWS))

    lane = lax.broadcasted_iota(jnp.int32, (1, ROWS), 1)
    keep_first = (lane > 0).astype(F32).astype(BF)
    keep_last = (lane < ROWS - 1).astype(F32).astype(BF)
    slow_one = has_slow.astype(F32)

    def store_taps(ref, x, at):
        n = x.shape[0]
        at = pl.ds(at * ROWS, ROWS)
        ref[0:n, at] = pltpu.roll(x, 1, 1) * keep_first
        ref[n : 2 * n, at] = x
        ref[2 * n : 3 * n, at] = pltpu.roll(x, ROWS - 1, 1) * keep_last

    def store_both(ref, h, at):
        for s in range(2):
            store_taps(ref, h[:, s * ROWS : (s + 1) * ROWS], 2 * at + s)

    def taps_of(ref, at):
        return jnp.concatenate(
            [ref[:, pl.ds((at + a) * 2 * ROWS, 2 * ROWS)] for a in range(3)], axis=0
        )

    def inside(h, c):
        return h * slow_one if c >= cols else h

    def first_done(pre, c):
        h = inside(silu_of_half(pre + eb_ref[...]), c)
        store_both(fh_ref, h.astype(BF), c + 2)

    def first(c):
        first_done(jnp.dot(w1_ref[...], taps_of(x2_ref, c + 2), preferred_element_type=F32), c)

    def first_pair(pair):
        taps = jnp.concatenate(
            [
                jnp.concatenate([x1_ref[:, lanes(c + 2 + a)] for c in pair], axis=1)
                for a in range(3)
            ],
            axis=0,
        )
        pre = jnp.dot(w1_ref[...], taps, preferred_element_type=F32)
        for n, c in enumerate(pair):
            p = pre[:, n * ROWS : (n + 1) * ROWS]
            first_done(jnp.concatenate([p, p], axis=1), c)

    def second(c):
        h = jnp.dot(w2_ref[...], taps_of(fh_ref, c + 1), preferred_element_type=F32)
        store_both(sh_ref, inside(silu_of_half(h), c).astype(BF), c + 1)

    def block(c):
        h = silu_of_half(jnp.dot(w3_ref[...], taps_of(sh_ref, c), preferred_element_type=F32))
        h = (h + fh_ref[128:256, pl.ds((c + 2) * 2 * ROWS, 2 * ROWS)].astype(F32)).astype(BF)
        for s in range(2):
            at = (s * half + c % half) * 128
            bo_ref[at : at + 128, pl.ds((c // half) * ROWS, ROWS)] = h[:, s * ROWS : (s + 1) * ROWS]

    def project(h):
        p = jnp.dot(wo_ref[...], bo_ref[:, lanes(h)], preferred_element_type=F32)
        return p[:rim] + nz_ref[0, halves[h], :], p[rim:] + nz_ref[1, halves[h], :]

    def inputs_first(c):
        store_taps(x1_ref, xb_ref[:, lanes(place(c))], c + HALO)

    for c in range(cols):
        inputs_first(c)
    for c in range(1, cols - 1, 2):
        first_pair((c, c + 1))
    hear(0)
    pass_on(1)
    for c in weights[0]:
        c.wait()
    w2_ref[...] = w2_ref[...] * BF(0.5)
    for c in range(2, cols - 2):
        second(c)
    hear(1)
    pass_on(2)
    for c in weights[1]:
        c.wait()
    w3_ref[...] = w3_ref[...] * BF(0.5)
    for c in range(3, cols - 3):
        block(c)
    get_wout.wait()
    wo = wout_ref[...].astype(F32) * (1.0 / STEPS)
    none = jnp.zeros((CH, 128), F32)
    lhs = []
    for sums in range(2):
        for j in range(half):
            parts = [wo if s <= sums and i == j else none for s in range(2) for i in range(half)]
            lhs.append(jnp.concatenate(parts, axis=1))
    wo_ref[...] = jnp.concatenate(lhs, axis=0).astype(BF)
    get_noise.wait()

    def put_noise(c, i):
        n0 = 0.3 * noise_ref[0, :, c, :]
        nz_ref[0, CH * i : CH * (i + 1), :] = n0
        nz_ref[1, CH * i : CH * (i + 1), :] = n0 + 0.3 * noise_ref[1, :, c, :]

    either_way(put_noise)

    halo_fast.wait_recv()
    for c in (-1, -2, -3):
        inputs_first(c)
    first_pair((0, -1))
    first_pair((-2,))
    for c in (1, 0, -1):
        second(c)
    for c in (2, 1, 0):
        block(c)
    for n in range(2, groups - 1):
        hear(n)
        pass_on(n + 1)

    def mids(d):
        def send(n, src, dst, tile):
            return remote(
                pg_ref.at[src],
                rx_ref.at[d - 1, dst],
                mid_send.at[d - 1, n],
                mid_recv.at[d - 1, n],
                k + d,
                tile,
            )

        return (
            send(0, halves[0], at_fast, fast),
            send(1, halves[0], own_fast, t),
            send(2, halves[1], at_slow, slow),
            send(3, halves[1], own_slow, t),
        )

    mid = {d: mids(d) for d in range(1, groups)}
    near_fast = remote(
        pa_ref.at[halves[0]], rxs_ref.at[at_fast], near_send.at[0], near_recv.at[0], k, fast
    )
    near_slow = remote(
        pa_ref.at[halves[1]], rxs_ref.at[at_slow], near_send.at[1], near_recv.at[1], k, slow
    )
    far = sorted(range(1, groups), key=lambda d: -min(d, groups - d))

    def put_sums(h):
        a, g = project(h)
        pg_ref[halves[h], :] = g.astype(BF)
        pa_ref[halves[h], :] = a.astype(BF)
        return a

    a_fast = put_sums(0)
    for d in far:

        @pl.when(k + d < groups)
        def _():
            mid[d][0].start()
            mid[d][1].start()

    near_fast.start()

    pl.when(has_slow)(halo_slow.wait_recv)
    for c in (cols, cols + 1, cols + 2):
        inputs_first(c)
    first_pair((cols - 1, cols))
    first_pair((cols + 1,))
    for c in (cols - 2, cols - 1, cols):
        second(c)
    for c in (cols - 3, cols - 2, cols - 1):
        block(c)
    a_slow = put_sums(1)
    for d in far:
        pl.when((k + d < groups) & has_slow)(mid[d][2].start)
        pl.when(k + d < groups)(mid[d][3].start)
    pl.when(has_slow)(near_slow.start)

    rim_fast.wait_recv()
    near_fast.wait_recv()
    for d in range(1, groups):

        @pl.when(k >= d)
        def _():
            mid[d][0].wait_recv()
            mid[d][1].wait_recv()
            mid[d][3].wait_recv()

    def base_of(rows):
        base = st_ref[rows, :]
        for d in range(groups - 1):
            base = base + rx_ref[d, rows, :].astype(F32)
        return base

    def inputs_next(c, base, step, row):
        cov = xb_ref[:, lanes(place(c))].astype(F32)[CH:]
        for s, state in enumerate((base, base + step)):
            v = jnp.concatenate([state[row : row + CH], cov], axis=0)
            store_taps(x2_ref, v.astype(BF), 2 * (c + HALO) + s)

    base = base_of(pl.ds(0, 3 * rim))
    base_ref[...] = base[rim:]
    step = jnp.concatenate([rxs_ref[at_fast, :].astype(F32), a_fast, a_slow], axis=0)
    for c in range(-HALO, cols):
        inputs_next(c, base, step, row_of(c))
    for c in range(-2, cols - 1):
        first(c)
    for c in range(-1, cols - 2):
        second(c)
    for c in range(cols - 3):
        block(c)

    def lasts(d):
        return [
            remote(
                pd_ref.at[at],
                rxf_ref.at[d - 1, at],
                last_send.at[d - 1, h],
                last_recv.at[d - 1, h],
                k + d,
                t,
            )
            for h, at in enumerate(halves)
        ]

    last = {d: lasts(d) for d in range(1, groups)}

    def put_last(h):
        a, g = project(h)
        pd_ref[halves[h], :] = (g - pg_ref[halves[h], :].astype(F32)).astype(BF)
        for d in far:
            pl.when(k + d < groups)(last[d][h].start)
        return a, g

    a_fast, g_fast = put_last(0)

    @pl.when(has_slow)
    def _():
        rim_slow.wait_recv()
        near_slow.wait_recv()

    for d in range(1, groups):
        pl.when((k >= d) & has_slow)(mid[d][2].wait_recv)
    base = base_of(at_slow)
    step = rxs_ref[at_slow, :].astype(F32)
    for c in range(cols, cols + HALO):
        inputs_next(c, base, step, row_of(c) - 3 * rim)
    for c in (cols - 1, cols, cols + 1):
        first(c)
    for c in (cols - 2, cols - 1, cols):
        second(c)
    for c in (cols - 3, cols - 2, cols - 1):
        block(c)
    a_slow, g_slow = put_last(1)

    halo_fast.wait_send()
    rim_fast.wait_send()
    near_fast.wait_send()

    @pl.when(has_slow)
    def _():
        halo_slow.wait_send()
        rim_slow.wait_send()
        near_slow.wait_send()

    for d in range(1, groups):

        @pl.when(k + d < groups)
        def _():
            mid[d][0].wait_send()
            mid[d][1].wait_send()
            mid[d][3].wait_send()

        pl.when((k + d < groups) & has_slow)(mid[d][2].wait_send)

    for d in range(1, groups):

        @pl.when(k >= d)
        def _():
            last[d][0].wait_recv()
            last[d][1].wait_recv()

    base = base_ref[...]
    for d in range(groups - 1):
        base = base + rxf_ref[d].astype(F32)
    sums = [
        base + jnp.concatenate(halves_of, axis=0)
        for halves_of in ((a_fast, a_slow), (g_fast, g_slow))
    ]

    def put_result(c, i):
        for s in range(2):
            out_ref[s, :, c, :] = sums[s][CH * i : CH * (i + 1)]

    either_way(put_result)
    for d in range(1, groups):

        @pl.when(k + d < groups)
        def _():
            last[d][0].wait_send()
            last[d][1].wait_send()


def solution(mesh):
    groups, tiles = mesh.shape["step"], mesh.shape["tile"]

    def local(start_state, covariates, noise, embedding, w_in, w_first, w_second, w_out):
        cols = start_state.shape[1]
        wide = cols + 2 * HALO
        hbm = pl.BlockSpec(memory_space=pltpu.HBM)
        dma = pltpu.SemaphoreType.DMA
        w_in = jnp.swapaxes(w_in, 1, 2).reshape(144, 128)

        def body(*refs):
            kernel(groups, tiles, *refs)

        args = [
            pltpu.with_memory_space_constraint(v, pltpu.HBM)
            for v in (start_state, covariates, noise, embedding, w_in, w_first, w_second, w_out)
        ]
        return pl.pallas_call(
            body,
            out_shape=pltpu.VMEM((2, 4, cols, ROWS), F32),
            in_specs=[hbm] * 8,
            out_specs=pl.BlockSpec(memory_space=pltpu.VMEM),
            scratch_shapes=[
                pltpu.VMEM((CH, cols, ROWS), F32),
                pltpu.VMEM((12, cols, ROWS), BF),
                pltpu.VMEM((2, CH, cols, ROWS), F32),
                pltpu.VMEM((2, 128), F32),
                pltpu.VMEM((144, 128), BF),
                pltpu.VMEM((CH, 128), BF),
                pltpu.VMEM((12, cols, ROWS), F32),
                pltpu.VMEM((2 * CH * cols, ROWS), F32),
                pltpu.VMEM((CH * cols, ROWS), F32),
                pltpu.VMEM((16, wide * ROWS), BF),
                pltpu.VMEM((48, wide * ROWS), BF),
                pltpu.VMEM((48, wide * 2 * ROWS), BF),
                pltpu.VMEM((128, 144), BF),
                pltpu.VMEM((128, 1152), BF),
                pltpu.VMEM((128, 1152), BF),
                pltpu.VMEM((CH * cols, 128 * cols), BF),
                pltpu.VMEM((128, 2 * ROWS), F32),
                pltpu.VMEM((2, CH * cols, ROWS), F32),
                pltpu.VMEM((384, (wide - 2) * 2 * ROWS), BF),
                pltpu.VMEM((384, (wide - 4) * 2 * ROWS), BF),
                pltpu.VMEM((128 * cols, 2 * ROWS), BF),
                pltpu.VMEM((CH * cols, ROWS), BF),
                pltpu.VMEM((CH * cols, ROWS), BF),
                pltpu.VMEM((CH * cols, ROWS), BF),
                pltpu.VMEM((groups - 1, 2 * CH * cols, ROWS), BF),
                pltpu.VMEM((2 * CH * cols, ROWS), BF),
                pltpu.VMEM((groups - 1, CH * cols, ROWS), BF),
                dma((5,)),
                dma((3,)),
                dma((2, 9)),
                dma((2,)),
                dma((2,)),
                dma((2,)),
                dma((2,)),
                dma((2,)),
                dma((2,)),
                dma((groups - 1, 4)),
                dma((groups - 1, 4)),
                dma((groups - 1, 2)),
                dma((groups - 1, 2)),
                pltpu.SemaphoreType.REGULAR((groups - 1,)),
            ],
            compiler_params=pltpu.CompilerParams(
                collective_id=0, has_side_effects=True, vmem_limit_bytes=40 << 20
            ),
        )(*args)

    in_specs = (
        P(None, "tile", None),
        P(None, "tile", None),
        P("step", None, "tile", None),
        P("step", None),
        P(),
        P(),
        P(),
        P(),
    )
    out_specs = P("step", None, "tile", None)
    return jax.shard_map(local, mesh=mesh, in_specs=in_specs, out_specs=out_specs, check_vma=False)
```

time: 19.1 us -> 18.5 us (0.969)
  the two profiles are of different devices: /device:TPU:127 before, /device:TPU:184 now
where the time goes in v5:
time: 18.5 us; the launch traced here: 18.4 us
  Pallas kernels  17.8 us (96%)
  local copies, waits for them, and re-layouts  0.62 us (3%)
    pallas_call x1, Pallas kernels, local(): pl.pallas_call(body, out_shape=pltpu.VMEM((2, 4, cols, ROWS), F32), in_sp...  17.8 us
    unnamed x1, local copies, waits for them, and re-layouts  0.62 us

profile of v5, /device:TPU:184, one launch (start us, length us, event | category | flops | bytes accessed | tf_op | source)
XLA Modules:
  0.0 18.4 jit_solution(4189758601621453402)
XLA Ops:
  0.0 17.8 %shard_map.82 = f32[2,4,8,128]{3,2,1,0:T(8,128)S(1)} custom-call(f32[4,8,128]{2,1,0:T(8,128)} %refs_0_.1, bf16[12,8,128]{2,1,0:T(8,128)(2,1)} %refs_1_.1, f32[2,4,8,128]{3,2,1,0:T(8,128)} %refs_2_.1, f32[2,128]{1,0:T(2,128)} %refs_3_.1, bf16[144,128]{1,0:T(8,128)(2,1)} %bitcast.3, bf16[9,128,128]{2,1,0:T(8,128)(2,1)} %refs_5_.1, ...), custom_call_target="tpu_custom_call" | custom-call | tf_op jit(solution)/shard_map/pallas_call | solution.py:546
  17.8 0.6 %copy.10 = f32[2,4,8,128]{3,2,1,0:T(8,128)} copy(f32[2,4,8,128]{3,2,1,0:T(8,128)S(1)} %shard_map.82) | data formatting | bytes 65536

commit v6 on v5

--- a/solution.py
+++ b/solution.py
@@ -46,12 +46,14 @@
     w1_ref,
     w2_ref,
     w3_ref,
-    wo_ref,
+    wo0_ref,
+    wo1_ref,
     eb_ref,
     nz_ref,
     fh_ref,
     sh_ref,
-    bo_ref,
+    bo0_ref,
+    bo1_ref,
     pa_ref,
     pg_ref,
     pd_ref,
@@ -76,8 +78,9 @@
     k = lax.axis_index("step")
     t = lax.axis_index("tile")
     cols = start_ref.shape[1]
-    half = cols // 2
-    rim = CH * half
+    soon = cols - HALO
+    rim = 16
+    early, late = 2 * rim, rim
 
     even = t % 2 == 0
     fast = jnp.where(even, t + 1, t - 1)
@@ -114,7 +117,7 @@
         pltpu.make_async_copy(
             win_hbm.at[pl.ds(a * 48, 48)],
             win_ref.at[pl.ds(pl.multiple_of(turned(a, 3) * 48, 48), 48)],
-            win_sem.at[a],
+            win_sem,
         )
         for a in range(3)
     ]
@@ -125,7 +128,7 @@
                 pltpu.make_async_copy(
                     src.at[3 * a + b],
                     dst.at[:, pl.ds(pl.multiple_of((3 * turned(a, 3) + b) * 128, 128), 128)],
-                    w_sem.at[n, 3 * a + b],
+                    w_sem.at[n],
                 )
                 for a in range(3)
                 for b in range(3)
@@ -164,8 +167,11 @@
         if i < 0:
             return CH * (-1 - i)
         if i >= cols:
-            return 3 * rim + CH * (half - 1 - (i - cols))
-        return rim + CH * i
+            return rim + early + late + CH * (HALO - 1 - (i - cols))
+        return rim + own_row(i)
+
+    def own_row(i):
+        return CH * i if i < soon else early + CH * (i - soon)
 
     get_cov.wait()
     covf_ref[...] = cov_ref[...].astype(F32)
@@ -192,6 +198,28 @@
             device_id_type=MESH,
         )
 
+    def for_later(f):
+        def at(d):
+            if d < groups:
+
+                @pl.when(k + d < groups)
+                def _():
+                    f(d)
+                    at(d + 1)
+
+        at(1)
+
+    def for_earlier(f):
+        def at(d):
+            if d < groups:
+
+                @pl.when(k >= d)
+                def _():
+                    f(d)
+                    at(d + 1)
+
+        at(1)
+
     def to_sides(ref, parts, send, recv):
         at_fast, own_fast, own_slow, at_slow = parts
         return (
@@ -204,14 +232,16 @@
     pl.when(has_slow)(halo_slow.start)
     halo_fast.start()
 
-    at_fast, own_fast, own_slow, at_slow = quarters = [pl.ds(n * rim, rim) for n in range(4)]
-    halves = (pl.ds(0, rim), pl.ds(rim, rim))
+    at_fast, own_fast = pl.ds(0, rim), pl.ds(rim, rim)
+    own_soon, own_late = pl.ds(rim, early), pl.ds(rim + early, late)
+    at_slow = pl.ds(rim + early + late, rim)
+    facing, parts = pl.ds(0, rim), (pl.ds(0, early), pl.ds(early, late))
 
     def put_state(c, i):
         st_ref[row_of(i) : row_of(i) + CH, :] = start_ref[:, c, :]
 
     either_way(put_state)
-    rim_fast, rim_slow = to_sides(st_ref, quarters, rim_send, rim_recv)
+    rim_fast, rim_slow = to_sides(st_ref, (at_fast, own_fast, own_late, at_slow), rim_send, rim_recv)
     pl.when(has_slow)(rim_slow.start)
     rim_fast.start()
 
@@ -224,8 +254,7 @@
 
     pass_on(0)
 
-    for c in get_win:
-        c.wait()
+    pltpu.make_async_copy(win_ref, win_ref, win_sem).wait()
     w1_ref[...] = jnp.transpose(win_ref[...].astype(F32) * 0.5).astype(BF)
     get_embed.wait()
     et = 0.5 * jnp.transpose(jnp.concatenate([embed_ref[...], jnp.zeros((6, 128), F32)], axis=0))
@@ -236,6 +265,8 @@
     keep_first = (lane > 0).astype(F32).astype(BF)
     keep_last = (lane < ROWS - 1).astype(F32).astype(BF)
     slow_one = has_slow.astype(F32)
+    bo_refs = (bo0_ref, bo1_ref)
+    wo_refs = (wo0_ref, wo1_ref)
 
     def store_taps(ref, x, at):
         n = x.shape[0]
@@ -283,16 +314,20 @@
     def block(c):
         h = silu_of_half(jnp.dot(w3_ref[...], taps_of(sh_ref, c), preferred_element_type=F32))
         h = (h + fh_ref[128:256, pl.ds((c + 2) * 2 * ROWS, 2 * ROWS)].astype(F32)).astype(BF)
+        n, j = (0, c) if c < soon else (1, c - soon)
+        count = (soon, HALO)[n]
         for s in range(2):
-            at = (s * half + c % half) * 128
-            bo_ref[at : at + 128, pl.ds((c // half) * ROWS, ROWS)] = h[:, s * ROWS : (s + 1) * ROWS]
-
-    def project(h):
-        p = jnp.dot(wo_ref[...], bo_ref[:, lanes(h)], preferred_element_type=F32)
-        return p[:rim] + nz_ref[0, halves[h], :], p[rim:] + nz_ref[1, halves[h], :]
+            at = (s * count + j) * 128
+            bo_refs[n][at : at + 128, :] = h[:, s * ROWS : (s + 1) * ROWS]
+
+    def project(n):
+        p = jnp.dot(wo_refs[n][...], bo_refs[n][...], preferred_element_type=F32)
+        size = (early, late)[n]
+        return p[:size] + nz_ref[0, parts[n], :], p[size:] + nz_ref[1, parts[n], :]
 
     def inputs_first(c):
-        store_taps(x1_ref, xb_ref[:, lanes(place(c))], c + HALO)
+        x = xb_ref[:, lanes(place(c))]
+        store_taps(x1_ref, x, c + HALO)
 
     for c in range(cols):
         inputs_first(c)
@@ -300,33 +335,35 @@
         first_pair((c, c + 1))
     hear(0)
     pass_on(1)
-    for c in weights[0]:
-        c.wait()
+    pltpu.make_async_copy(w2_ref, w2_ref, w_sem.at[0]).wait()
     w2_ref[...] = w2_ref[...] * BF(0.5)
     for c in range(2, cols - 2):
         second(c)
     hear(1)
     pass_on(2)
-    for c in weights[1]:
-        c.wait()
+    pltpu.make_async_copy(w3_ref, w3_ref, w_sem.at[1]).wait()
     w3_ref[...] = w3_ref[...] * BF(0.5)
     for c in range(3, cols - 3):
         block(c)
     get_wout.wait()
     wo = wout_ref[...].astype(F32) * (1.0 / STEPS)
     none = jnp.zeros((CH, 128), F32)
-    lhs = []
-    for sums in range(2):
-        for j in range(half):
-            parts = [wo if s <= sums and i == j else none for s in range(2) for i in range(half)]
-            lhs.append(jnp.concatenate(parts, axis=1))
-    wo_ref[...] = jnp.concatenate(lhs, axis=0).astype(BF)
+    for n, (count, size) in enumerate(((soon, early), (HALO, late))):
+        lhs = []
+        for sums in range(2):
+            for j in range(count):
+                blocks = [wo if s <= sums and i == j else none for s in range(2) for i in range(count)]
+                lhs.append(jnp.concatenate(blocks, axis=1))
+            lhs.append(jnp.zeros((size - CH * count, 2 * 128 * count), F32))
+        wo_refs[n][...] = jnp.concatenate(lhs, axis=0).astype(BF)
     get_noise.wait()
+    nz_ref[...] = jnp.zeros_like(nz_ref)
 
     def put_noise(c, i):
+        at = own_row(i)
         n0 = 0.3 * noise_ref[0, :, c, :]
-        nz_ref[0, CH * i : CH * (i + 1), :] = n0
-        nz_ref[1, CH * i : CH * (i + 1), :] = n0 + 0.3 * noise_ref[1, :, c, :]
+        nz_ref[0, at : at + CH, :] = n0
+        nz_ref[1, at : at + CH, :] = n0 + 0.3 * noise_ref[1, :, c, :]
 
     either_way(put_noise)
 
@@ -355,35 +392,42 @@
             )
 
         return (
-            send(0, halves[0], at_fast, fast),
-            send(1, halves[0], own_fast, t),
-            send(2, halves[1], at_slow, slow),
-            send(3, halves[1], own_slow, t),
+            send(0, facing, at_fast, fast),
+            send(1, parts[0], own_soon, t),
+            send(2, parts[1], at_slow, slow),
+            send(3, parts[1], own_late, t),
         )
 
     mid = {d: mids(d) for d in range(1, groups)}
     near_fast = remote(
-        pa_ref.at[halves[0]], rxs_ref.at[at_fast], near_send.at[0], near_recv.at[0], k, fast
+        pa_ref.at[facing], rxs_ref.at[at_fast], near_send.at[0], near_recv.at[0], k, fast
     )
     near_slow = remote(
-        pa_ref.at[halves[1]], rxs_ref.at[at_slow], near_send.at[1], near_recv.at[1], k, slow
+        pa_ref.at[parts[1]], rxs_ref.at[at_slow], near_send.at[1], near_recv.at[1], k, slow
     )
-    far = sorted(range(1, groups), key=lambda d: -min(d, groups - d))
-
-    def put_sums(h):
-        a, g = project(h)
-        pg_ref[halves[h], :] = g.astype(BF)
-        pa_ref[halves[h], :] = a.astype(BF)
+
+    def put_sums(n):
+        a, g = project(n)
+        pg_ref[parts[n], :] = g.astype(BF)
+        pa_ref[parts[n], :] = a.astype(BF)
         return a
 
-    a_fast = put_sums(0)
-    for d in far:
-
-        @pl.when(k + d < groups)
-        def _():
-            mid[d][0].start()
-            mid[d][1].start()
-
+    def start_mid(*ns):
+        def f(d):
+            for n in ns:
+                mid[d][n].start()
+
+        return f
+
+    def wait_mid(*ns):
+        def f(d):
+            for n in ns:
+                mid[d][n].wait_recv()
+
+        return f
+
+    a_soon = put_sums(0)
+    for_later(start_mid(1, 0))
     near_fast.start()
 
     pl.when(has_slow)(halo_slow.wait_recv)
@@ -395,21 +439,18 @@
         second(c)
     for c in (cols - 3, cols - 2, cols - 1):
         block(c)
-    a_slow = put_sums(1)
-    for d in far:
-        pl.when((k + d < groups) & has_slow)(mid[d][2].start)
-        pl.when(k + d < groups)(mid[d][3].start)
-    pl.when(has_slow)(near_slow.start)
+    a_late = put_sums(1)
+
+    @pl.when(has_slow)
+    def _():
+        for_later(start_mid(2, 3))
+        near_slow.start()
+
+    pl.when(jnp.logical_not(has_slow))(lambda: for_later(start_mid(3)))
 
     rim_fast.wait_recv()
     near_fast.wait_recv()
-    for d in range(1, groups):
-
-        @pl.when(k >= d)
-        def _():
-            mid[d][0].wait_recv()
-            mid[d][1].wait_recv()
-            mid[d][3].wait_recv()
+    for_earlier(wait_mid(0, 1))
 
     def base_of(rows):
         base = st_ref[rows, :]
@@ -423,107 +464,100 @@
             v = jnp.concatenate([state[row : row + CH], cov], axis=0)
             store_taps(x2_ref, v.astype(BF), 2 * (c + HALO) + s)
 
-    base = base_of(pl.ds(0, 3 * rim))
-    base_ref[...] = base[rim:]
-    step = jnp.concatenate([rxs_ref[at_fast, :].astype(F32), a_fast, a_slow], axis=0)
-    for c in range(-HALO, cols):
-        inputs_next(c, base, step, row_of(c))
-    for c in range(-2, cols - 1):
-        first(c)
-    for c in range(-1, cols - 2):
-        second(c)
-    for c in range(cols - 3):
-        block(c)
+    def next_columns(columns, rows, step, firsts, seconds, blocks):
+        base = base_of(rows)
+        for c in columns:
+            inputs_next(c, base, step, row_of(c) - rows.start)
+        for c in firsts:
+            first(c)
+        for c in seconds:
+            second(c)
+        for c in blocks:
+            block(c)
+        return base
+
+    step = jnp.concatenate([rxs_ref[at_fast, :].astype(F32), a_soon], axis=0)
+    base = next_columns(
+        range(-HALO, soon), pl.ds(0, rim + early), step, range(-2, soon - 1), range(-1, soon - 2), range(soon - 3)
+    )
+    base_ref[parts[0], :] = base[rim:]
+
+    for_earlier(wait_mid(3))
+    base_ref[parts[1], :] = next_columns(
+        range(soon, cols), own_late, a_late, range(soon - 1, cols - 1), range(soon - 2, cols - 2), range(soon - 3, soon)
+    )
 
     def lasts(d):
         return [
             remote(
                 pd_ref.at[at],
                 rxf_ref.at[d - 1, at],
-                last_send.at[d - 1, h],
-                last_recv.at[d - 1, h],
+                last_send.at[d - 1, n],
+                last_recv.at[d - 1, n],
                 k + d,
                 t,
             )
-            for h, at in enumerate(halves)
+            for n, at in enumerate(parts)
         ]
 
     last = {d: lasts(d) for d in range(1, groups)}
 
-    def put_last(h):
-        a, g = project(h)
-        pd_ref[halves[h], :] = (g - pg_ref[halves[h], :].astype(F32)).astype(BF)
-        for d in far:
-            pl.when(k + d < groups)(last[d][h].start)
+    def put_last(n):
+        a, g = project(n)
+        pd_ref[parts[n], :] = (g - pg_ref[parts[n], :].astype(F32)).astype(BF)
+        for_later(lambda d: last[d][n].start())
         return a, g
 
-    a_fast, g_fast = put_last(0)
+    a_soon, g_soon = put_last(0)
 
     @pl.when(has_slow)
     def _():
         rim_slow.wait_recv()
         near_slow.wait_recv()
-
-    for d in range(1, groups):
-        pl.when((k >= d) & has_slow)(mid[d][2].wait_recv)
-    base = base_of(at_slow)
-    step = rxs_ref[at_slow, :].astype(F32)
-    for c in range(cols, cols + HALO):
-        inputs_next(c, base, step, row_of(c) - 3 * rim)
-    for c in (cols - 1, cols, cols + 1):
-        first(c)
-    for c in (cols - 2, cols - 1, cols):
-        second(c)
-    for c in (cols - 3, cols - 2, cols - 1):
-        block(c)
-    a_slow, g_slow = put_last(1)
-
-    halo_fast.wait_send()
-    rim_fast.wait_send()
-    near_fast.wait_send()
+        for_earlier(wait_mid(2))
+
+    next_columns(
+        range(cols, cols + HALO),
+        at_slow,
+        rxs_ref[at_slow, :].astype(F32),
+        range(cols - 1, cols + 2),
+        range(cols - 2, cols + 1),
+        range(soon, cols),
+    )
+    a_late, g_late = put_last(1)
+
+    def all_sent(*copies):
+        for c in copies:
+            c.wait_send()
+
+    all_sent(halo_fast, rim_fast, near_fast)
+    for_later(lambda d: all_sent(mid[d][0], mid[d][1], mid[d][3]))
 
     @pl.when(has_slow)
     def _():
-        halo_slow.wait_send()
-        rim_slow.wait_send()
-        near_slow.wait_send()
-
-    for d in range(1, groups):
-
-        @pl.when(k + d < groups)
-        def _():
-            mid[d][0].wait_send()
-            mid[d][1].wait_send()
-            mid[d][3].wait_send()
-
-        pl.when((k + d < groups) & has_slow)(mid[d][2].wait_send)
-
-    for d in range(1, groups):
-
-        @pl.when(k >= d)
-        def _():
-            last[d][0].wait_recv()
-            last[d][1].wait_recv()
-
+        all_sent(halo_slow, rim_slow, near_slow)
+        for_later(lambda d: all_sent(mid[d][2]))
+
+    def got(d):
+        for c in last[d]:
+            c.wait_recv()
+
+    for_earlier(got)
     base = base_ref[...]
     for d in range(groups - 1):
         base = base + rxf_ref[d].astype(F32)
     sums = [
-        base + jnp.concatenate(halves_of, axis=0)
-        for halves_of in ((a_fast, a_slow), (g_fast, g_slow))
+        base + jnp.concatenate(both, axis=0) for both in ((a_soon, a_late), (g_soon, g_late))
     ]
 
     def put_result(c, i):
+        at = own_row(i)
         for s in range(2):
-            out_ref[s, :, c, :] = sums[s][CH * i : CH * (i + 1)]
+            out_ref[s, :, c, :] = sums[s][at : at + CH]
 
     either_way(put_result)
-    for d in range(1, groups):
-
-        @pl.when(k + d < groups)
-        def _():
-            last[d][0].wait_send()
-            last[d][1].wait_send()
+
+    for_later(lambda d: all_sent(*last[d]))
 
 
 def solution(mesh):
@@ -532,6 +566,7 @@
     def local(start_state, covariates, noise, embedding, w_in, w_first, w_second, w_out):
         cols = start_state.shape[1]
         wide = cols + 2 * HALO
+        own = 48
         hbm = pl.BlockSpec(memory_space=pltpu.HBM)
         dma = pltpu.SemaphoreType.DMA
         w_in = jnp.swapaxes(w_in, 1, 2).reshape(144, 128)
@@ -556,29 +591,31 @@
                 pltpu.VMEM((144, 128), BF),
                 pltpu.VMEM((CH, 128), BF),
                 pltpu.VMEM((12, cols, ROWS), F32),
-                pltpu.VMEM((2 * CH * cols, ROWS), F32),
-                pltpu.VMEM((CH * cols, ROWS), F32),
+                pltpu.VMEM((own + 32, ROWS), F32),
+                pltpu.VMEM((own, ROWS), F32),
                 pltpu.VMEM((16, wide * ROWS), BF),
                 pltpu.VMEM((48, wide * ROWS), BF),
                 pltpu.VMEM((48, wide * 2 * ROWS), BF),
                 pltpu.VMEM((128, 144), BF),
                 pltpu.VMEM((128, 1152), BF),
                 pltpu.VMEM((128, 1152), BF),
-                pltpu.VMEM((CH * cols, 128 * cols), BF),
+                pltpu.VMEM((64, 256 * (cols - HALO)), BF),
+                pltpu.VMEM((32, 256 * HALO), BF),
                 pltpu.VMEM((128, 2 * ROWS), F32),
-                pltpu.VMEM((2, CH * cols, ROWS), F32),
+                pltpu.VMEM((2, own, ROWS), F32),
                 pltpu.VMEM((384, (wide - 2) * 2 * ROWS), BF),
                 pltpu.VMEM((384, (wide - 4) * 2 * ROWS), BF),
-                pltpu.VMEM((128 * cols, 2 * ROWS), BF),
-                pltpu.VMEM((CH * cols, ROWS), BF),
-                pltpu.VMEM((CH * cols, ROWS), BF),
-                pltpu.VMEM((CH * cols, ROWS), BF),
-                pltpu.VMEM((groups - 1, 2 * CH * cols, ROWS), BF),
-                pltpu.VMEM((2 * CH * cols, ROWS), BF),
-                pltpu.VMEM((groups - 1, CH * cols, ROWS), BF),
+                pltpu.VMEM((256 * (cols - HALO), ROWS), BF),
+                pltpu.VMEM((256 * HALO, ROWS), BF),
+                pltpu.VMEM((own, ROWS), BF),
+                pltpu.VMEM((own, ROWS), BF),
+                pltpu.VMEM((own, ROWS), BF),
+                pltpu.VMEM((groups - 1, own + 32, ROWS), BF),
+                pltpu.VMEM((own + 32, ROWS), BF),
+                pltpu.VMEM((groups - 1, own, ROWS), BF),
                 dma((5,)),
-                dma((3,)),
-                dma((2, 9)),
+                dma(()),
+                dma((2,)),
                 dma((2,)),
                 dma((2,)),
                 dma((2,)),

time: 18.5 us -> 17.8 us (0.962)
  the two profiles are of different devices: /device:TPU:184 before, /device:TPU:248 now
where the time goes in v6:
time: 17.8 us; the launch traced here: 17.6 us
  Pallas kernels  17 us (96%)
  local copies, waits for them, and re-layouts  0.62 us (3%)
    pallas_call x1, Pallas kernels, local(): pl.pallas_call(body, out_shape=pltpu.VMEM((2, 4, cols, ROWS), F32), in_sp...  17 us
    unnamed x1, local copies, waits for them, and re-layouts  0.62 us

profile of v6, /device:TPU:248, one launch (start us, length us, event | category | flops | bytes accessed | tf_op | source)
XLA Modules:
  0.0 17.6 jit_solution(4459605542185996396)
XLA Ops:
  0.0 17.0 %shard_map.82 = f32[2,4,8,128]{3,2,1,0:T(8,128)S(1)} custom-call(f32[4,8,128]{2,1,0:T(8,128)} %refs_0_.1, bf16[12,8,128]{2,1,0:T(8,128)(2,1)} %refs_1_.1, f32[2,4,8,128]{3,2,1,0:T(8,128)} %refs_2_.1, f32[2,128]{1,0:T(2,128)} %refs_3_.1, bf16[144,128]{1,0:T(8,128)(2,1)} %bitcast.3, bf16[9,128,128]{2,1,0:T(8,128)(2,1)} %refs_5_.1, ...), custom_call_target="tpu_custom_call" | custom-call | tf_op jit(solution)/shard_map/pallas_call | solution.py:581
  17.0 0.6 %copy.10 = f32[2,4,8,128]{3,2,1,0:T(8,128)} copy(f32[2,4,8,128]{3,2,1,0:T(8,128)S(1)} %shard_map.82) | data formatting | bytes 65536

commit v7 on v6

--- a/solution.py
+++ b/solution.py
@@ -146,8 +146,8 @@
         pl.semaphore_signal(sem, inc=1, device_id=(step, tile), device_id_type=MESH)
 
     pl.when(has_slow)(lambda: signal(barrier, k, slow))
-    pl.when(k > 0)(lambda: signal(barrier, k - 1, t))
-    pl.when(k < groups - 1)(lambda: signal(barrier, k + 1, t))
+    for d in (groups // 2, *[d for d in range(1, groups) if d != groups // 2]):
+        signal(barrier, lax.rem(k + d, groups), t)
     signal(barrier, k, fast)
 
     for c in (*get_win, get_embed, *weights[0], *weights[1], get_noise, get_wout):
@@ -186,7 +186,7 @@
     def one(p):
         return p.astype(jnp.int32)
 
-    pl.semaphore_wait(barrier, 1 + one(has_slow) + one(k > 0) + one(k < groups - 1))
+    pl.semaphore_wait(barrier, groups + one(has_slow))
 
     def remote(src, dst, send, recv, step, tile):
         return pltpu.make_async_remote_copy(
@@ -245,14 +245,7 @@
     pl.when(has_slow)(rim_slow.start)
     rim_fast.start()
 
-    def pass_on(n):
-        if n < groups - 1:
-            pl.when((k > 0) & (k < groups - n))(lambda: signal(chain.at[n], k - 1, t))
-
-    def hear(n):
-        pl.when(k < groups - 1 - n)(lambda: pl.semaphore_wait(chain.at[n], 1))
-
-    pass_on(0)
+    for_earlier(lambda d: signal(chain, k - d, t))
 
     pltpu.make_async_copy(win_ref, win_ref, win_sem).wait()
     w1_ref[...] = jnp.transpose(win_ref[...].astype(F32) * 0.5).astype(BF)
@@ -333,14 +326,10 @@
         inputs_first(c)
     for c in range(1, cols - 1, 2):
         first_pair((c, c + 1))
-    hear(0)
-    pass_on(1)
     pltpu.make_async_copy(w2_ref, w2_ref, w_sem.at[0]).wait()
     w2_ref[...] = w2_ref[...] * BF(0.5)
     for c in range(2, cols - 2):
         second(c)
-    hear(1)
-    pass_on(2)
     pltpu.make_async_copy(w3_ref, w3_ref, w_sem.at[1]).wait()
     w3_ref[...] = w3_ref[...] * BF(0.5)
     for c in range(3, cols - 3):
@@ -376,9 +365,6 @@
         second(c)
     for c in (2, 1, 0):
         block(c)
-    for n in range(2, groups - 1):
-        hear(n)
-        pass_on(n + 1)
 
     def mids(d):
         def send(n, src, dst, tile):
@@ -427,6 +413,7 @@
         return f
 
     a_soon = put_sums(0)
+    pl.when(k < groups - 1)(lambda: pl.semaphore_wait(chain, groups - 1 - k))
     for_later(start_mid(1, 0))
     near_fast.start()
 
@@ -626,7 +613,7 @@
                 dma((groups - 1, 4)),
                 dma((groups - 1, 2)),
                 dma((groups - 1, 2)),
-                pltpu.SemaphoreType.REGULAR((groups - 1,)),
+                pltpu.SemaphoreType.REGULAR,
             ],
             compiler_params=pltpu.CompilerParams(
                 collective_id=0, has_side_effects=True, vmem_limit_bytes=40 << 20

time: 17.8 us -> 17.4 us (0.978)
  the two profiles are of different devices: /device:TPU:248 before, /device:TPU:152 now
where the time goes in v7:
time: 17.4 us; the launch traced here: 17.2 us
  Pallas kernels  16.6 us (95%)
  local copies, waits for them, and re-layouts  0.62 us (4%)
    pallas_call x1, Pallas kernels, local(): pl.pallas_call(body, out_shape=pltpu.VMEM((2, 4, cols, ROWS), F32), in_sp...  16.6 us
    unnamed x1, local copies, waits for them, and re-layouts  0.62 us

profile of v7, /device:TPU:152, one launch (start us, length us, event | category | flops | bytes accessed | tf_op | source)
XLA Modules:
  0.0 17.2 jit_solution(15097039495682797426)
XLA Ops:
  0.0 16.6 %shard_map.82 = f32[2,4,8,128]{3,2,1,0:T(8,128)S(1)} custom-call(f32[4,8,128]{2,1,0:T(8,128)} %refs_0_.1, bf16[12,8,128]{2,1,0:T(8,128)(2,1)} %refs_1_.1, f32[2,4,8,128]{3,2,1,0:T(8,128)} %refs_2_.1, f32[2,128]{1,0:T(2,128)} %refs_3_.1, bf16[144,128]{1,0:T(8,128)(2,1)} %bitcast.3, bf16[9,128,128]{2,1,0:T(8,128)(2,1)} %refs_5_.1, ...), custom_call_target="tpu_custom_call" | custom-call | tf_op jit(solution)/shard_map/pallas_call | solution.py:568
  16.6 0.6 %copy.10 = f32[2,4,8,128]{3,2,1,0:T(8,128)} copy(f32[2,4,8,128]{3,2,1,0:T(8,128)S(1)} %shard_map.82) | data formatting | bytes 65536

commit v8 on v7

--- a/solution.py
+++ b/solution.py
@@ -73,7 +73,8 @@
     mid_recv,
     last_send,
     last_recv,
-    chain,
+    up,
+    down,
 ):
     k = lax.axis_index("step")
     t = lax.axis_index("tile")
@@ -134,8 +135,6 @@
                 for b in range(3)
             ]
         )
-    get_start.start()
-    get_cov.start()
 
     for ref in (st_ref, xb_ref, rx_ref, rxs_ref, rxf_ref):
         ref[...] = jnp.zeros_like(ref)
@@ -146,11 +145,11 @@
         pl.semaphore_signal(sem, inc=1, device_id=(step, tile), device_id_type=MESH)
 
     pl.when(has_slow)(lambda: signal(barrier, k, slow))
-    for d in (groups // 2, *[d for d in range(1, groups) if d != groups // 2]):
-        signal(barrier, lax.rem(k + d, groups), t)
+    pl.when(k > 0)(lambda: signal(barrier, k - 1, t))
+    pl.when(k < groups - 1)(lambda: signal(barrier, k + 1, t))
     signal(barrier, k, fast)
 
-    for c in (*get_win, get_embed, *weights[0], *weights[1], get_noise, get_wout):
+    for c in (get_cov, get_start, *get_win, get_embed, *weights[0], *weights[1], get_noise, get_wout):
         c.start()
 
     def lanes(n, width=1):
@@ -186,7 +185,7 @@
     def one(p):
         return p.astype(jnp.int32)
 
-    pl.semaphore_wait(barrier, groups + one(has_slow))
+    pl.semaphore_wait(barrier, 1 + one(has_slow) + one(k > 0) + one(k < groups - 1))
 
     def remote(src, dst, send, recv, step, tile):
         return pltpu.make_async_remote_copy(
@@ -245,7 +244,18 @@
     pl.when(has_slow)(rim_slow.start)
     rim_fast.start()
 
-    for_earlier(lambda d: signal(chain, k - d, t))
+    pl.when((k > 0) & (k < groups - 1))(lambda: signal(up.at[0], k + 1, t))
+    pl.when(k > 0)(lambda: signal(down.at[0], k - 1, t))
+
+    def tell_earlier():
+        for n in range(1, groups - 1):
+
+            @pl.when(k > n)
+            def _():
+                pl.semaphore_wait(up.at[n - 1], 1)
+                if n < groups - 2:
+                    pl.when(k < groups - 1)(lambda: signal(up.at[n], k + 1, t))
+                signal(down.at[n], k - n - 1, t)
 
     pltpu.make_async_copy(win_ref, win_ref, win_sem).wait()
     w1_ref[...] = jnp.transpose(win_ref[...].astype(F32) * 0.5).astype(BF)
@@ -328,6 +338,7 @@
         first_pair((c, c + 1))
     pltpu.make_async_copy(w2_ref, w2_ref, w_sem.at[0]).wait()
     w2_ref[...] = w2_ref[...] * BF(0.5)
+    tell_earlier()
     for c in range(2, cols - 2):
         second(c)
     pltpu.make_async_copy(w3_ref, w3_ref, w_sem.at[1]).wait()
@@ -398,13 +409,6 @@
         pa_ref[parts[n], :] = a.astype(BF)
         return a
 
-    def start_mid(*ns):
-        def f(d):
-            for n in ns:
-                mid[d][n].start()
-
-        return f
-
     def wait_mid(*ns):
         def f(d):
             for n in ns:
@@ -412,10 +416,15 @@
 
         return f
 
+    def start_soon(d):
+        pl.semaphore_wait(down.at[d - 1], 1)
+        mid[d][1].start()
+        mid[d][0].start()
+
+    patient = groups - 1
     a_soon = put_sums(0)
-    pl.when(k < groups - 1)(lambda: pl.semaphore_wait(chain, groups - 1 - k))
-    for_later(start_mid(1, 0))
     near_fast.start()
+    for_later(lambda d: start_soon(d) if d < patient else None)
 
     pl.when(has_slow)(halo_slow.wait_recv)
     for c in (cols, cols + 1, cols + 2):
@@ -428,12 +437,14 @@
         block(c)
     a_late = put_sums(1)
 
-    @pl.when(has_slow)
-    def _():
-        for_later(start_mid(2, 3))
-        near_slow.start()
-
-    pl.when(jnp.logical_not(has_slow))(lambda: for_later(start_mid(3)))
+    def start_late(d):
+        if d == patient:
+            start_soon(d)
+        pl.when(has_slow)(mid[d][2].start)
+        mid[d][3].start()
+
+    pl.when(has_slow)(near_slow.start)
+    for_later(start_late)
 
     rim_fast.wait_recv()
     near_fast.wait_recv()
@@ -613,7 +624,8 @@
                 dma((groups - 1, 4)),
                 dma((groups - 1, 2)),
                 dma((groups - 1, 2)),
-                pltpu.SemaphoreType.REGULAR,
+                pltpu.SemaphoreType.REGULAR((groups - 1,)),
+                pltpu.SemaphoreType.REGULAR((groups - 1,)),
             ],
             compiler_params=pltpu.CompilerParams(
                 collective_id=0, has_side_effects=True, vmem_limit_bytes=40 << 20

time: 17.4 us -> 16.8 us (0.966)
  Pallas kernels: 16.6 us -> 15.8 us
    pallas_call x1, Pallas kernels: 16.6 us -> 15.8 us  [local(): pl.pallas_call(body, out_shape=pltpu.VMEM((2, 4, cols, ROWS), F32), in_sp...]
where the time goes in v8:
time: 16.8 us; the launch traced here: 16.5 us
  Pallas kernels  15.8 us (94%)
  local copies, waits for them, and re-layouts  0.62 us (4%)
    pallas_call x1, Pallas kernels, local(): pl.pallas_call(body, out_shape=pltpu.VMEM((2, 4, cols, ROWS), F32), in_sp...  15.8 us
    unnamed x1, local copies, waits for them, and re-layouts  0.62 us

profile of v8, /device:TPU:152, one launch (start us, length us, event | category | flops | bytes accessed | tf_op | source)
XLA Modules:
  0.0 16.5 jit_solution(2960568187532113172)
XLA Ops:
  0.0 15.8 %shard_map.82 = f32[2,4,8,128]{3,2,1,0:T(8,128)S(1)} custom-call(f32[4,8,128]{2,1,0:T(8,128)} %refs_0_.1, bf16[12,8,128]{2,1,0:T(8,128)(2,1)} %refs_1_.1, f32[2,4,8,128]{3,2,1,0:T(8,128)} %refs_2_.1, f32[2,128]{1,0:T(2,128)} %refs_3_.1, bf16[144,128]{1,0:T(8,128)(2,1)} %bitcast.3, bf16[9,128,128]{2,1,0:T(8,128)(2,1)} %refs_5_.1, ...), custom_call_target="tpu_custom_call" | custom-call | tf_op jit(solution)/shard_map/pallas_call | solution.py:579
  15.9 0.6 %copy.10 = f32[2,4,8,128]{3,2,1,0:T(8,128)} copy(f32[2,4,8,128]{3,2,1,0:T(8,128)S(1)} %shard_map.82) | data formatting | bytes 65536

commit v9 on v8

--- a/solution.py
+++ b/solution.py
@@ -9,6 +9,7 @@
 SWEEPS = 2
 CH = 4
 HALO = 3
+FAR = 2 * HALO
 ROWS = 128
 BF = jnp.bfloat16
 F32 = jnp.float32
@@ -50,10 +51,12 @@
     wo1_ref,
     eb_ref,
     nz_ref,
+    nzs_ref,
     fh_ref,
     sh_ref,
     bo0_ref,
     bo1_ref,
+    bo2_ref,
     pa_ref,
     pg_ref,
     pd_ref,
@@ -67,13 +70,14 @@
     halo_recv,
     rim_send,
     rim_recv,
+    noise_send,
+    noise_recv,
     near_send,
     near_recv,
     mid_send,
     mid_recv,
     last_send,
     last_recv,
-    up,
     down,
 ):
     k = lax.axis_index("step")
@@ -90,6 +94,28 @@
 
     def turned(n, count):
         return jnp.where(even, count - 1 - n, n)
+
+    def for_later(f):
+        def at(d):
+            if d < groups:
+
+                @pl.when(k + d < groups)
+                def _():
+                    f(d)
+                    at(d + 1)
+
+        at(1)
+
+    def for_earlier(f):
+        def at(d):
+            if d < groups:
+
+                @pl.when(k >= d)
+                def _():
+                    f(d)
+                    at(d + 1)
+
+        at(1)
 
     def either_way(f):
         @pl.when(even)
@@ -136,7 +162,7 @@
             ]
         )
 
-    for ref in (st_ref, xb_ref, rx_ref, rxs_ref, rxf_ref):
+    for ref in (st_ref, xb_ref, nzs_ref, rx_ref, rxs_ref, rxf_ref):
         ref[...] = jnp.zeros_like(ref)
 
     barrier = pltpu.get_barrier_semaphore()
@@ -145,9 +171,8 @@
         pl.semaphore_signal(sem, inc=1, device_id=(step, tile), device_id_type=MESH)
 
     pl.when(has_slow)(lambda: signal(barrier, k, slow))
-    pl.when(k > 0)(lambda: signal(barrier, k - 1, t))
-    pl.when(k < groups - 1)(lambda: signal(barrier, k + 1, t))
     signal(barrier, k, fast)
+    for_later(lambda d: signal(barrier, k + d, t))
 
     for c in (get_cov, get_start, *get_win, get_embed, *weights[0], *weights[1], get_noise, get_wout):
         c.start()
@@ -159,7 +184,7 @@
         if i < 0:
             return -1 - i
         if i >= cols:
-            return HALO + cols + HALO - 1 - (i - cols)
+            return HALO + cols + FAR - 1 - (i - cols)
         return HALO + i
 
     def row_of(i):
@@ -185,7 +210,7 @@
     def one(p):
         return p.astype(jnp.int32)
 
-    pl.semaphore_wait(barrier, 1 + one(has_slow) + one(k > 0) + one(k < groups - 1))
+    pl.semaphore_wait(barrier, 1 + one(has_slow) + k)
 
     def remote(src, dst, send, recv, step, tile):
         return pltpu.make_async_remote_copy(
@@ -197,28 +222,6 @@
             device_id_type=MESH,
         )
 
-    def for_later(f):
-        def at(d):
-            if d < groups:
-
-                @pl.when(k + d < groups)
-                def _():
-                    f(d)
-                    at(d + 1)
-
-        at(1)
-
-    def for_earlier(f):
-        def at(d):
-            if d < groups:
-
-                @pl.when(k >= d)
-                def _():
-                    f(d)
-                    at(d + 1)
-
-        at(1)
-
     def to_sides(ref, parts, send, recv):
         at_fast, own_fast, own_slow, at_slow = parts
         return (
@@ -226,7 +229,10 @@
             remote(ref.at[own_slow], ref.at[at_slow], send.at[1], recv.at[1], k, slow),
         )
 
-    strips = [(slice(None), lanes(n, HALO)) for n in (0, HALO, cols, cols + HALO)]
+    strips = [
+        (slice(None), lanes(n, width))
+        for n, width in ((0, HALO), (HALO, HALO), (HALO + cols - FAR, FAR), (HALO + cols, FAR))
+    ]
     halo_fast, halo_slow = to_sides(xb_ref, strips, halo_send, halo_recv)
     pl.when(has_slow)(halo_slow.start)
     halo_fast.start()
@@ -234,7 +240,8 @@
     at_fast, own_fast = pl.ds(0, rim), pl.ds(rim, rim)
     own_soon, own_late = pl.ds(rim, early), pl.ds(rim + early, late)
     at_slow = pl.ds(rim + early + late, rim)
-    facing, parts = pl.ds(0, rim), (pl.ds(0, early), pl.ds(early, late))
+    facing, parts = pl.ds(0, rim), (pl.ds(0, early), pl.ds(early, late), pl.ds(early + late, late))
+    late_out, own_late_out = pl.ds(early, 2 * late), pl.ds(rim + early, 2 * late)
 
     def put_state(c, i):
         st_ref[row_of(i) : row_of(i) + CH, :] = start_ref[:, c, :]
@@ -244,18 +251,7 @@
     pl.when(has_slow)(rim_slow.start)
     rim_fast.start()
 
-    pl.when((k > 0) & (k < groups - 1))(lambda: signal(up.at[0], k + 1, t))
-    pl.when(k > 0)(lambda: signal(down.at[0], k - 1, t))
-
-    def tell_earlier():
-        for n in range(1, groups - 1):
-
-            @pl.when(k > n)
-            def _():
-                pl.semaphore_wait(up.at[n - 1], 1)
-                if n < groups - 2:
-                    pl.when(k < groups - 1)(lambda: signal(up.at[n], k + 1, t))
-                signal(down.at[n], k - n - 1, t)
+    for_earlier(lambda d: signal(down.at[d - 1], k - d, t))
 
     pltpu.make_async_copy(win_ref, win_ref, win_sem).wait()
     w1_ref[...] = jnp.transpose(win_ref[...].astype(F32) * 0.5).astype(BF)
@@ -268,8 +264,8 @@
     keep_first = (lane > 0).astype(F32).astype(BF)
     keep_last = (lane < ROWS - 1).astype(F32).astype(BF)
     slow_one = has_slow.astype(F32)
-    bo_refs = (bo0_ref, bo1_ref)
-    wo_refs = (wo0_ref, wo1_ref)
+    bo_refs = (bo0_ref, bo1_ref, bo2_ref)
+    wo_refs = (wo0_ref, wo1_ref, wo1_ref)
 
     def store_taps(ref, x, at):
         n = x.shape[0]
@@ -317,16 +313,17 @@
     def block(c):
         h = silu_of_half(jnp.dot(w3_ref[...], taps_of(sh_ref, c), preferred_element_type=F32))
         h = (h + fh_ref[128:256, pl.ds((c + 2) * 2 * ROWS, 2 * ROWS)].astype(F32)).astype(BF)
-        n, j = (0, c) if c < soon else (1, c - soon)
-        count = (soon, HALO)[n]
+        n, j = (0, c) if c < soon else (1, c - soon) if c < cols else (2, cols + HALO - 1 - c)
+        count = (soon, HALO, HALO)[n]
         for s in range(2):
             at = (s * count + j) * 128
             bo_refs[n][at : at + 128, :] = h[:, s * ROWS : (s + 1) * ROWS]
 
     def project(n):
         p = jnp.dot(wo_refs[n][...], bo_refs[n][...], preferred_element_type=F32)
-        size = (early, late)[n]
-        return p[:size] + nz_ref[0, parts[n], :], p[size:] + nz_ref[1, parts[n], :]
+        size = (early, late, late)[n]
+        noises = (nzs_ref[0], nzs_ref[1]) if n == 2 else (nz_ref[0, parts[n], :], nz_ref[1, parts[n], :])
+        return p[:size] + noises[0], p[size:] + noises[1]
 
     def inputs_first(c):
         x = xb_ref[:, lanes(place(c))]
@@ -338,7 +335,6 @@
         first_pair((c, c + 1))
     pltpu.make_async_copy(w2_ref, w2_ref, w_sem.at[0]).wait()
     w2_ref[...] = w2_ref[...] * BF(0.5)
-    tell_earlier()
     for c in range(2, cols - 2):
         second(c)
     pltpu.make_async_copy(w3_ref, w3_ref, w_sem.at[1]).wait()
@@ -366,6 +362,8 @@
         nz_ref[1, at : at + CH, :] = n0 + 0.3 * noise_ref[1, :, c, :]
 
     either_way(put_noise)
+    noise_slow = remote(nz_ref.at[:, parts[1]], nzs_ref, noise_send, noise_recv, k, slow)
+    pl.when(has_slow)(noise_slow.start)
 
     halo_fast.wait_recv()
     for c in (-1, -2, -3):
@@ -391,22 +389,19 @@
         return (
             send(0, facing, at_fast, fast),
             send(1, parts[0], own_soon, t),
-            send(2, parts[1], at_slow, slow),
-            send(3, parts[1], own_late, t),
+            send(2, late_out, own_late_out, t),
         )
 
     mid = {d: mids(d) for d in range(1, groups)}
     near_fast = remote(
-        pa_ref.at[facing], rxs_ref.at[at_fast], near_send.at[0], near_recv.at[0], k, fast
-    )
-    near_slow = remote(
-        pa_ref.at[parts[1]], rxs_ref.at[at_slow], near_send.at[1], near_recv.at[1], k, slow
+        pa_ref, rxs_ref, near_send, near_recv, k, fast
     )
 
     def put_sums(n):
         a, g = project(n)
         pg_ref[parts[n], :] = g.astype(BF)
-        pa_ref[parts[n], :] = a.astype(BF)
+        if n == 0:
+            pa_ref[...] = a[:rim].astype(BF)
         return a
 
     def wait_mid(*ns):
@@ -421,30 +416,24 @@
         mid[d][1].start()
         mid[d][0].start()
 
-    patient = groups - 1
     a_soon = put_sums(0)
     near_fast.start()
-    for_later(lambda d: start_soon(d) if d < patient else None)
+    for_later(start_soon)
 
     pl.when(has_slow)(halo_slow.wait_recv)
-    for c in (cols, cols + 1, cols + 2):
+    for c in range(cols, cols + FAR):
         inputs_first(c)
-    first_pair((cols - 1, cols))
-    first_pair((cols + 1,))
-    for c in (cols - 2, cols - 1, cols):
+    for c in range(cols - 1, cols + 5, 2):
+        first_pair((c, c + 1))
+    for c in range(cols - 2, cols + 4):
         second(c)
-    for c in (cols - 3, cols - 2, cols - 1):
+    for c in range(cols - 3, cols + 3):
         block(c)
     a_late = put_sums(1)
-
-    def start_late(d):
-        if d == patient:
-            start_soon(d)
-        pl.when(has_slow)(mid[d][2].start)
-        mid[d][3].start()
-
-    pl.when(has_slow)(near_slow.start)
-    for_later(start_late)
+    pl.when(has_slow)(noise_slow.wait_recv)
+    a_out = put_sums(2)
+
+    for_later(lambda d: mid[d][2].start())
 
     rim_fast.wait_recv()
     near_fast.wait_recv()
@@ -460,6 +449,8 @@
         cov = xb_ref[:, lanes(place(c))].astype(F32)[CH:]
         for s, state in enumerate((base, base + step)):
             v = jnp.concatenate([state[row : row + CH], cov], axis=0)
+            if c >= cols:
+                v = v * slow_one
             store_taps(x2_ref, v.astype(BF), 2 * (c + HALO) + s)
 
     def next_columns(columns, rows, step, firsts, seconds, blocks):
@@ -474,73 +465,44 @@
             block(c)
         return base
 
-    step = jnp.concatenate([rxs_ref[at_fast, :].astype(F32), a_soon], axis=0)
+    step = jnp.concatenate([rxs_ref[...].astype(F32), a_soon], axis=0)
     base = next_columns(
         range(-HALO, soon), pl.ds(0, rim + early), step, range(-2, soon - 1), range(-1, soon - 2), range(soon - 3)
     )
     base_ref[parts[0], :] = base[rim:]
 
-    for_earlier(wait_mid(3))
-    base_ref[parts[1], :] = next_columns(
-        range(soon, cols), own_late, a_late, range(soon - 1, cols - 1), range(soon - 2, cols - 2), range(soon - 3, soon)
+    pl.when(has_slow)(rim_slow.wait_recv)
+    for_earlier(wait_mid(2))
+    base = next_columns(
+        range(soon, cols + HALO),
+        own_late_out,
+        jnp.concatenate([a_late, a_out], axis=0),
+        range(soon - 1, cols + 2),
+        range(soon - 2, cols + 1),
+        range(soon - 3, cols),
     )
-
-    def lasts(d):
-        return [
-            remote(
-                pd_ref.at[at],
-                rxf_ref.at[d - 1, at],
-                last_send.at[d - 1, n],
-                last_recv.at[d - 1, n],
-                k + d,
-                t,
-            )
-            for n, at in enumerate(parts)
-        ]
-
-    last = {d: lasts(d) for d in range(1, groups)}
-
-    def put_last(n):
-        a, g = project(n)
+    base_ref[parts[1], :] = base[:late]
+
+    last = {
+        d: remote(pd_ref, rxf_ref.at[d - 1], last_send.at[d - 1], last_recv.at[d - 1], k + d, t)
+        for d in range(1, groups)
+    }
+    both = [project(n) for n in range(2)]
+    for n, (a, g) in enumerate(both):
         pd_ref[parts[n], :] = (g - pg_ref[parts[n], :].astype(F32)).astype(BF)
-        for_later(lambda d: last[d][n].start())
-        return a, g
-
-    a_soon, g_soon = put_last(0)
-
-    @pl.when(has_slow)
-    def _():
-        rim_slow.wait_recv()
-        near_slow.wait_recv()
-        for_earlier(wait_mid(2))
-
-    next_columns(
-        range(cols, cols + HALO),
-        at_slow,
-        rxs_ref[at_slow, :].astype(F32),
-        range(cols - 1, cols + 2),
-        range(cols - 2, cols + 1),
-        range(soon, cols),
-    )
-    a_late, g_late = put_last(1)
+    for_later(lambda d: last[d].start())
+    (a_soon, g_soon), (a_late, g_late) = both
 
     def all_sent(*copies):
         for c in copies:
             c.wait_send()
 
     all_sent(halo_fast, rim_fast, near_fast)
-    for_later(lambda d: all_sent(mid[d][0], mid[d][1], mid[d][3]))
-
-    @pl.when(has_slow)
-    def _():
-        all_sent(halo_slow, rim_slow, near_slow)
-        for_later(lambda d: all_sent(mid[d][2]))
-
-    def got(d):
-        for c in last[d]:
-            c.wait_recv()
-
-    for_earlier(got)
+    for_later(lambda d: all_sent(*mid[d]))
+
+    pl.when(has_slow)(lambda: all_sent(halo_slow, rim_slow, noise_slow))
+
+    for_earlier(lambda d: last[d].wait_recv())
     base = base_ref[...]
     for d in range(groups - 1):
         base = base + rxf_ref[d].astype(F32)
@@ -555,7 +517,7 @@
 
     either_way(put_result)
 
-    for_later(lambda d: all_sent(*last[d]))
+    for_later(lambda d: all_sent(last[d]))
 
 
 def solution(mesh):
@@ -591,8 +553,8 @@
                 pltpu.VMEM((12, cols, ROWS), F32),
                 pltpu.VMEM((own + 32, ROWS), F32),
                 pltpu.VMEM((own, ROWS), F32),
-                pltpu.VMEM((16, wide * ROWS), BF),
-                pltpu.VMEM((48, wide * ROWS), BF),
+                pltpu.VMEM((16, (wide + HALO) * ROWS), BF),
+                pltpu.VMEM((48, (wide + HALO) * ROWS), BF),
                 pltpu.VMEM((48, wide * 2 * ROWS), BF),
                 pltpu.VMEM((128, 144), BF),
                 pltpu.VMEM((128, 1152), BF),
@@ -601,15 +563,17 @@
                 pltpu.VMEM((32, 256 * HALO), BF),
                 pltpu.VMEM((128, 2 * ROWS), F32),
                 pltpu.VMEM((2, own, ROWS), F32),
-                pltpu.VMEM((384, (wide - 2) * 2 * ROWS), BF),
-                pltpu.VMEM((384, (wide - 4) * 2 * ROWS), BF),
+                pltpu.VMEM((2, 16, ROWS), F32),
+                pltpu.VMEM((384, (wide + 1) * 2 * ROWS), BF),
+                pltpu.VMEM((384, (wide - 1) * 2 * ROWS), BF),
                 pltpu.VMEM((256 * (cols - HALO), ROWS), BF),
                 pltpu.VMEM((256 * HALO, ROWS), BF),
-                pltpu.VMEM((own, ROWS), BF),
-                pltpu.VMEM((own, ROWS), BF),
+                pltpu.VMEM((256 * HALO, ROWS), BF),
+                pltpu.VMEM((16, ROWS), BF),
+                pltpu.VMEM((own + 16, ROWS), BF),
                 pltpu.VMEM((own, ROWS), BF),
                 pltpu.VMEM((groups - 1, own + 32, ROWS), BF),
-                pltpu.VMEM((own + 32, ROWS), BF),
+                pltpu.VMEM((16, ROWS), BF),
                 pltpu.VMEM((groups - 1, own, ROWS), BF),
                 dma((5,)),
                 dma(()),
@@ -618,13 +582,14 @@
                 dma((2,)),
                 dma((2,)),
                 dma((2,)),
-                dma((2,)),
-                dma((2,)),
-                dma((groups - 1, 4)),
-                dma((groups - 1, 4)),
-                dma((groups - 1, 2)),
-                dma((groups - 1, 2)),
-                pltpu.SemaphoreType.REGULAR((groups - 1,)),
+                dma(()),
+                dma(()),
+                dma(()),
+                dma(()),
+                dma((groups - 1, 3)),
+                dma((groups - 1, 3)),
+                dma((groups - 1,)),
+                dma((groups - 1,)),
                 pltpu.SemaphoreType.REGULAR((groups - 1,)),
             ],
             compiler_params=pltpu.CompilerParams(

time: 16.8 us -> 16.4 us (0.976)
  Pallas kernels: 15.8 us -> 15.6 us
    pallas_call x1, Pallas kernels: 15.8 us -> 15.6 us  [local(): pl.pallas_call(body, out_shape=pltpu.VMEM((2, 4, cols, ROWS), F32), in_sp...]
where the time goes in v9:
time: 16.4 us; the launch traced here: 16.2 us
  Pallas kernels  15.6 us (95%)
  local copies, waits for them, and re-layouts  0.62 us (4%)
    pallas_call x1, Pallas kernels, local(): pl.pallas_call(body, out_shape=pltpu.VMEM((2, 4, cols, ROWS), F32), in_sp...  15.6 us
    unnamed x1, local copies, waits for them, and re-layouts  0.62 us

profile of v9, /device:TPU:152, one launch (start us, length us, event | category | flops | bytes accessed | tf_op | source)
XLA Modules:
  0.0 16.2 jit_solution(9777996310065988305)
XLA Ops:
  0.0 15.6 %shard_map.82 = f32[2,4,8,128]{3,2,1,0:T(8,128)S(1)} custom-call(f32[4,8,128]{2,1,0:T(8,128)} %refs_0_.1, bf16[12,8,128]{2,1,0:T(8,128)(2,1)} %refs_1_.1, f32[2,4,8,128]{3,2,1,0:T(8,128)} %refs_2_.1, f32[2,128]{1,0:T(2,128)} %refs_3_.1, bf16[144,128]{1,0:T(8,128)(2,1)} %bitcast.3, bf16[9,128,128]{2,1,0:T(8,128)(2,1)} %refs_5_.1, ...), custom_call_target="tpu_custom_call" | custom-call | tf_op jit(solution)/shard_map/pallas_call | solution.py:541
  15.6 0.6 %copy.10 = f32[2,4,8,128]{3,2,1,0:T(8,128)} copy(f32[2,4,8,128]{3,2,1,0:T(8,128)S(1)} %shard_map.82) | data formatting | bytes 65536

commit v10 on v9

--- a/solution.py
+++ b/solution.py
@@ -51,6 +51,7 @@
     wo1_ref,
     eb_ref,
     nz_ref,
+    nzb_ref,
     nzs_ref,
     fh_ref,
     sh_ref,
@@ -174,7 +175,7 @@
     signal(barrier, k, fast)
     for_later(lambda d: signal(barrier, k + d, t))
 
-    for c in (get_cov, get_start, *get_win, get_embed, *weights[0], *weights[1], get_noise, get_wout):
+    for c in (get_cov, get_start, get_noise, *get_win, get_embed, *weights[0], *weights[1], get_wout):
         c.start()
 
     def lanes(n, width=1):
@@ -197,6 +198,12 @@
     def own_row(i):
         return CH * i if i < soon else early + CH * (i - soon)
 
+    at_fast, own_fast = pl.ds(0, rim), pl.ds(rim, rim)
+    own_soon, own_late = pl.ds(rim, early), pl.ds(rim + early, late)
+    at_slow = pl.ds(rim + early + late, rim)
+    facing, parts = pl.ds(0, rim), (pl.ds(0, early), pl.ds(early, late), pl.ds(early + late, late))
+    late_out, own_late_out = pl.ds(early, 2 * late), pl.ds(rim + early, 2 * late)
+
     get_cov.wait()
     covf_ref[...] = cov_ref[...].astype(F32)
     get_start.wait()
@@ -206,6 +213,17 @@
         xb_ref[:, lanes(place(i))] = x.astype(BF)
 
     either_way(put_inputs)
+    get_noise.wait()
+    nz_ref[...] = jnp.zeros_like(nz_ref)
+
+    def put_noise(c, i):
+        at = own_row(i)
+        n0 = 0.3 * noise_ref[0, :, c, :]
+        nz_ref[0, at : at + CH, :] = n0
+        nz_ref[1, at : at + CH, :] = n0 + 0.3 * noise_ref[1, :, c, :]
+
+    either_way(put_noise)
+    nzb_ref[...] = nz_ref[:, parts[1], :].astype(BF)
 
     def one(p):
         return p.astype(jnp.int32)
@@ -234,14 +252,14 @@
         for n, width in ((0, HALO), (HALO, HALO), (HALO + cols - FAR, FAR), (HALO + cols, FAR))
     ]
     halo_fast, halo_slow = to_sides(xb_ref, strips, halo_send, halo_recv)
-    pl.when(has_slow)(halo_slow.start)
+    noise_slow = remote(nzb_ref, nzs_ref, noise_send, noise_recv, k, slow)
+
+    @pl.when(has_slow)
+    def _():
+        halo_slow.start()
+        noise_slow.start()
+
     halo_fast.start()
-
-    at_fast, own_fast = pl.ds(0, rim), pl.ds(rim, rim)
-    own_soon, own_late = pl.ds(rim, early), pl.ds(rim + early, late)
-    at_slow = pl.ds(rim + early + late, rim)
-    facing, parts = pl.ds(0, rim), (pl.ds(0, early), pl.ds(early, late), pl.ds(early + late, late))
-    late_out, own_late_out = pl.ds(early, 2 * late), pl.ds(rim + early, 2 * late)
 
     def put_state(c, i):
         st_ref[row_of(i) : row_of(i) + CH, :] = start_ref[:, c, :]
@@ -322,7 +340,7 @@
     def project(n):
         p = jnp.dot(wo_refs[n][...], bo_refs[n][...], preferred_element_type=F32)
         size = (early, late, late)[n]
-        noises = (nzs_ref[0], nzs_ref[1]) if n == 2 else (nz_ref[0, parts[n], :], nz_ref[1, parts[n], :])
+        noises = [nzs_ref[m].astype(F32) if n == 2 else nz_ref[m, parts[n], :] for m in range(2)]
         return p[:size] + noises[0], p[size:] + noises[1]
 
     def inputs_first(c):
@@ -352,18 +370,6 @@
                 lhs.append(jnp.concatenate(blocks, axis=1))
             lhs.append(jnp.zeros((size - CH * count, 2 * 128 * count), F32))
         wo_refs[n][...] = jnp.concatenate(lhs, axis=0).astype(BF)
-    get_noise.wait()
-    nz_ref[...] = jnp.zeros_like(nz_ref)
-
-    def put_noise(c, i):
-        at = own_row(i)
-        n0 = 0.3 * noise_ref[0, :, c, :]
-        nz_ref[0, at : at + CH, :] = n0
-        nz_ref[1, at : at + CH, :] = n0 + 0.3 * noise_ref[1, :, c, :]
-
-    either_way(put_noise)
-    noise_slow = remote(nz_ref.at[:, parts[1]], nzs_ref, noise_send, noise_recv, k, slow)
-    pl.when(has_slow)(noise_slow.start)
 
     halo_fast.wait_recv()
     for c in (-1, -2, -3):
@@ -420,7 +426,11 @@
     near_fast.start()
     for_later(start_soon)
 
-    pl.when(has_slow)(halo_slow.wait_recv)
+    @pl.when(has_slow)
+    def _():
+        halo_slow.wait_recv()
+        noise_slow.wait_recv()
+
     for c in range(cols, cols + FAR):
         inputs_first(c)
     for c in range(cols - 1, cols + 5, 2):
@@ -430,7 +440,6 @@
     for c in range(cols - 3, cols + 3):
         block(c)
     a_late = put_sums(1)
-    pl.when(has_slow)(noise_slow.wait_recv)
     a_out = put_sums(2)
 
     for_later(lambda d: mid[d][2].start())
@@ -563,7 +572,8 @@
                 pltpu.VMEM((32, 256 * HALO), BF),
                 pltpu.VMEM((128, 2 * ROWS), F32),
                 pltpu.VMEM((2, own, ROWS), F32),
-                pltpu.VMEM((2, 16, ROWS), F32),
+                pltpu.VMEM((2, 16, ROWS), BF),
+                pltpu.VMEM((2, 16, ROWS), BF),
                 pltpu.VMEM((384, (wide + 1) * 2 * ROWS), BF),
                 pltpu.VMEM((384, (wide - 1) * 2 * ROWS), BF),
                 pltpu.VMEM((256 * (cols - HALO), ROWS), BF),

time: 16.4 us -> 16.3 us (level)
  no operation moved by 1% of the time
where the time goes in v10:
time: 16.3 us; the launch traced here: 16.1 us
  Pallas kernels  15.5 us (95%)
  local copies, waits for them, and re-layouts  0.62 us (4%)
    pallas_call x1, Pallas kernels, local(): pl.pallas_call(body, out_shape=pltpu.VMEM((2, 4, cols, ROWS), F32), in_sp...  15.5 us
    unnamed x1, local copies, waits for them, and re-layouts  0.62 us

profile of v10, /device:TPU:152, one launch (start us, length us, event | category | flops | bytes accessed | tf_op | source)
XLA Modules:
  0.0 16.1 jit_solution(578156681748056509)
XLA Ops:
  0.0 15.5 %shard_map.82 = f32[2,4,8,128]{3,2,1,0:T(8,128)S(1)} custom-call(f32[4,8,128]{2,1,0:T(8,128)} %refs_0_.1, bf16[12,8,128]{2,1,0:T(8,128)(2,1)} %refs_1_.1, f32[2,4,8,128]{3,2,1,0:T(8,128)} %refs_2_.1, f32[2,128]{1,0:T(2,128)} %refs_3_.1, bf16[144,128]{1,0:T(8,128)(2,1)} %bitcast.3, bf16[9,128,128]{2,1,0:T(8,128)(2,1)} %refs_5_.1, ...), custom_call_target="tpu_custom_call" | custom-call | tf_op jit(solution)/shard_map/pallas_call | solution.py:550
  15.5 0.6 %copy.10 = f32[2,4,8,128]{3,2,1,0:T(8,128)} copy(f32[2,4,8,128]{3,2,1,0:T(8,128)S(1)} %shard_map.82) | data formatting | bytes 65536

commit v11 on v10

--- a/solution.py
+++ b/solution.py
@@ -55,6 +55,7 @@
     nzs_ref,
     fh_ref,
     sh_ref,
+    pr_ref,
     bo0_ref,
     bo1_ref,
     bo2_ref,
@@ -296,10 +297,24 @@
         for s in range(2):
             store_taps(ref, h[:, s * ROWS : (s + 1) * ROWS], 2 * at + s)
 
-    def taps_of(ref, at):
+    def taps_of(ref, at, which=range(3)):
         return jnp.concatenate(
-            [ref[:, pl.ds((at + a) * 2 * ROWS, 2 * ROWS)] for a in range(3)], axis=0
-        )
+            [ref[:, pl.ds((at + a) * 2 * ROWS, 2 * ROWS)] for a in which], axis=0
+        )
+
+    def conv(w_ref, ref, at, which):
+        w = w_ref[:, pl.ds(which[0] * 384, len(which) * 384)]
+        return jnp.dot(w, taps_of(ref, at, which), preferred_element_type=F32)
+
+    def ahead(c):
+        for n, (w_ref, ref, at) in enumerate(((w2_ref, fh_ref, c + 2), (w3_ref, sh_ref, c))):
+            pr_ref[2 * n] = conv(w_ref, ref, at, range(2))
+            pr_ref[2 * n + 1] = conv(w_ref, ref, at + 1, range(1))
+
+    def whole(n, done, w_ref, ref, at):
+        if not done:
+            return conv(w_ref, ref, at, range(3))
+        return conv(w_ref, ref, at, range(done, 3)) + pr_ref[2 * n + 2 - done]
 
     def inside(h, c):
         return h * slow_one if c >= cols else h
@@ -324,12 +339,12 @@
             p = pre[:, n * ROWS : (n + 1) * ROWS]
             first_done(jnp.concatenate([p, p], axis=1), c)
 
-    def second(c):
-        h = jnp.dot(w2_ref[...], taps_of(fh_ref, c + 1), preferred_element_type=F32)
+    def second(c, done=0):
+        h = whole(0, done, w2_ref, fh_ref, c + 1)
         store_both(sh_ref, inside(silu_of_half(h), c).astype(BF), c + 1)
 
-    def block(c):
-        h = silu_of_half(jnp.dot(w3_ref[...], taps_of(sh_ref, c), preferred_element_type=F32))
+    def block(c, done=0):
+        h = silu_of_half(whole(1, done, w3_ref, sh_ref, c))
         h = (h + fh_ref[128:256, pl.ds((c + 2) * 2 * ROWS, 2 * ROWS)].astype(F32)).astype(BF)
         n, j = (0, c) if c < soon else (1, c - soon) if c < cols else (2, cols + HALO - 1 - c)
         count = (soon, HALO, HALO)[n]
@@ -426,6 +441,8 @@
     near_fast.start()
     for_later(start_soon)
 
+    ahead(soon)
+
     @pl.when(has_slow)
     def _():
         halo_slow.wait_recv()
@@ -436,9 +453,9 @@
     for c in range(cols - 1, cols + 5, 2):
         first_pair((c, c + 1))
     for c in range(cols - 2, cols + 4):
-        second(c)
+        second(c, max(0, cols - c))
     for c in range(cols - 3, cols + 3):
-        block(c)
+        block(c, max(0, soon + 2 - c))
     a_late = put_sums(1)
     a_out = put_sums(2)
 
@@ -462,23 +479,24 @@
                 v = v * slow_one
             store_taps(x2_ref, v.astype(BF), 2 * (c + HALO) + s)
 
-    def next_columns(columns, rows, step, firsts, seconds, blocks):
+    def next_columns(columns, rows, step, firsts, seconds, blocks, done):
         base = base_of(rows)
         for c in columns:
             inputs_next(c, base, step, row_of(c) - rows.start)
         for c in firsts:
             first(c)
-        for c in seconds:
-            second(c)
-        for c in blocks:
-            block(c)
+        for n, c in enumerate(seconds):
+            second(c, max(0, done - n))
+        for n, c in enumerate(blocks):
+            block(c, max(0, done - n))
         return base
 
     step = jnp.concatenate([rxs_ref[...].astype(F32), a_soon], axis=0)
     base = next_columns(
-        range(-HALO, soon), pl.ds(0, rim + early), step, range(-2, soon - 1), range(-1, soon - 2), range(soon - 3)
+        range(-HALO, soon), pl.ds(0, rim + early), step, range(-2, soon - 1), range(-1, soon - 2), range(soon - 3), 0
     )
     base_ref[parts[0], :] = base[rim:]
+    ahead(soon - 3)
 
     pl.when(has_slow)(rim_slow.wait_recv)
     for_earlier(wait_mid(2))
@@ -489,6 +507,7 @@
         range(soon - 1, cols + 2),
         range(soon - 2, cols + 1),
         range(soon - 3, cols),
+        2,
     )
     base_ref[parts[1], :] = base[:late]
 
@@ -576,6 +595,7 @@
                 pltpu.VMEM((2, 16, ROWS), BF),
                 pltpu.VMEM((384, (wide + 1) * 2 * ROWS), BF),
                 pltpu.VMEM((384, (wide - 1) * 2 * ROWS), BF),
+                pltpu.VMEM((4, 128, 2 * ROWS), F32),
                 pltpu.VMEM((256 * (cols - HALO), ROWS), BF),
                 pltpu.VMEM((256 * HALO, ROWS), BF),
                 pltpu.VMEM((256 * HALO, ROWS), BF),

time: 16.3 us -> 16.1 us (0.988)
  Pallas kernels: 15.5 us -> 15.3 us
    pallas_call x1, Pallas kernels: 15.5 us -> 15.3 us  [local(): pl.pallas_call(body, out_shape=pltpu.VMEM((2, 4, cols, ROWS), F32), in_sp...]
where the time goes in v11:
time: 16.1 us; the launch traced here: 15.9 us
  Pallas kernels  15.3 us (95%)
  local copies, waits for them, and re-layouts  0.62 us (4%)
    pallas_call x1, Pallas kernels, local(): pl.pallas_call(body, out_shape=pltpu.VMEM((2, 4, cols, ROWS), F32), in_sp...  15.3 us
    unnamed x1, local copies, waits for them, and re-layouts  0.62 us

profile of v11, /device:TPU:152, one launch (start us, length us, event | category | flops | bytes accessed | tf_op | source)
XLA Modules:
  0.0 15.9 jit_solution(2826501834692962935)
XLA Ops:
  0.0 15.3 %shard_map.82 = f32[2,4,8,128]{3,2,1,0:T(8,128)S(1)} custom-call(f32[4,8,128]{2,1,0:T(8,128)} %refs_0_.1, bf16[12,8,128]{2,1,0:T(8,128)(2,1)} %refs_1_.1, f32[2,4,8,128]{3,2,1,0:T(8,128)} %refs_2_.1, f32[2,128]{1,0:T(2,128)} %refs_3_.1, bf16[144,128]{1,0:T(8,128)(2,1)} %bitcast.3, bf16[9,128,128]{2,1,0:T(8,128)(2,1)} %refs_5_.1, ...), custom_call_target="tpu_custom_call" | custom-call | tf_op jit(solution)/shard_map/pallas_call | solution.py:569
  15.3 0.6 %copy.10 = f32[2,4,8,128]{3,2,1,0:T(8,128)} copy(f32[2,4,8,128]{3,2,1,0:T(8,128)S(1)} %shard_map.82) | data formatting | bytes 65536

commit v12 on v11

--- a/solution.py
+++ b/solution.py
@@ -459,7 +459,8 @@
     a_late = put_sums(1)
     a_out = put_sums(2)
 
-    for_later(lambda d: mid[d][2].start())
+    for d in sorted(range(1, groups), key=lambda d: -min(d, groups - d)):
+        pl.when(k + d < groups)(mid[d][2].start)
 
     rim_fast.wait_recv()
     near_fast.wait_recv()

time: 16.1 us -> 16.2 us (level)
  no operation moved by 1% of the time
where the time goes in v12:
time: 16.2 us; the launch traced here: 16 us
  Pallas kernels  15.4 us (95%)
  local copies, waits for them, and re-layouts  0.62 us (4%)
    pallas_call x1, Pallas kernels, local(): pl.pallas_call(body, out_shape=pltpu.VMEM((2, 4, cols, ROWS), F32), in_sp...  15.4 us
    unnamed x1, local copies, waits for them, and re-layouts  0.62 us

profile of v12, /device:TPU:152, one launch (start us, length us, event | category | flops | bytes accessed | tf_op | source)
XLA Modules:
  0.0 16.0 jit_solution(5576805571219470358)
XLA Ops:
  0.0 15.4 %shard_map.82 = f32[2,4,8,128]{3,2,1,0:T(8,128)S(1)} custom-call(f32[4,8,128]{2,1,0:T(8,128)} %refs_0_.1, bf16[12,8,128]{2,1,0:T(8,128)(2,1)} %refs_1_.1, f32[2,4,8,128]{3,2,1,0:T(8,128)} %refs_2_.1, f32[2,128]{1,0:T(2,128)} %refs_3_.1, bf16[144,128]{1,0:T(8,128)(2,1)} %bitcast.3, bf16[9,128,128]{2,1,0:T(8,128)(2,1)} %refs_5_.1, ...), custom_call_target="tpu_custom_call" | custom-call | tf_op jit(solution)/shard_map/pallas_call | solution.py:570
  15.4 0.6 %copy.10 = f32[2,4,8,128]{3,2,1,0:T(8,128)} copy(f32[2,4,8,128]{3,2,1,0:T(8,128)S(1)} %shard_map.82) | data formatting | bytes 65536

commit v13 on v11

--- a/solution.py
+++ b/solution.py
@@ -262,6 +262,9 @@
 
     halo_fast.start()
 
+    for_earlier(lambda d: signal(down.at[d - 1], k - d, t))
+
+
     def put_state(c, i):
         st_ref[row_of(i) : row_of(i) + CH, :] = start_ref[:, c, :]
 
@@ -269,8 +272,6 @@
     rim_fast, rim_slow = to_sides(st_ref, (at_fast, own_fast, own_late, at_slow), rim_send, rim_recv)
     pl.when(has_slow)(rim_slow.start)
     rim_fast.start()
-
-    for_earlier(lambda d: signal(down.at[d - 1], k - d, t))
 
     pltpu.make_async_copy(win_ref, win_ref, win_sem).wait()
     w1_ref[...] = jnp.transpose(win_ref[...].astype(F32) * 0.5).astype(BF)

time: 16.1 us -> 16.1 us (level)
  no operation moved by 1% of the time
where the time goes in v13:
time: 16.1 us; the launch traced here: 15.9 us
  Pallas kernels  15.3 us (95%)
  local copies, waits for them, and re-layouts  0.62 us (4%)
    pallas_call x1, Pallas kernels, local(): pl.pallas_call(body, out_shape=pltpu.VMEM((2, 4, cols, ROWS), F32), in_sp...  15.3 us
    unnamed x1, local copies, waits for them, and re-layouts  0.62 us

profile of v13, /device:TPU:152, one launch (start us, length us, event | category | flops | bytes accessed | tf_op | source)
XLA Modules:
  0.0 15.9 jit_solution(17277791228346070835)
XLA Ops:
  0.0 15.3 %shard_map.82 = f32[2,4,8,128]{3,2,1,0:T(8,128)S(1)} custom-call(f32[4,8,128]{2,1,0:T(8,128)} %refs_0_.1, bf16[12,8,128]{2,1,0:T(8,128)(2,1)} %refs_1_.1, f32[2,4,8,128]{3,2,1,0:T(8,128)} %refs_2_.1, f32[2,128]{1,0:T(2,128)} %refs_3_.1, bf16[144,128]{1,0:T(8,128)(2,1)} %bitcast.3, bf16[9,128,128]{2,1,0:T(8,128)(2,1)} %refs_5_.1, ...), custom_call_target="tpu_custom_call" | custom-call | tf_op jit(solution)/shard_map/pallas_call | solution.py:570
  15.3 0.6 %copy.10 = f32[2,4,8,128]{3,2,1,0:T(8,128)} copy(f32[2,4,8,128]{3,2,1,0:T(8,128)S(1)} %shard_map.82) | data formatting | bytes 65536
